TPU v7x, 512 devices: a whole 4x8x8 slice. The times are simulated.
512 devices in a mesh: row: 32 (over x, z), col: 16 (over y, core).
Axes of the slice: x: 4, y: 8, z: 8, core: 2. Of those that a mesh axis runs over, the one named last changes fastest.
Arguments:
- momentum: float32 [8192, 14336], P('row', 'col'), may hold values from -230 to 230
- gradient: bfloat16 [8192, 14336], P('row', 'col'), may hold values from -6 to 6
- right_basis: float32 [14336, 512], P('col', 'row'), may hold values from -6 to 6
Outputs:
- update: float32 [8192, 14336], P('row', 'col')
- new_momentum: float32 [8192, 14336], P('row', 'col')
- new_basis: float32 [14336, 512], P('col', 'row')
All inputs are finite; a program needn't handle non-finite values.
Results may differ from a plain program's by a relative error of at most 0.0003.
Values sent between devices are 32-bit elements; how exact they have to be, the bound alone decides.
No kernel may reach another device: no remote copies, remote signals or barrier semaphores. Data moves between devices by JAX's collectives and lax.ppermute only.
A program may use at most 64 MiB of HBM per device.

v0:
```python
import math

import jax
import jax.numpy as jnp
from jax import lax
from jax.sharding import PartitionSpec as P

ROWS = 8192
COLS = 14336
RANK = 512


HIGH = lax.Precision.HIGHEST
epsilon_norm = 1e-06
retain = 0.7


def inner_rows(first, second):
    return lax.dot_general(
        first, second, (((0,), (0,)), ((), ())), precision=HIGH, preferred_element_type=jnp.float32
    )


def outer_cols(first, second):
    return lax.dot_general(
        first, second, (((1,), (1,)), ((), ())), precision=HIGH, preferred_element_type=jnp.float32
    )


def solve_left(gram_matrix, left_rows):
    chol_factor = jnp.linalg.cholesky(gram_matrix)
    return jax.scipy.linalg.solve_triangular(chol_factor, left_rows.T, lower=True).T


def body(momentum, gradient, right_basis):
    blended = momentum + gradient.astype(jnp.float32)
    scale = math.sqrt(ROWS * COLS / RANK)
    left_part = jnp.dot(
        blended,
        lax.all_gather(right_basis, "row", axis=1, tiled=True),
        precision=HIGH,
        preferred_element_type=jnp.float32,
    )
    left_full = lax.psum(left_part, "col")
    gram_matrix = lax.psum(inner_rows(left_full, left_full), "row")
    orthonormal = solve_left(gram_matrix, left_full)
    right_part = inner_rows(blended, orthonormal)
    right_factor = lax.psum(right_part, "row")
    squares = lax.psum(jnp.sum(right_factor * right_factor, axis=0), "col")
    normed = right_factor / jnp.sqrt(squares + epsilon_norm)[None, :]
    new_momentum = blended - (1.0 - retain) * outer_cols(orthonormal, right_factor)
    update = scale * outer_cols(orthonormal, normed)
    width = right_factor.shape[1] // lax.axis_size("row")
    new_basis = lax.dynamic_slice_in_dim(normed, lax.axis_index("row") * width, width, 1)
    return (update, new_momentum, new_basis)


def solution(mesh):
    in_specs = (P("row", "col"), P("row", "col"), P("col", "row"))
    out_specs = (P("row", "col"), P("row", "col"), P("col", "row"))
    return jax.shard_map(body, mesh=mesh, in_specs=in_specs, out_specs=out_specs, check_vma=False)
```

profile of v0, /device:TPU:1, one launch (start us, length us, event | category | flops | bytes accessed | tf_op | source)
XLA Modules:
  0.0 734.9 jit_solution(14650317432565492737)
XLA Ops:
  7.2 0.7 all-gather.2.cloned.1.call-update
  7.9 88.4 %all-gather.2.cloned.1.call-done = f32[896,512]{0,1:T(8,128)} async-done(((f32[896,16]{0,1:T(8,128)}), f32[896,512]{0,1:T(8,128)}) %all-gather.2.cloned.1.call-update) | async-done | bytes 1835024 | tf_op jit(solution)/shard_map/all_gather | solution.py:40
  96.3 4.6 fusion.8
  101.0 115.7 %all-reduce.5.cloned.1.call-done = f32[256,512]{1,0:T(8,128)} async-done(((f32[256,512]{1,0:T(8,128)}), f32[256,512]{1,0:T(8,128)}) %all-reduce.5.cloned.1.call-update) | async-done | bytes 524304 | tf_op jit(solution)/shard_map/psum | solution.py:44
  216.8 3.3 fusion.37
  220.4 157.5 %all-reduce.7.cloned.1.call-done = f32[512,512]{0,1:T(8,128)} async-done(((f32[512,512]{0,1:T(8,128)}), f32[512,512]{0,1:T(8,128)}) %all-reduce.7.cloned.1.call-update) | async-done | bytes 1048592 | tf_op jit(solution)/shard_map/psum | solution.py:45
  377.9 1.6 copy.7
  379.8 11.7 %cholesky.104 = f32[128,128]{1,0:T(8,128)S(1)} custom-call(f32[128,128]{1,0:T(8,128)S(1)} %cholesky.266), custom_call_target="Cholesky" | custom-call | tf_op jit(solution)/shard_map/jit(cholesky)/cholesky | solution.py:31
  391.6 9.8 %custom-call.31 = f32[1,128,128]{1,2,0:T(8,128)S(1)} custom-call(f32[1,128,128]{2,1,0:T(8,128)S(1)} %get-tuple-element.33), custom_call_target="InvertDiagBlocksLowerTriangular" | custom-call | tf_op jit(solution)/shard_map/jit(cholesky)/cholesky | solution.py:31
  402.2 11.7 %cholesky.217 = f32[128,128]{1,0:T(8,128)S(1)} custom-call(f32[128,128]{1,0:T(8,128)S(1)} %cholesky.270), custom_call_target="Cholesky" | custom-call | tf_op jit(solution)/shard_map/jit(cholesky)/cholesky | solution.py:31
  413.9 10.3 %custom-call.32 = f32[1,128,128]{1,2,0:T(8,128)S(1)} custom-call(f32[1,128,128]{2,1,0:T(8,128)S(1)} %get-tuple-element.30), custom_call_target="InvertDiagBlocksLowerTriangular" | custom-call | tf_op jit(solution)/shard_map/jit(cholesky)/cholesky | solution.py:31
  424.9 11.7 %cholesky.238 = f32[128,128]{1,0:T(8,128)S(1)} custom-call(f32[128,128]{1,0:T(8,128)S(1)} %cholesky.275), custom_call_target="Cholesky" | custom-call | tf_op jit(solution)/shard_map/jit(cholesky)/cholesky | solution.py:31
  436.7 0.7 compare_reduce_fusion.1
  437.4 9.8 %custom-call.33 = f32[1,128,128]{1,2,0:T(8,128)S(1)} custom-call(f32[1,128,128]{2,1,0:T(8,128)S(1)} %get-tuple-element.27), custom_call_target="InvertDiagBlocksLowerTriangular" | custom-call | tf_op jit(solution)/shard_map/jit(cholesky)/cholesky | solution.py:31
  447.8 11.7 %cholesky.255 = f32[128,128]{1,0:T(8,128)S(1)} custom-call(f32[128,128]{1,0:T(8,128)S(1)} %convolution_subtract_fusion.5), custom_call_target="Cholesky" | custom-call | tf_op jit(solution)/shard_map/jit(cholesky)/cholesky | solution.py:31
  460.2 0.7 compare_reduce_fusion.2
  463.7 10.9 %while.1 = (s32[]{:T(128)}, f32[512,512]{1,0:T(8,128)S(1)}, s32[4,2]{0,1:T(2,128)S(1)}, f32[4,128,128]{2,1,0:T(8,128)}, s32[]{:T(128)}) while((s32[]{:T(128)}, f32[512,512]{1,0:T(8,128)S(1)}, s32[4,2]{0,1:T(2,128)S(1)}, f32[4,128,128]{2,1,0:T(8,128)}, s32[]{:T(128)}) %tuple.32), condition=%wide.while_cond, body=%wide.while_body.sunk | while | flops 2 | bytes 132705 | solution.py:32
  464.4 2.1 bitcast_dynamic-update-slice_fusion.2
  467.1 2.1 bitcast_dynamic-update-slice_fusion.2
  469.8 2.1 bitcast_dynamic-update-slice_fusion.2
  472.6 2.1 bitcast_dynamic-update-slice_fusion.2
  474.6 40.2 %custom-call.34 = f32[4,128,128]{1,2,0:T(8,128)S(1)} custom-call(f32[4,128,128]{2,1,0:T(8,128)} %get-tuple-element.10), custom_call_target="InvertDiagBlocksLowerTriangular" | custom-call | tf_op jit(solution)/shard_map/jit(_solve_triangular)/triangular_solve | solution.py:32
  516.8 0.8 convolution_subtract_fusion.1
  518.6 4.3 fusion.7
  522.9 162.5 %all-reduce.9.cloned.1.call-done = f32[896,512]{1,0:T(8,128)} async-done(((f32[896,512]{1,0:T(8,128)}), f32[896,512]{1,0:T(8,128)}) %all-reduce.9.cloned.1.call-update) | async-done | bytes 1835024 | tf_op jit(solution)/shard_map/psum | solution.py:48
  685.4 1.8 multiply_reduce_fusion
  687.2 27.4 %psum.31 = f32[512]{0:T(512)S(1)} all-reduce(f32[512]{0:T(512)S(1)} %multiply_reduce_fusion), channel_id=1, replica_groups=mesh['row'=32,'col'=16] {'col'}, use_global_device_ids=true, to_apply=%region_12.13 | all-reduce | flops 512 | bytes 4096 | tf_op jit(solution)/shard_map/psum | solution.py:49
  714.9 0.7 copy-done.7
  715.6 4.4 convolution_multiply_fusion.1
  720.0 1.0 constant_dynamic-slice_fusion.1
  721.0 1.8 copy.8
  722.8 5.3 fusion
  (62 shorter events, 9.7 us)
Async XLA Ops:
  7.2 89.1 %all-gather.2.cloned.1.call-start = ((), (), s32[]{:S(2)}) async-start(), calls=%async_computation | async-start | bytes 1892352 | tf_op jit(solution)/shard_map/all_gather | solution.py:40
  7.9 208.9 %all-reduce.5.cloned.1.call-start = ((), (), s32[]{:S(2)}) async-start(), calls=%async_computation.1 | async-start | bytes 1048576 | tf_op jit(solution)/shard_map/psum | solution.py:44
  101.0 276.9 %all-reduce.7.cloned.1.call-start = ((), (), s32[]{:S(2)}) async-start(), calls=%async_computation.2 | async-start | bytes 2097152 | tf_op jit(solution)/shard_map/psum | solution.py:45
  220.1 465.3 %all-reduce.9.cloned.1.call-start = ((), (), s32[]{:S(2)}) async-start(), calls=%async_computation.3 | async-start | bytes 3670016 | tf_op jit(solution)/shard_map/psum | solution.py:48
  377.9 1.7 copy-start.3
  436.7 78.2 %copy-start.2 = (f32[256,512]{1,0:T(8,128)S(1)}, f32[256,512]{1,0:T(8,128)}, u32[]{:S(2)}) copy-start(f32[256,512]{1,0:T(8,128)} %all-reduce.5.cloned.1.call-done) | copy-start | bytes 1572868
  474.6 44.0 %copy-start.1 = (f32[256,896]{1,0:T(8,128)S(1)}, f32[256,896]{1,0:T(8,128)}, u32[]{:S(2)}) copy-start(f32[256,896]{1,0:T(8,128)} %param.3) | copy-start | bytes 2752516
  474.6 44.0 %copy-start.4 = (bf16[256,896]{1,0:T(8,128)(2,1)S(1)}, bf16[256,896]{1,0:T(8,128)(2,1)}, u32[]{:S(2)}) copy-start(bf16[256,896]{1,0:T(8,128)(2,1)} %param.4) | copy-start | bytes 1376260
  516.8 1.2 copy-start.6
  518.0 0.6 copy-start.8
  685.4 29.2 %copy-start = (f32[896,512]{1,0:T(8,128)S(1)}, f32[896,512]{1,0:T(8,128)}, u32[]{:S(2)}) copy-start(f32[896,512]{1,0:T(8,128)} %all-reduce.9.cloned.1.call-done) | copy-start | bytes 5505028
  714.6 0.9 copy-start.7
  714.6 1.0 copy-start.9
  715.6 7.2 copy-start.5
Sparse Core Ops, SparseCore 0:
  11.2 85.0 all-gather.1
  101.1 115.6 all-reduce.4
  220.6 157.2 all-reduce.6
  523.0 162.3 all-reduce.8
where the time goes:
time: 738 us; the launch traced here: 735 us
  waiting for transfers between devices  525 us (71%)
  other arithmetic  122 us (17%)
  blocking collectives  27.4 us (4%)
  matrix products  26.9 us (4%)
  local copies, waits for them, and re-layouts  16.8 us (2%)
  between operations  16.8 us (2%)
    psum x1, waiting for transfers between devices, body(): right_factor = lax.psum(right_part, 'row')  162 us
    psum x1, waiting for transfers between devices, body(): gram_matrix = lax.psum(inner_rows(left_full, left_full), 'row')  157 us
    psum x1, waiting for transfers between devices, body(): left_full = lax.psum(left_part, 'col')  116 us
    all_gather x1, waiting for transfers between devices, body(): lax.all_gather(right_basis, 'row', axis=1, tiled=True)  88.4 us
    another operation x14, other arithmetic, solve_left(): chol_factor = jnp.linalg.cholesky(gram_matrix)  78.9 us
    another operation x3, other arithmetic, solve_left(): jax.scipy.linalg.solve_triangular(chol_factor, left_rows.T, lower=True)  40.5 us
    psum x1, blocking collectives, body(): squares = lax.psum(jnp.sum(right_factor * right_factor, axis=0), 'col')  27.4 us
  transfers between devices with their start and end apart: 4, of which 4 were waited for; matrix products, arithmetic and copies ran while one was open for 0% of the time, Pallas kernels for 0%

commit v1 on v0

v1 whole, which is shorter than its diff:
```python
import math

import jax
import jax.numpy as jnp
from jax import lax
from jax.experimental import pallas as pl
from jax.experimental.pallas import tpu as pltpu
from jax.sharding import PartitionSpec as P

ROWS = 8192
COLS = 14336
RANK = 512
BLOCK = 128
X, Y, Z, CORES = 4, 8, 8, 2


HIGH = lax.Precision.HIGH
HIGHEST = lax.Precision.HIGHEST
epsilon_norm = 1e-06
retain = 0.7


def dot(first, second, over, precision):
    return lax.dot_general(
        first, second, ((over[:1], over[1:]), ((), ())), precision=precision, preferred_element_type=jnp.float32
    )


def chips(way):
    upper = Z // 2
    row = lambda x, high, low: (x * upper + high) * 2 + low
    if way == "wide":
        return "row", [[row(x, high, low) for x in range(X) for low in range(2)] for high in range(upper)], 2 * X
    if way == "long":
        return "row", [[row(x, high, low) for high in range(upper)] for x in range(X) for low in range(2)], upper
    return "col", [[y * CORES + core for y in range(Y)] for core in range(CORES)], Y


def exchange(blocks, way):
    name, groups, _ = chips(way)
    return lax.all_to_all(blocks, name, 0, 0, axis_index_groups=groups, tiled=False)


def scatter_sum(whole, way):
    count = chips(way)[2]
    return jnp.sum(exchange(whole.reshape((count, whole.shape[0] // count) + whole.shape[1:]), way), axis=0)


def gather(part, way):
    count = chips(way)[2]
    return exchange(jnp.broadcast_to(part[None], (count,) + part.shape), way).reshape(
        (count * part.shape[0],) + part.shape[1:]
    )


def swap(part):
    return lax.ppermute(part, "col", [(i, i ^ 1) for i in range(Y * CORES)])


def halves(whole):
    half = whole.shape[0] // CORES
    core = lax.axis_index("col") % CORES
    return (
        lax.dynamic_slice_in_dim(whole, core * half, half, 0),
        lax.dynamic_slice_in_dim(whole, (1 - core) * half, half, 0),
    )


def join(own, other):
    first = lax.axis_index("col") % CORES == 0
    return jnp.concatenate([jnp.where(first, own, other), jnp.where(first, other, own)], axis=0)


def split(value):
    high = value.astype(jnp.bfloat16)
    return high, (value - high.astype(jnp.float32)).astype(jnp.bfloat16)


def dot3(first, second, over):
    one = lambda a, b: lax.dot_general(
        a, b, ((over[:1], over[1:]), ((), ())), preferred_element_type=jnp.float32
    )
    return one(first[0], second[0]) + (one(first[0], second[1]) + one(first[1], second[0]))


def products_kernel(left_ref, blended_ref, out_ref):
    half = left_ref.shape[0] // 2
    cols = blended_ref.shape[1]
    top, low = left_ref[:half, :], left_ref[half:, :]
    out_ref[:, :cols] = dot3(split(left_ref[...]), split(blended_ref[...]), (1, 0))
    out_ref[:half, cols : cols + half] = dot(top, top, (1, 1), HIGHEST)
    out_ref[half:, cols : cols + half] = dot(low, low, (1, 1), HIGHEST)
    across = dot(top, low, (1, 1), HIGHEST)
    out_ref[:half, cols + half :] = across[:, : half // 2]
    out_ref[half:, cols + half :] = across[:, half // 2 :]


def products(left, blended):
    rank, cols = left.shape[0], blended.shape[1]
    return pl.pallas_call(
        products_kernel,
        out_shape=jax.ShapeDtypeStruct((rank, cols + 3 * rank // 4), jnp.float32),
        in_specs=[pl.BlockSpec(memory_space=pltpu.VMEM)] * 2,
        out_specs=pl.BlockSpec(memory_space=pltpu.VMEM),
        compiler_params=pltpu.CompilerParams(vmem_limit_bytes=32 * 2**20),
        cost_estimate=pl.CostEstimate(flops=2 * 10**9, bytes_accessed=2 * 2**20, transcendentals=0),
        name="products",
    )(left, blended)


def invert_block(block):
    groups = BLOCK // 8
    sub = lax.broadcasted_iota(jnp.int32, (8, BLOCK), 0)
    lane = lax.broadcasted_iota(jnp.int32, (8, BLOCK), 1)
    work = [block[8 * q : 8 * q + 8, :] for q in range(groups)]
    side = [jnp.where(lane == sub + 8 * q, 1.0, 0.0).astype(jnp.float32) for q in range(groups)]
    out = []
    for p in range(groups):
        spread = {
            q: [jnp.broadcast_to(work[q][:, 8 * p + j : 8 * p + j + 1], (8, BLOCK)) for j in range(8)]
            for q in range(p, groups)
        }
        pivots = jnp.ones((8, BLOCK), jnp.float32)
        for j in range(8):
            row = [jnp.broadcast_to(spread[p][k][j : j + 1, :], (8, BLOCK)) for k in range(j, 8)]
            pivots = jnp.where(sub == j, row[0], pivots)
            inverse = 1.0 / row[0]
            row_work = jnp.broadcast_to(work[p][j : j + 1, :], (8, BLOCK))
            row_side = jnp.broadcast_to(side[p][j : j + 1, :], (8, BLOCK))
            for q in range(p, groups):
                times = spread[q][j] * inverse
                if q == p:
                    times = jnp.where(sub > j, times, 0.0)
                for k in range(j + 1, 8):
                    spread[q][k] = spread[q][k] - times * row[k - j]
                work[q] = work[q] - times * row_work
                side[q] = side[q] - times * row_side
        out.append(side[p] * lax.rsqrt(pivots))
    return jnp.concatenate(out, axis=0)


def factor_kernel(gram_ref, out_ref, work):
    rank = gram_ref.shape[0]
    half = rank // 2
    count = rank // BLOCK
    work[:half, : half + half // 2] = gram_ref[:half, :]
    work[half:, :half] = jnp.zeros((half, half), jnp.float32)
    work[half:, half:] = gram_ref[half:, :half]
    work[:half, half + half // 2 :] = gram_ref[half:, half:]
    rows = lax.broadcasted_iota(jnp.int32, (rank, rank), 0)
    cols = lax.broadcasted_iota(jnp.int32, (rank, rank), 1)
    out_ref[...] = jnp.where(rows == cols, 1.0, 0.0)

    def step(k, carry):
        at = pl.ds(pl.multiple_of(k * BLOCK, BLOCK), BLOCK)
        inverse = invert_block(work[at, at])
        upper = dot(inverse, work[at, :], (1, 0), HIGHEST)
        side = dot(inverse, out_ref[at, :], (1, 0), HIGHEST)
        out_ref[at, :] = side
        for i in range(1, count):

            @pl.when(i > k)
            def _():
                below = pl.ds(i * BLOCK, BLOCK)
                times = upper[:, i * BLOCK : (i + 1) * BLOCK]
                work[below, :] -= dot(times, upper, (0, 0), HIGHEST)
                out_ref[below, :] -= dot(times, side, (0, 0), HIGHEST)

        return carry

    lax.fori_loop(0, count, step, 0)


def inverse_factor(gram_matrix):
    rank = gram_matrix.shape[0]
    return pl.pallas_call(
        factor_kernel,
        out_shape=jax.ShapeDtypeStruct((rank, rank), jnp.float32),
        in_specs=[pl.BlockSpec(memory_space=pltpu.VMEM)],
        out_specs=pl.BlockSpec(memory_space=pltpu.VMEM),
        scratch_shapes=[pltpu.VMEM((rank, rank), jnp.float32)],
        compiler_params=pltpu.CompilerParams(vmem_limit_bytes=16 * 2**20),
        cost_estimate=pl.CostEstimate(flops=2 * 10**9, bytes_accessed=2 * 2**20, transcendentals=0),
        name="inverse_factor",
    )(gram_matrix)


def right_kernel(inverse_ref, raw_ref, left_ref, right_ref, ortho_ref, squares_ref):
    rank = inverse_ref.shape[0]
    raw, left = split(raw_ref[...]), split(left_ref[...])
    eye = lax.broadcasted_iota(jnp.int32, (BLOCK, BLOCK), 0) == lax.broadcasted_iota(jnp.int32, (BLOCK, BLOCK), 1)
    for i in range(rank // BLOCK):
        at, upto = pl.ds(i * BLOCK, BLOCK), (i + 1) * BLOCK
        inverse = split(inverse_ref[at, :upto])
        right = dot3(inverse, [part[:upto] for part in raw], (1, 0))
        right_ref[at, :] = right
        ortho_ref[at, :] = dot3(inverse, [part[:upto] for part in left], (1, 0))
        sums = jnp.sum(right * right, axis=1, keepdims=True)
        squares_ref[pl.ds(i, 1), :] = jnp.sum(jnp.where(eye, sums, 0.0), axis=0, keepdims=True)


def momentum_kernel(blended_ref, ortho_ref, right_ref, out_ref):
    out_ref[...] = blended_ref[...] - (1.0 - retain) * dot3(split(ortho_ref[...]), split(right_ref[...]), (0, 0))


def update_kernel(start_ref, squares_ref, ortho_ref, right_ref, update_ref, basis_ref, scaled):
    scale = math.sqrt(ROWS * COLS / RANK)
    rank, width = ortho_ref.shape[0], basis_ref.shape[0]
    rows = jnp.sum(squares_ref[...], axis=0)
    factors = lax.rsqrt(rows + epsilon_norm)
    eye = lax.broadcasted_iota(jnp.int32, (BLOCK, BLOCK), 0) == lax.broadcasted_iota(jnp.int32, (BLOCK, BLOCK), 1)
    for i in range(rank // BLOCK):
        at = pl.ds(i * BLOCK, BLOCK)
        column = jnp.sum(jnp.where(eye, factors[i : i + 1, :], 0.0), axis=1, keepdims=True)
        scaled[at, :] = jnp.broadcast_to(column, (BLOCK, BLOCK))
    ortho = ortho_ref[...] * (scale * scaled[:, :1])
    update_ref[...] = dot3(split(ortho), split(right_ref[...]), (0, 0))
    own = pl.ds(pl.multiple_of(start_ref[0], width), width)
    basis_ref[...] = right_ref[own, :] * scaled[own, :1]


VMEM = pl.BlockSpec(memory_space=pltpu.VMEM)


def call(kernel, name, shapes, specs, flops, *operands, scratch=()):
    return pl.pallas_call(
        kernel,
        out_shape=[jax.ShapeDtypeStruct(shape, jnp.float32) for shape in shapes],
        in_specs=specs,
        out_specs=[VMEM] * len(shapes),
        scratch_shapes=list(scratch),
        compiler_params=pltpu.CompilerParams(vmem_limit_bytes=32 * 2**20),
        cost_estimate=pl.CostEstimate(flops=flops, bytes_accessed=4 * 2**20, transcendentals=0),
        name=name,
    )(*operands)


def body(momentum, gradient, right_basis):
    rank = right_basis.shape[1] * lax.axis_size("row")
    scale = math.sqrt(ROWS * COLS / RANK)
    with jax.named_scope("basis_gather"):
        basis = gather(gather(right_basis.T, "long"), "wide")
    blended = momentum + gradient.astype(jnp.float32)
    with jax.named_scope("left"):
        left_own, left_other = halves(dot(basis, blended, (1, 1), HIGH))
        left_own = gather(scatter_sum(left_own + swap(left_other), "y"), "y")
        left = join(left_own, swap(left_own)).reshape(X, 2, Z // 2, -1, blended.shape[0])
        left = left.transpose(0, 2, 1, 3, 4).reshape(rank, blended.shape[0])
    with jax.named_scope("sums"):
        cols = blended.shape[1]
        sums = gather(scatter_sum(scatter_sum(products(left, blended), "wide"), "long"), "long")
        gram_matrix = gather(sums[:, cols:], "wide")
        right_raw = gather(sums[:, :cols], "wide")
    with jax.named_scope("factor"):
        inverse = inverse_factor(gram_matrix)
    rows = blended.shape[0]
    width = right_basis.shape[1]
    with jax.named_scope("right"):
        right, ortho, squares = call(
            right_kernel,
            "right",
            [(rank, cols), (rank, rows), (rank // BLOCK, BLOCK)],
            [VMEM] * 3,
            2 * 10**9,
            inverse,
            right_raw,
            left,
        )
    with jax.named_scope("squares"):
        peers = lax.axis_size("col")
        squares = lax.all_to_all(jnp.broadcast_to(squares[None], (peers,) + squares.shape), "col", 0, 0, tiled=False)
    with jax.named_scope("outputs"):
        (new_momentum,) = call(
            momentum_kernel, "momentum", [(rows, cols)], [VMEM] * 3, 10**9, blended, ortho, right
        )
        start = (lax.axis_index("row") * width).astype(jnp.int32).reshape(1)
        update, new_basis = call(
            update_kernel,
            "update",
            [(rows, cols), (width, cols)],
            [pl.BlockSpec(memory_space=pltpu.SMEM)] + [VMEM] * 3,
            10**9,
            start,
            squares,
            ortho,
            right,
            scratch=[pltpu.VMEM((rank, BLOCK), jnp.float32)],
        )
        new_basis = new_basis.T
    return (update, new_momentum, new_basis)


def solution(mesh):
    in_specs = (P("row", "col"), P("row", "col"), P("col", "row"))
    out_specs = (P("row", "col"), P("row", "col"), P("col", "row"))
    return jax.shard_map(body, mesh=mesh, in_specs=in_specs, out_specs=out_specs, check_vma=False)
```

time: 738 us -> 226 us (0.31)
  waiting for transfers between devices: 525 us -> 37.7 us
  other arithmetic: 122 us -> 2.29 us
  blocking collectives: 27.4 us -> 112 us
  Pallas kernels: 0 us -> 30.1 us
  starting transfers between devices: 0.45 us -> 30.1 us
  matrix products: 26.9 us -> 1.04 us
  between operations: 16.8 us -> 0.84 us
    psum x3 -> x0, waiting for transfers between devices: 436 us -> none  [the longest x1 162 us: body(): right_factor = lax.psum(right_part, 'row')]
    another operation x17 -> x0, other arithmetic: 119 us -> none  [the longest x14 78.9 us: solve_left(): chol_factor = jnp.linalg.cholesky(gram_matrix)]
    all_to_all x0 -> x6, blocking collectives: none -> 112 us  [exchange(): lax.all_to_all(blocks, name, 0, 0, axis_index_groups=groups, tiled=False)]
    all_gather x1 -> x0, waiting for transfers between devices: 88.4 us -> none  [body(): lax.all_gather(right_basis, 'row', axis=1, tiled=True)]
    all_to_all x0 -> x4, waiting for transfers between devices: none -> 35.4 us  [the longest x3 31.4 us: exchange(): lax.all_to_all(blocks, name, 0, 0, axis_index_groups=groups, tiled=False)]
    pallas_call x0 -> x5, Pallas kernels: none -> 30.1 us  [the longest x1 22.5 us: inverse_factor(): pl.pallas_call(factor_kernel, out_shape=jax.ShapeDtypeStruct((rank, rank)...]
    psum x1 -> x0, blocking collectives: 27.4 us -> none  [body(): squares = lax.psum(jnp.sum(right_factor * right_factor, axis=0), 'col')]
    dot_general x5 -> x1, matrix products: 22 us -> 1.04 us  [dot(): lax.dot_general(first, second, ((over[:1], over[1:]), ((), ())), precisio...]
  transfers between devices with their start and end apart: 4 -> 6, of which waited for: 4 -> 5; matrix products, arithmetic and copies ran while one was open for 0% -> 1% of each run, Pallas kernels for 0% -> 11%
where the time goes in v1:
time: 226 us; the launch traced here: 225 us
  blocking collectives  112 us (50%)
  waiting for transfers between devices  37.7 us (17%)
  starting transfers between devices  30.1 us (13%)
  Pallas kernels  30.1 us (13%)
  local copies, waits for them, and re-layouts  11.4 us (5%)
  other arithmetic  2.29 us (1%)
    all_to_all x6, blocking collectives, exchange(): lax.all_to_all(blocks, name, 0, 0, axis_index_groups=groups, tiled=False)  112 us
    all_to_all x3, waiting for transfers between devices, exchange(): lax.all_to_all(blocks, name, 0, 0, axis_index_groups=groups, tiled=False)  31.4 us
    pallas_call x1, Pallas kernels, inverse_factor(): pl.pallas_call(factor_kernel, out_shape=jax.ShapeDtypeStruct((rank, rank)...  22.5 us
    all_to_all x3, starting transfers between devices, exchange(): lax.all_to_all(blocks, name, 0, 0, axis_index_groups=groups, tiled=False)  13.5 us
    ppermute x2, starting transfers between devices, swap(): return lax.ppermute(part, 'col', [(i, i ^ 1) for i in range(Y * CORES)])  10.2 us
    all_to_all x1, starting transfers between devices, body(): lax.all_to_all(jnp.broadcast_to(squares[None], (peers,) + squares.shape),...  6.31 us
    unnamed x16, local copies, waits for them, and re-layouts  5.99 us
    pallas_call x3, Pallas kernels, call(): pl.pallas_call(kernel, out_shape=[jax.ShapeDtypeStruct(shape, jnp.float32...  5.93 us
  transfers between devices with their start and end apart: 6, of which 5 were waited for; matrix products, arithmetic and copies ran while one was open for 1% of the time, Pallas kernels for 11%

profile of v1, /device:TPU:1, one launch (start us, length us, event | category | flops | bytes accessed | tf_op | source)
XLA Modules:
  0.0 225.1 jit_solution(14009811690911668347)
XLA Ops:
  1.5 19.0 %all_to_all.50 = f32[4,16,896]{2,1,0:T(8,128)S(1)} all-to-all(f32[4,16,896]{2,1,0:T(8,128)S(1)} %broadcast_in_dim.16), channel_id=1, replica_groups={{0,32,64,96},{16,48,80,112},{128,160,192,224},{144,176,208,240},{256,28..., dimensions={0} | all-to-all | bytes 458752 | tf_op jit(solution)/shard_map/basis_gather/all_to_all | solution.py:41
  20.4 1.4 broadcast_in_dim.18
  21.8 6.2 %all-to-all-start.1 = ((f32[8,64,896]{2,1,0:T(8,128)}), f32[8,64,896]{2,1,0:T(8,128)S(1)}, u32[]{:S(2)}, u32[]{:S(2)}) async-start(f32[8,64,896]{2,1,0:T(8,128)} %broadcast_in_dim.18), calls=%async_computation.1 | async-start | bytes 3670016 | tf_op jit(solution)/shard_map/basis_gather/all_to_all | solution.py:41
  28.0 1.3 convert_add_fusion.blended_ref
  29.3 20.5 %all-to-all-done.1 = f32[8,64,896]{2,1,0:T(8,128)S(1)} async-done(((f32[8,64,896]{2,1,0:T(8,128)}), f32[8,64,896]{2,1,0:T(8,128)S(1)}, u32[]{:S(2)}, u32[]{:S(2)}) %all-to-all-start.1) | async-done | bytes 1835040 | tf_op jit(solution)/shard_map/basis_gather/all_to_all | solution.py:41
  49.9 1.0 fusion
  50.9 5.2 %collective-permute-start = (f32[256,256]{0,1:T(8,128)S(1)}, f32[256,256]{0,1:T(8,128)S(1)}, u32[]{:S(2)}, u32[]{:S(2)}) collective-permute-start(f32[256,256]{0,1:T(8,128)S(1)} %dynamic-slice_bitcast_fusion), channel_id=1, source_target_pairs={{0,1},{1,0},{2,3},{3,2},{4,5},{5,4},{6,7},{7,6},{8,9},{9,8},{10,11... | collective-permute-start | bytes 786440 | tf_op jit(solution)/shard_map/left/ppermute | solution.py:57
  56.1 1.1 collective-permute-done
  57.4 17.7 %all_to_all.51 = f32[8,32,256]{2,1,0:T(8,128)S(1)} all-to-all(f32[8,32,256]{2,1,0:T(8,128)S(1)} %bitcast.34), channel_id=1, replica_groups={{0,2,4,6,8,10,12,14},{1,3,5,7,9,11,13,15},{16,18,20,22,24,26,28,30},{17..., dimensions={0} | all-to-all | bytes 524288 | tf_op jit(solution)/shard_map/left/all_to_all | solution.py:41
  75.2 12.1 %all_to_all.52 = f32[8,32,256]{2,1,0:T(8,128)S(1)} all-to-all(f32[8,32,256]{2,1,0:T(8,128)S(1)} %broadcast_in_dim.19), channel_id=1, replica_groups={{0,2,4,6,8,10,12,14},{1,3,5,7,9,11,13,15},{16,18,20,22,24,26,28,30},{17..., dimensions={0} | all-to-all | bytes 524288 | tf_op jit(solution)/shard_map/left/all_to_all | solution.py:41
  87.3 5.0 %collective-permute-start.1 = (f32[256,256]{1,0:T(8,128)S(1)}, f32[256,256]{1,0:T(8,128)S(1)}, u32[]{:S(2)}, u32[]{:S(2)}) collective-permute-start(f32[256,256]{1,0:T(8,128)S(1)} %bitcast.35), channel_id=1, source_target_pairs={{0,1},{1,0},{2,3},{3,2},{4,5},{5,4},{6,7},{7,6},{8,9},{9,8},{10,11... | collective-permute-start | bytes 786440 | tf_op jit(solution)/shard_map/left/ppermute | solution.py:57
  92.4 1.1 collective-permute-done.1
  93.7 1.6 products.1
  95.3 34.7 %all_to_all.53 = f32[8,64,1280]{2,1,0:T(8,128)S(1)} all-to-all(f32[8,64,1280]{2,1,0:T(8,128)S(1)} %bitcast.24), channel_id=1, replica_groups={{0,16,128,144,256,272,384,400},{32,48,160,176,288,304,416,432},{64,80,1..., dimensions={0} | all-to-all | bytes 5242880 | tf_op jit(solution)/shard_map/sums/all_to_all | solution.py:41
  130.8 13.8 %all_to_all.54 = f32[4,16,1280]{2,1,0:T(8,128)S(1)} all-to-all(f32[4,16,1280]{2,1,0:T(8,128)} %bitcast.31), channel_id=1, replica_groups={{0,32,64,96},{16,48,80,112},{128,160,192,224},{144,176,208,240},{256,28..., dimensions={0} | all-to-all | bytes 655360 | tf_op jit(solution)/shard_map/sums/all_to_all | solution.py:41
  144.6 14.5 %all_to_all.55 = f32[4,16,1280]{2,1,0:T(8,128)S(1)} all-to-all(f32[4,16,1280]{2,1,0:T(8,128)S(1)} %broadcast_in_dim.20), channel_id=1, replica_groups={{0,32,64,96},{16,48,80,112},{128,160,192,224},{144,176,208,240},{256,28..., dimensions={0} | all-to-all | bytes 655360 | tf_op jit(solution)/shard_map/sums/all_to_all | solution.py:41
  159.2 0.9 broadcast_in_dim.21
  160.1 3.5 %all-to-all-start.7 = ((f32[8,64,384]{2,1,0:T(8,128)}), f32[8,64,384]{2,1,0:T(8,128)S(1)}, u32[]{:S(2)}, u32[]{:S(2)}) async-start(f32[8,64,384]{2,1,0:T(8,128)} %broadcast_in_dim.21), calls=%async_computation.7 | async-start | bytes 1572864 | tf_op jit(solution)/shard_map/sums/all_to_all | solution.py:41
  163.7 10.8 %all-to-all-done.7 = f32[8,64,384]{2,1,0:T(8,128)S(1)} async-done(((f32[8,64,384]{2,1,0:T(8,128)}), f32[8,64,384]{2,1,0:T(8,128)S(1)}, u32[]{:S(2)}, u32[]{:S(2)}) %all-to-all-start.7) | async-done | bytes 786464 | tf_op jit(solution)/shard_map/sums/all_to_all | solution.py:41
  174.5 1.4 broadcast_in_dim.22
  175.9 3.8 %all-to-all-start.8 = ((f32[8,64,896]{2,1,0:T(8,128)}), f32[8,64,896]{2,1,0:T(8,128)S(1)}, u32[]{:S(2)}, u32[]{:S(2)}) async-start(f32[8,64,896]{2,1,0:T(8,128)} %broadcast_in_dim.22), calls=%async_computation.8 | async-start | bytes 3670016 | tf_op jit(solution)/shard_map/sums/all_to_all | solution.py:41
  179.7 22.5 %inverse_factor.1.inverse_ref = f32[512,512]{1,0:T(8,128)S(1)} custom-call(f32[512,384]{1,0:T(8,128)S(1)} %bitcast.26), custom_call_target="tpu_custom_call" | custom-call | flops 2000000000 | bytes 2097152 | tf_op jit(solution)/shard_map/factor/inverse_factor/pallas_call | solution.py:176
  202.2 1.0 copy-done.5
  203.2 1.0 copy-done.4
  204.3 1.2 copy-done.6
  205.5 1.8 right.1
  207.3 1.2 copy-done
  209.1 6.3 %all-to-all-start.9 = ((f32[16,4,128]{2,1,0:T(4,128)}), f32[16,4,128]{2,1,0:T(4,128)S(1)}, u32[]{:S(2)}, u32[]{:S(2)}) async-start(f32[16,4,128]{2,1,0:T(4,128)} %broadcast_in_dim.23), calls=%async_computation.9 | async-start | bytes 65536 | tf_op jit(solution)/shard_map/squares/all_to_all | solution.py:271
  215.4 1.5 copy-done.1
  216.9 2.0 momentum.1
  218.9 4.0 %all-to-all-done.9.squares_ref = f32[16,4,128]{2,1,0:T(4,128)S(1)} async-done(((f32[16,4,128]{2,1,0:T(4,128)}), f32[16,4,128]{2,1,0:T(4,128)S(1)}, u32[]{:S(2)}, u32[]{:S(2)}) %all-to-all-start.9) | async-done | bytes 32800 | tf_op jit(solution)/shard_map/squares/all_to_all | solution.py:271
  222.9 2.2 update.1
  (27 shorter events, 2.8 us)
Async XLA Ops:
  21.8 6.2 %copy-start.7 = (bf16[256,896]{1,0:T(8,128)(2,1)S(1)}, bf16[256,896]{1,0:T(8,128)(2,1)}, u32[]{:S(2)}) copy-start(bf16[256,896]{1,0:T(8,128)(2,1)} %param.4) | copy-start | bytes 1376260
  21.8 28.0 %all-to-all-start.1 = ((f32[8,64,896]{2,1,0:T(8,128)}), f32[8,64,896]{2,1,0:T(8,128)S(1)}, u32[]{:S(2)}, u32[]{:S(2)}) async-start(f32[8,64,896]{2,1,0:T(8,128)} %broadcast_in_dim.18), calls=%async_computation.1 | async-start | bytes 3670016 | tf_op jit(solution)/shard_map/basis_gather/all_to_all | solution.py:41
  50.9 6.3 %collective-permute-start = (f32[256,256]{0,1:T(8,128)S(1)}, f32[256,256]{0,1:T(8,128)S(1)}, u32[]{:S(2)}, u32[]{:S(2)}) collective-permute-start(f32[256,256]{0,1:T(8,128)S(1)} %dynamic-slice_bitcast_fusion), channel_id=1, source_target_pairs={{0,1},{1,0},{2,3},{3,2},{4,5},{5,4},{6,7},{7,6},{8,9},{9,8},{10,11... | collective-permute-start | bytes 786440 | tf_op jit(solution)/shard_map/left/ppermute | solution.py:57
  87.3 6.2 %collective-permute-start.1 = (f32[256,256]{1,0:T(8,128)S(1)}, f32[256,256]{1,0:T(8,128)S(1)}, u32[]{:S(2)}, u32[]{:S(2)}) collective-permute-start(f32[256,256]{1,0:T(8,128)S(1)} %bitcast.35), channel_id=1, source_target_pairs={{0,1},{1,0},{2,3},{3,2},{4,5},{5,4},{6,7},{7,6},{8,9},{9,8},{10,11... | collective-permute-start | bytes 786440 | tf_op jit(solution)/shard_map/left/ppermute | solution.py:57
  93.6 1.6 copy-start.3
  160.1 14.4 %all-to-all-start.7 = ((f32[8,64,384]{2,1,0:T(8,128)}), f32[8,64,384]{2,1,0:T(8,128)S(1)}, u32[]{:S(2)}, u32[]{:S(2)}) async-start(f32[8,64,384]{2,1,0:T(8,128)} %broadcast_in_dim.21), calls=%async_computation.7 | async-start | bytes 1572864 | tf_op jit(solution)/shard_map/sums/all_to_all | solution.py:41
  175.9 27.3 %all-to-all-start.8 = ((f32[8,64,896]{2,1,0:T(8,128)}), f32[8,64,896]{2,1,0:T(8,128)S(1)}, u32[]{:S(2)}, u32[]{:S(2)}) async-start(f32[8,64,896]{2,1,0:T(8,128)} %broadcast_in_dim.22), calls=%async_computation.8 | async-start | bytes 3670016 | tf_op jit(solution)/shard_map/sums/all_to_all | solution.py:41
  202.2 1.0 copy-start.5
  203.2 1.0 copy-start.4
  204.3 1.2 copy-start.6
  207.3 1.3 copy-start
  209.1 13.8 %all-to-all-start.9 = ((f32[16,4,128]{2,1,0:T(4,128)}), f32[16,4,128]{2,1,0:T(4,128)S(1)}, u32[]{:S(2)}, u32[]{:S(2)}) async-start(f32[16,4,128]{2,1,0:T(4,128)} %broadcast_in_dim.23), calls=%async_computation.9 | async-start | bytes 65536 | tf_op jit(solution)/shard_map/squares/all_to_all | solution.py:271
  215.4 1.5 copy-start.1
  216.9 6.0 %copy-start.2 = (f32[512,896]{1,0:T(8,128)S(1)}, f32[512,896]{1,0:T(8,128)}, u32[]{:S(2)}) copy-start(f32[512,896]{1,0:T(8,128)} %copy-done) | copy-start | bytes 5505028

commit v2 on v1

--- a/solution.py
+++ b/solution.py
@@ -12,6 +12,10 @@
 RANK = 512
 BLOCK = 128
 X, Y, Z, CORES = 4, 8, 8, 2
+CORE_BLOCKS = (
+    ((0, 0), (0, 1), (0, 2), (0, 3), (1, 1)),
+    ((1, 2), (1, 3), (2, 2), (2, 3), (3, 3)),
+)
 
 
 HIGH = lax.Precision.HIGH
@@ -41,16 +45,16 @@
     return lax.all_to_all(blocks, name, 0, 0, axis_index_groups=groups, tiled=False)
 
 
-def scatter_sum(whole, way):
-    count = chips(way)[2]
-    return jnp.sum(exchange(whole.reshape((count, whole.shape[0] // count) + whole.shape[1:]), way), axis=0)
+def scatter_sum(blocks, way):
+    return jnp.sum(exchange(blocks, way), axis=0)
+
+
+def copies(part, way):
+    return jnp.broadcast_to(part[None], (chips(way)[2],) + part.shape)
 
 
 def gather(part, way):
-    count = chips(way)[2]
-    return exchange(jnp.broadcast_to(part[None], (count,) + part.shape), way).reshape(
-        (count * part.shape[0],) + part.shape[1:]
-    )
+    return exchange(copies(part, way), way)
 
 
 def swap(part):
@@ -83,29 +87,40 @@
     return one(first[0], second[0]) + (one(first[0], second[1]) + one(first[1], second[0]))
 
 
-def products_kernel(left_ref, blended_ref, out_ref):
-    half = left_ref.shape[0] // 2
-    cols = blended_ref.shape[1]
-    top, low = left_ref[:half, :], left_ref[half:, :]
-    out_ref[:, :cols] = dot3(split(left_ref[...]), split(blended_ref[...]), (1, 0))
-    out_ref[:half, cols : cols + half] = dot(top, top, (1, 1), HIGHEST)
-    out_ref[half:, cols : cols + half] = dot(low, low, (1, 1), HIGHEST)
-    across = dot(top, low, (1, 1), HIGHEST)
-    out_ref[:half, cols + half :] = across[:, : half // 2]
-    out_ref[half:, cols + half :] = across[:, half // 2 :]
-
-
-def products(left, blended):
-    rank, cols = left.shape[0], blended.shape[1]
-    return pl.pallas_call(
-        products_kernel,
-        out_shape=jax.ShapeDtypeStruct((rank, cols + 3 * rank // 4), jnp.float32),
-        in_specs=[pl.BlockSpec(memory_space=pltpu.VMEM)] * 2,
-        out_specs=pl.BlockSpec(memory_space=pltpu.VMEM),
-        compiler_params=pltpu.CompilerParams(vmem_limit_bytes=32 * 2**20),
-        cost_estimate=pl.CostEstimate(flops=2 * 10**9, bytes_accessed=2 * 2**20, transcendentals=0),
-        name="products",
-    )(left, blended)
+def square(k):
+    return pl.ds(k * BLOCK, BLOCK)
+
+
+def products_kernel(core_ref, left_ref, blended_ref, out_ref):
+    members, uppers = out_ref.shape[:2]
+    deep = left_ref.shape[0] // (8 * members * uppers)
+    lanes = blended_ref.shape[1] // BLOCK
+    right = dot3(split(left_ref[...]), split(blended_ref[...]), (1, 0))
+    for j in range(lanes):
+        tiles = right[:, j * BLOCK : (j + 1) * BLOCK].reshape(members, uppers, deep, 8, BLOCK)
+        for i in range(deep):
+            out_ref[:, :, i * lanes + j] = tiles[:, :, i]
+
+    def gram(blocks):
+        found = [dot(left_ref[square(k), :], left_ref[square(l), :], (1, 1), HIGHEST) for k, l in blocks]
+        found.append(jnp.zeros((BLOCK, BLOCK), jnp.float32))
+        for t in range(len(found) // 2):
+            pair = jnp.concatenate(found[2 * t : 2 * t + 2], axis=0)
+            out_ref[:, :, deep * lanes + t] = pair.reshape(members, uppers, 8, BLOCK)
+
+    pl.when(core_ref[0] == 0)(lambda: gram(CORE_BLOCKS[0]))
+    pl.when(core_ref[0] != 0)(lambda: gram(CORE_BLOCKS[1]))
+
+
+def copies_kernel(sums_ref, out_ref):
+    members, rows, cols = out_ref.shape
+    uppers = sums_ref.shape[0]
+    deep, lanes = rows // (8 * uppers), cols // BLOCK
+    for j in range(lanes):
+        tiles = [sums_ref[:, i * lanes + j] for i in range(deep)]
+        piece = jnp.stack(tiles, axis=1).reshape(rows, BLOCK)
+        for member in range(members):
+            out_ref[member, :, j * BLOCK : (j + 1) * BLOCK] = piece
 
 
 def invert_block(block):
@@ -139,14 +154,20 @@
     return jnp.concatenate(out, axis=0)
 
 
-def factor_kernel(gram_ref, out_ref, work):
-    rank = gram_ref.shape[0]
-    half = rank // 2
+def factor_kernel(core_ref, own_ref, other_ref, out_ref, work):
+    rank = out_ref.shape[0]
     count = rank // BLOCK
-    work[:half, : half + half // 2] = gram_ref[:half, :]
-    work[half:, :half] = jnp.zeros((half, half), jnp.float32)
-    work[half:, half:] = gram_ref[half:, :half]
-    work[:half, half + half // 2 :] = gram_ref[half:, half:]
+    work[...] = jnp.zeros((rank, rank), jnp.float32)
+
+    def place(parts):
+        for part_ref, blocks in zip(parts, CORE_BLOCKS):
+            half = part_ref.shape[0] // 2
+            for i, (k, l) in enumerate(blocks):
+                tiles = part_ref[i % 2 * half : (i % 2 + 1) * half, :, i // 2]
+                work[square(k), square(l)] = tiles.reshape(BLOCK, BLOCK)
+
+    pl.when(core_ref[0] == 0)(lambda: place((own_ref, other_ref)))
+    pl.when(core_ref[0] != 0)(lambda: place((other_ref, own_ref)))
     rows = lax.broadcasted_iota(jnp.int32, (rank, rank), 0)
     cols = lax.broadcasted_iota(jnp.int32, (rank, rank), 1)
     out_ref[...] = jnp.where(rows == cols, 1.0, 0.0)
@@ -169,20 +190,6 @@
         return carry
 
     lax.fori_loop(0, count, step, 0)
-
-
-def inverse_factor(gram_matrix):
-    rank = gram_matrix.shape[0]
-    return pl.pallas_call(
-        factor_kernel,
-        out_shape=jax.ShapeDtypeStruct((rank, rank), jnp.float32),
-        in_specs=[pl.BlockSpec(memory_space=pltpu.VMEM)],
-        out_specs=pl.BlockSpec(memory_space=pltpu.VMEM),
-        scratch_shapes=[pltpu.VMEM((rank, rank), jnp.float32)],
-        compiler_params=pltpu.CompilerParams(vmem_limit_bytes=16 * 2**20),
-        cost_estimate=pl.CostEstimate(flops=2 * 10**9, bytes_accessed=2 * 2**20, transcendentals=0),
-        name="inverse_factor",
-    )(gram_matrix)
 
 
 def right_kernel(inverse_ref, raw_ref, left_ref, right_ref, ortho_ref, squares_ref):
@@ -220,71 +227,72 @@
 
 
 VMEM = pl.BlockSpec(memory_space=pltpu.VMEM)
-
-
-def call(kernel, name, shapes, specs, flops, *operands, scratch=()):
+SMEM = pl.BlockSpec(memory_space=pltpu.SMEM)
+
+
+def call(kernel, name, shapes, flops, *operands, scratch=(), limit=10):
     return pl.pallas_call(
         kernel,
         out_shape=[jax.ShapeDtypeStruct(shape, jnp.float32) for shape in shapes],
-        in_specs=specs,
+        in_specs=[SMEM if operand.dtype == jnp.int32 else VMEM for operand in operands],
         out_specs=[VMEM] * len(shapes),
         scratch_shapes=list(scratch),
-        compiler_params=pltpu.CompilerParams(vmem_limit_bytes=32 * 2**20),
+        compiler_params=pltpu.CompilerParams(vmem_limit_bytes=limit * 2**20),
         cost_estimate=pl.CostEstimate(flops=flops, bytes_accessed=4 * 2**20, transcendentals=0),
         name=name,
     )(*operands)
 
 
 def body(momentum, gradient, right_basis):
-    rank = right_basis.shape[1] * lax.axis_size("row")
-    scale = math.sqrt(ROWS * COLS / RANK)
+    cols, width = right_basis.shape
+    rows = momentum.shape[0]
+    rank = width * lax.axis_size("row")
+    members, uppers = chips("wide")[2], chips("long")[2]
+    core = (lax.axis_index("col") % CORES).astype(jnp.int32).reshape(1)
     with jax.named_scope("basis_gather"):
-        basis = gather(gather(right_basis.T, "long"), "wide")
+        basis = gather(gather(right_basis.T, "long"), "wide").reshape(rank, cols)
     blended = momentum + gradient.astype(jnp.float32)
     with jax.named_scope("left"):
         left_own, left_other = halves(dot(basis, blended, (1, 1), HIGH))
-        left_own = gather(scatter_sum(left_own + swap(left_other), "y"), "y")
-        left = join(left_own, swap(left_own)).reshape(X, 2, Z // 2, -1, blended.shape[0])
-        left = left.transpose(0, 2, 1, 3, 4).reshape(rank, blended.shape[0])
+        left_own = left_own + swap(left_other)
+        left_own = gather(scatter_sum(left_own.reshape(Y, -1, rows), "y"), "y").reshape(-1, rows)
+        left = join(left_own, swap(left_own)).reshape(X, 2, uppers, width, rows)
+        left = left.transpose(0, 2, 1, 3, 4).reshape(rank, rows)
     with jax.named_scope("sums"):
-        cols = blended.shape[1]
-        sums = gather(scatter_sum(scatter_sum(products(left, blended), "wide"), "long"), "long")
-        gram_matrix = gather(sums[:, cols:], "wide")
-        right_raw = gather(sums[:, :cols], "wide")
+        tiles = width // 8 * (cols // BLOCK)
+        per_core = (len(CORE_BLOCKS[0]) + 1) // 2
+        shape = (members, uppers, tiles + per_core, 8, BLOCK)
+        (sums,) = call(products_kernel, "products", [shape], 2 * 10**9, core, left, blended)
+        sums = gather(scatter_sum(scatter_sum(sums, "wide"), "long"), "long")
+        gram_own = gather(sums[:, tiles:], "wide")
+        (raw,) = call(copies_kernel, "copies", [(members, rank // members, cols)], 10**6, sums)
+        gram_own, raw = lax.optimization_barrier((gram_own, raw))
+        gram_other = swap(gram_own)
+        right_raw = exchange(raw, "wide").reshape(rank, cols)
     with jax.named_scope("factor"):
-        inverse = inverse_factor(gram_matrix)
-    rows = blended.shape[0]
-    width = right_basis.shape[1]
+        (inverse,) = call(
+            factor_kernel,
+            "inverse_factor",
+            [(rank, rank)],
+            2 * 10**9,
+            core,
+            gram_own,
+            gram_other,
+            scratch=[pltpu.VMEM((rank, rank), jnp.float32)],
+        )
     with jax.named_scope("right"):
-        right, ortho, squares = call(
-            right_kernel,
-            "right",
-            [(rank, cols), (rank, rows), (rank // BLOCK, BLOCK)],
-            [VMEM] * 3,
-            2 * 10**9,
-            inverse,
-            right_raw,
-            left,
-        )
+        shapes = [(rank, cols), (rank, rows), (rank // BLOCK, BLOCK)]
+        right, ortho, squares = call(right_kernel, "right", shapes, 2 * 10**9, inverse, right_raw, left)
     with jax.named_scope("squares"):
-        peers = lax.axis_size("col")
-        squares = lax.all_to_all(jnp.broadcast_to(squares[None], (peers,) + squares.shape), "col", 0, 0, tiled=False)
+        squares = jnp.broadcast_to(squares[None], (lax.axis_size("col"),) + squares.shape)
+        squares = lax.all_to_all(squares, "col", 0, 0, tiled=False)
     with jax.named_scope("outputs"):
-        (new_momentum,) = call(
-            momentum_kernel, "momentum", [(rows, cols)], [VMEM] * 3, 10**9, blended, ortho, right
-        )
+        (new_momentum,) = call(momentum_kernel, "momentum", [(rows, cols)], 10**9, blended, ortho, right)
         start = (lax.axis_index("row") * width).astype(jnp.int32).reshape(1)
+        shapes = [(rows, cols), (width, cols)]
+        scratch = [pltpu.VMEM((rank, BLOCK), jnp.float32)]
         update, new_basis = call(
-            update_kernel,
-            "update",
-            [(rows, cols), (width, cols)],
-            [pl.BlockSpec(memory_space=pltpu.SMEM)] + [VMEM] * 3,
-            10**9,
-            start,
-            squares,
-            ortho,
-            right,
-            scratch=[pltpu.VMEM((rank, BLOCK), jnp.float32)],
+            update_kernel, "update", shapes, 10**9, start, squares, ortho, right, scratch=scratch
         )
         new_basis = new_basis.T
     return (update, new_momentum, new_basis)

time: 226 us -> 221 us (0.978)
  blocking collectives: 112 us -> 104 us
  waiting for transfers between devices: 37.7 us -> 32.8 us
  starting transfers between devices: 30.1 us -> 33.7 us
  Pallas kernels: 30.1 us -> 32.8 us
    pallas_call x3 -> x6, Pallas kernels: 5.93 us -> 32.8 us  [call(): pl.pallas_call(kernel, out_shape=[jax.ShapeDtypeStruct(shape, jnp.float32...]
    pallas_call x2 -> x0, Pallas kernels: 24.1 us -> none  [the longest x1 22.5 us: inverse_factor(): pl.pallas_call(factor_kernel, out_shape=jax.ShapeDtypeStruct((rank, rank)...]
    all_to_all x6, blocking collectives: 112 us -> 104 us  [exchange(): lax.all_to_all(blocks, name, 0, 0, axis_index_groups=groups, tiled=False)]
    ppermute x2 -> x3, starting transfers between devices: 10.2 us -> 16.8 us  [swap(): return lax.ppermute(part, 'col', [(i, i ^ 1) for i in range(Y * CORES)])]
    all_to_all x3, waiting for transfers between devices: 31.4 us -> 25.9 us  [exchange(): lax.all_to_all(blocks, name, 0, 0, axis_index_groups=groups, tiled=False)]
    all_to_all x1, starting transfers between devices: 6.31 us -> 3.66 us  [body(): squares = lax.all_to_all(squares, 'col', 0, 0, tiled=False)]
    unnamed x16 -> x22, local copies, waits for them, and re-layouts: 5.99 us -> 8.56 us
    broadcast_in_dim x7 -> x6, local copies, waits for them, and re-layouts: 5.2 us -> 3.7 us  [the longest x5 3.08 us: copies(): return jnp.broadcast_to(part[None], (chips(way)[2],) + part.shape)]
  transfers between devices with their start and end apart: 6 -> 7, of which waited for: 5 -> 6; matrix products, arithmetic and copies ran while one was open for 1% -> 1% of each run, Pallas kernels for 11% -> 12%
where the time goes in v2:
time: 221 us; the launch traced here: 220 us
  blocking collectives  104 us (47%)
  starting transfers between devices  33.7 us (15%)
  waiting for transfers between devices  32.8 us (15%)
  Pallas kernels  32.8 us (15%)
  local copies, waits for them, and re-layouts  12.5 us (6%)
  other arithmetic  3.18 us (1%)
    all_to_all x6, blocking collectives, exchange(): lax.all_to_all(blocks, name, 0, 0, axis_index_groups=groups, tiled=False)  104 us
    pallas_call x6, Pallas kernels, call(): pl.pallas_call(kernel, out_shape=[jax.ShapeDtypeStruct(shape, jnp.float32...  32.8 us
    all_to_all x3, waiting for transfers between devices, exchange(): lax.all_to_all(blocks, name, 0, 0, axis_index_groups=groups, tiled=False)  25.9 us
    ppermute x3, starting transfers between devices, swap(): return lax.ppermute(part, 'col', [(i, i ^ 1) for i in range(Y * CORES)])  16.8 us
    all_to_all x3, starting transfers between devices, exchange(): lax.all_to_all(blocks, name, 0, 0, axis_index_groups=groups, tiled=False)  13.3 us
    unnamed x22, local copies, waits for them, and re-layouts  8.56 us
  transfers between devices with their start and end apart: 7, of which 6 were waited for; matrix products, arithmetic and copies ran while one was open for 1% of the time, Pallas kernels for 12%

profile of v2, /device:TPU:1, one launch (start us, length us, event | category | flops | bytes accessed | tf_op | source)
XLA Modules:
  0.0 220.4 jit_solution(17291062805984383836)
XLA Ops:
  1.5 19.0 %all_to_all.50 = f32[4,16,896]{2,1,0:T(8,128)S(1)} all-to-all(f32[4,16,896]{2,1,0:T(8,128)S(1)} %broadcast_in_dim.12), channel_id=1, replica_groups={{0,32,64,96},{16,48,80,112},{128,160,192,224},{144,176,208,240},{256,28..., dimensions={0} | all-to-all | bytes 458752 | tf_op jit(solution)/shard_map/basis_gather/all_to_all | solution.py:45
  20.4 1.4 broadcast_in_dim.13
  21.9 6.2 %all-to-all-start.1 = ((f32[8,4,16,896]{3,2,1,0:T(8,128)}), f32[8,4,16,896]{3,2,1,0:T(8,128)S(1)}, u32[]{:S(2)}, u32[]{:S(2)}) async-start(f32[8,4,16,896]{3,2,1,0:T(8,128)} %broadcast_in_dim.13), calls=%async_computation.1 | async-start | bytes 3670016 | tf_op jit(solution)/shard_map/basis_gather/all_to_all | solution.py:45
  28.1 1.3 convert_add_fusion.blended_ref
  29.4 20.5 %all-to-all-done.1 = f32[8,4,16,896]{3,2,1,0:T(8,128)S(1)} async-done(((f32[8,4,16,896]{3,2,1,0:T(8,128)}), f32[8,4,16,896]{3,2,1,0:T(8,128)S(1)}, u32[]{:S(2)}, u32[]{:S(2)}) %all-to-all-start.1) | async-done | bytes 1835040 | tf_op jit(solution)/shard_map/basis_gather/all_to_all | solution.py:45
  49.9 1.0 fusion
  51.0 5.2 %collective-permute-start = (f32[256,256]{0,1:T(8,128)S(1)}, f32[256,256]{0,1:T(8,128)S(1)}, u32[]{:S(2)}, u32[]{:S(2)}) collective-permute-start(f32[256,256]{0,1:T(8,128)S(1)} %dynamic-slice_bitcast_fusion), channel_id=1, source_target_pairs={{0,1},{1,0},{2,3},{3,2},{4,5},{5,4},{6,7},{7,6},{8,9},{9,8},{10,11... | collective-permute-start | bytes 786440 | tf_op jit(solution)/shard_map/left/ppermute | solution.py:61
  56.2 1.1 collective-permute-done
  57.5 17.7 %all_to_all.51 = f32[8,32,256]{2,1,0:T(8,128)S(1)} all-to-all(f32[8,32,256]{2,1,0:T(8,128)S(1)} %bitcast.25), channel_id=1, replica_groups={{0,2,4,6,8,10,12,14},{1,3,5,7,9,11,13,15},{16,18,20,22,24,26,28,30},{17..., dimensions={0} | all-to-all | bytes 524288 | tf_op jit(solution)/shard_map/left/all_to_all | solution.py:45
  75.3 12.1 %all_to_all.52 = f32[8,32,256]{2,1,0:T(8,128)S(1)} all-to-all(f32[8,32,256]{2,1,0:T(8,128)S(1)} %broadcast_in_dim.14), channel_id=1, replica_groups={{0,2,4,6,8,10,12,14},{1,3,5,7,9,11,13,15},{16,18,20,22,24,26,28,30},{17..., dimensions={0} | all-to-all | bytes 524288 | tf_op jit(solution)/shard_map/left/all_to_all | solution.py:45
  87.4 5.0 %collective-permute-start.1 = (f32[256,256]{1,0:T(8,128)S(1)}, f32[256,256]{1,0:T(8,128)S(1)}, u32[]{:S(2)}, u32[]{:S(2)}) collective-permute-start(f32[256,256]{1,0:T(8,128)S(1)} %bitcast.26), channel_id=1, source_target_pairs={{0,1},{1,0},{2,3},{3,2},{4,5},{5,4},{6,7},{7,6},{8,9},{9,8},{10,11... | collective-permute-start | bytes 786440 | tf_op jit(solution)/shard_map/left/ppermute | solution.py:61
  92.4 1.1 collective-permute-done.1
  93.7 1.7 products.1
  95.4 31.2 %all_to_all.53 = f32[8,4,17,8,128]{4,3,2,1,0:T(8,128)} all-to-all(f32[8,4,17,8,128]{4,3,2,1,0:T(8,128)S(1)} %products.1), channel_id=1, replica_groups={{0,16,128,144,256,272,384,400},{32,48,160,176,288,304,416,432},{64,80,1..., dimensions={0} | all-to-all | bytes 4456448 | tf_op jit(solution)/shard_map/sums/all_to_all | solution.py:45
  126.6 1.8 reduce_sum.28
  128.4 10.9 %all_to_all.54 = f32[4,17,8,128]{3,2,1,0:T(8,128)S(1)} all-to-all(f32[4,17,8,128]{3,2,1,0:T(8,128)S(1)} %reduce_sum.28), channel_id=1, replica_groups={{0,32,64,96},{16,48,80,112},{128,160,192,224},{144,176,208,240},{256,28..., dimensions={0} | all-to-all | bytes 557056 | tf_op jit(solution)/shard_map/sums/all_to_all | solution.py:45
  139.3 12.6 %all_to_all.55.sums_ref = f32[4,17,8,128]{3,2,1,0:T(8,128)S(1)} all-to-all(f32[4,17,8,128]{3,2,1,0:T(8,128)S(1)} %broadcast_in_dim.15), channel_id=1, replica_groups={{0,32,64,96},{16,48,80,112},{128,160,192,224},{144,176,208,240},{256,28..., dimensions={0} | all-to-all | bytes 557056 | tf_op jit(solution)/shard_map/sums/all_to_all | solution.py:45
  152.7 3.5 %all-to-all-start.7 = ((f32[8,4,3,8,128]{4,3,2,1,0:T(8,128)}), f32[8,4,3,8,128]{4,3,2,1,0:T(8,128)S(1)}, u32[]{:S(2)}, u32[]{:S(2)}) async-start(f32[8,4,3,8,128]{4,3,2,1,0:T(8,128)} %broadcast_in_dim.16), calls=%async_computation.7 | async-start | bytes 786432 | tf_op jit(solution)/shard_map/sums/all_to_all | solution.py:45
  156.2 1.4 copies.1
  157.6 5.4 %all-to-all-done.7.own_ref = f32[8,4,3,8,128]{4,3,2,1,0:T(8,128)S(1)} async-done(((f32[8,4,3,8,128]{4,3,2,1,0:T(8,128)}), f32[8,4,3,8,128]{4,3,2,1,0:T(8,128)S(1)}, u32[]{:S(2)}, u32[]{:S(2)}) %all-to-all-start.7) | async-done | bytes 393248 | tf_op jit(solution)/shard_map/sums/all_to_all | solution.py:45
  163.7 3.6 %all-to-all-start.8 = ((f32[8,64,896]{2,1,0:T(8,128)}), f32[8,64,896]{2,1,0:T(8,128)S(1)}, u32[]{:S(2)}, u32[]{:S(2)}) async-start(f32[8,64,896]{2,1,0:T(8,128)} %copies.1), calls=%async_computation.8 | async-start | bytes 3670016 | tf_op jit(solution)/shard_map/sums/all_to_all | solution.py:45
  167.3 6.6 %collective-permute-start.2 = (f32[8,4,3,8,128]{4,3,2,1,0:T(8,128)}, f32[8,4,3,8,128]{4,3,2,1,0:T(8,128)}, u32[]{:S(2)}, u32[]{:S(2)}) collective-permute-start(f32[8,4,3,8,128]{4,3,2,1,0:T(8,128)} %copy-done.6), channel_id=1, source_target_pairs={{0,1},{1,0},{2,3},{3,2},{4,5},{5,4},{6,7},{7,6},{8,9},{9,8},{10,11... | collective-permute-start | bytes 1179656 | tf_op jit(solution)/shard_map/sums/ppermute | solution.py:61
  173.9 1.7 collective-permute-done.2.other_ref
  176.5 23.7 %inverse_factor.1.inverse_ref = f32[512,512]{1,0:T(8,128)S(1)} custom-call(s32[1]{0:T(128)} %bitcast.1.core_ref, f32[8,4,3,8,128]{4,3,2,1,0:T(8,128)S(1)} %copy-done.7, f32[8,4,3,8,128]{4,3,2,1,0:T(8,128)} %collective-permute-done.2.other_ref), custom_call_target="tpu_custom_call" | custom-call | flops 2000000000 | bytes 4194304 | tf_op jit(solution)/shard_map/factor/inverse_factor/pallas_call | solution.py:234
  201.3 1.2 copy-done.9
  202.5 1.8 right.1
  204.4 1.3 copy-done
  207.0 3.7 %all-to-all-start.9 = ((f32[16,4,128]{2,1,0:T(4,128)}), f32[16,4,128]{2,1,0:T(4,128)S(1)}, u32[]{:S(2)}, u32[]{:S(2)}) async-start(f32[16,4,128]{2,1,0:T(4,128)} %broadcast_in_dim.17), calls=%async_computation.9 | async-start | bytes 65536 | tf_op jit(solution)/shard_map/squares/all_to_all | solution.py:288
  210.7 1.5 copy-done.1
  213.2 2.0 momentum.1
  215.2 3.0 %all-to-all-done.9.squares_ref = f32[16,4,128]{2,1,0:T(4,128)S(1)} async-done(((f32[16,4,128]{2,1,0:T(4,128)}), f32[16,4,128]{2,1,0:T(4,128)S(1)}, u32[]{:S(2)}, u32[]{:S(2)}) %all-to-all-start.9) | async-done | bytes 32800 | tf_op jit(solution)/shard_map/squares/all_to_all | solution.py:288
  218.2 2.2 update.1
  (34 shorter events, 7.2 us)
Async XLA Ops:
  21.9 6.2 %copy-start.10 = (bf16[256,896]{1,0:T(8,128)(2,1)S(1)}, bf16[256,896]{1,0:T(8,128)(2,1)}, u32[]{:S(2)}) copy-start(bf16[256,896]{1,0:T(8,128)(2,1)} %param.4) | copy-start | bytes 1376260
  21.9 28.0 %all-to-all-start.1 = ((f32[8,4,16,896]{3,2,1,0:T(8,128)}), f32[8,4,16,896]{3,2,1,0:T(8,128)S(1)}, u32[]{:S(2)}, u32[]{:S(2)}) async-start(f32[8,4,16,896]{3,2,1,0:T(8,128)} %broadcast_in_dim.13), calls=%async_computation.1 | async-start | bytes 3670016 | tf_op jit(solution)/shard_map/basis_gather/all_to_all | solution.py:45
  51.0 6.3 %collective-permute-start = (f32[256,256]{0,1:T(8,128)S(1)}, f32[256,256]{0,1:T(8,128)S(1)}, u32[]{:S(2)}, u32[]{:S(2)}) collective-permute-start(f32[256,256]{0,1:T(8,128)S(1)} %dynamic-slice_bitcast_fusion), channel_id=1, source_target_pairs={{0,1},{1,0},{2,3},{3,2},{4,5},{5,4},{6,7},{7,6},{8,9},{9,8},{10,11... | collective-permute-start | bytes 786440 | tf_op jit(solution)/shard_map/left/ppermute | solution.py:61
  87.4 6.2 %collective-permute-start.1 = (f32[256,256]{1,0:T(8,128)S(1)}, f32[256,256]{1,0:T(8,128)S(1)}, u32[]{:S(2)}, u32[]{:S(2)}) collective-permute-start(f32[256,256]{1,0:T(8,128)S(1)} %bitcast.26), channel_id=1, source_target_pairs={{0,1},{1,0},{2,3},{3,2},{4,5},{5,4},{6,7},{7,6},{8,9},{9,8},{10,11... | collective-permute-start | bytes 786440 | tf_op jit(solution)/shard_map/left/ppermute | solution.py:61
  152.7 10.2 %all-to-all-start.7 = ((f32[8,4,3,8,128]{4,3,2,1,0:T(8,128)}), f32[8,4,3,8,128]{4,3,2,1,0:T(8,128)S(1)}, u32[]{:S(2)}, u32[]{:S(2)}) async-start(f32[8,4,3,8,128]{4,3,2,1,0:T(8,128)} %broadcast_in_dim.16), calls=%async_computation.7 | async-start | bytes 786432 | tf_op jit(solution)/shard_map/sums/all_to_all | solution.py:45
  162.9 0.7 copy-start.6
  163.7 37.6 %all-to-all-start.8 = ((f32[8,64,896]{2,1,0:T(8,128)}), f32[8,64,896]{2,1,0:T(8,128)S(1)}, u32[]{:S(2)}, u32[]{:S(2)}) async-start(f32[8,64,896]{2,1,0:T(8,128)} %copies.1), calls=%async_computation.8 | async-start | bytes 3670016 | tf_op jit(solution)/shard_map/sums/all_to_all | solution.py:45
  167.3 8.3 %collective-permute-start.2 = (f32[8,4,3,8,128]{4,3,2,1,0:T(8,128)}, f32[8,4,3,8,128]{4,3,2,1,0:T(8,128)}, u32[]{:S(2)}, u32[]{:S(2)}) collective-permute-start(f32[8,4,3,8,128]{4,3,2,1,0:T(8,128)} %copy-done.6), channel_id=1, source_target_pairs={{0,1},{1,0},{2,3},{3,2},{4,5},{5,4},{6,7},{7,6},{8,9},{9,8},{10,11... | collective-permute-start | bytes 1179656 | tf_op jit(solution)/shard_map/sums/ppermute | solution.py:61
  175.5 1.0 copy-start.7
  200.3 1.0 copy-start.8
  201.3 1.2 copy-start.9
  204.3 1.3 copy-start
  205.6 0.8 copy-start.3
  207.0 11.1 %all-to-all-start.9 = ((f32[16,4,128]{2,1,0:T(4,128)}), f32[16,4,128]{2,1,0:T(4,128)S(1)}, u32[]{:S(2)}, u32[]{:S(2)}) async-start(f32[16,4,128]{2,1,0:T(4,128)} %broadcast_in_dim.17), calls=%async_computation.9 | async-start | bytes 65536 | tf_op jit(solution)/shard_map/squares/all_to_all | solution.py:288
  210.7 1.5 copy-start.1
  212.2 1.0 copy-start.4
  213.2 4.9 %copy-start.2 = (f32[512,896]{1,0:T(8,128)S(1)}, f32[512,896]{1,0:T(8,128)}, u32[]{:S(2)}) copy-start(f32[512,896]{1,0:T(8,128)} %copy-done) | copy-start | bytes 5505028
  213.2 4.9 %copy-start.5 = (f32[512,256]{1,0:T(8,128)S(1)}, f32[512,256]{1,0:T(8,128)}, u32[]{:S(2)}) copy-start(f32[512,256]{1,0:T(8,128)} %copy-done.3) | copy-start | bytes 1572868

commit v3 on v2

--- a/solution.py
+++ b/solution.py
@@ -154,9 +154,15 @@
     return jnp.concatenate(out, axis=0)
 
 
-def factor_kernel(core_ref, own_ref, other_ref, out_ref, work):
+def factor_kernel(core_ref, own_hbm, other_hbm, out_hbm, own_ref, other_ref, out_ref, work, sems):
     rank = out_ref.shape[0]
     count = rank // BLOCK
+    arrive = [
+        pltpu.make_async_copy(own_hbm, own_ref, sems.at[0]),
+        pltpu.make_async_copy(other_hbm, other_ref, sems.at[1]),
+    ]
+    for part in arrive:
+        part.start()
     work[...] = jnp.zeros((rank, rank), jnp.float32)
 
     def place(parts):
@@ -166,6 +172,8 @@
                 tiles = part_ref[i % 2 * half : (i % 2 + 1) * half, :, i // 2]
                 work[square(k), square(l)] = tiles.reshape(BLOCK, BLOCK)
 
+    for part in arrive:
+        part.wait()
     pl.when(core_ref[0] == 0)(lambda: place((own_ref, other_ref)))
     pl.when(core_ref[0] != 0)(lambda: place((other_ref, own_ref)))
     rows = lax.broadcasted_iota(jnp.int32, (rank, rank), 0)
@@ -190,20 +198,36 @@
         return carry
 
     lax.fori_loop(0, count, step, 0)
-
-
-def right_kernel(inverse_ref, raw_ref, left_ref, right_ref, ortho_ref, squares_ref):
-    rank = inverse_ref.shape[0]
+    leave = pltpu.make_async_copy(out_ref, out_hbm, sems.at[2])
+    leave.start()
+    leave.wait()
+
+
+def right_kernel(
+    inverse_hbm, raw_ref, left_ref, right_hbm, ortho_hbm, squares_ref, inverse_ref, right_ref, ortho_ref, arrive, leave
+):
+    count = raw_ref.shape[0] // BLOCK
+    blocks = [pltpu.make_async_copy(inverse_hbm.at[square(i)], inverse_ref.at[square(i)], arrive.at[i]) for i in range(count)]
+    for block in blocks:
+        block.start()
     raw, left = split(raw_ref[...]), split(left_ref[...])
     eye = lax.broadcasted_iota(jnp.int32, (BLOCK, BLOCK), 0) == lax.broadcasted_iota(jnp.int32, (BLOCK, BLOCK), 1)
-    for i in range(rank // BLOCK):
-        at, upto = pl.ds(i * BLOCK, BLOCK), (i + 1) * BLOCK
+    out = []
+    for i in range(count):
+        at, upto = square(i), (i + 1) * BLOCK
+        blocks[i].wait()
         inverse = split(inverse_ref[at, :upto])
         right = dot3(inverse, [part[:upto] for part in raw], (1, 0))
         right_ref[at, :] = right
         ortho_ref[at, :] = dot3(inverse, [part[:upto] for part in left], (1, 0))
+        out.append(pltpu.make_async_copy(right_ref.at[at], right_hbm.at[at], leave.at[0, i]))
+        out.append(pltpu.make_async_copy(ortho_ref.at[at], ortho_hbm.at[at], leave.at[1, i]))
+        out[-2].start()
+        out[-1].start()
         sums = jnp.sum(right * right, axis=1, keepdims=True)
         squares_ref[pl.ds(i, 1), :] = jnp.sum(jnp.where(eye, sums, 0.0), axis=0, keepdims=True)
+    for block in out:
+        block.wait()
 
 
 def momentum_kernel(blended_ref, ortho_ref, right_ref, out_ref):
@@ -228,14 +252,17 @@
 
 VMEM = pl.BlockSpec(memory_space=pltpu.VMEM)
 SMEM = pl.BlockSpec(memory_space=pltpu.SMEM)
-
-
-def call(kernel, name, shapes, flops, *operands, scratch=(), limit=10):
+HBM = pl.BlockSpec(memory_space=pltpu.HBM)
+
+
+def call(kernel, name, shapes, flops, *operands, scratch=(), limit=10, takes=(), gives=()):
     return pl.pallas_call(
         kernel,
         out_shape=[jax.ShapeDtypeStruct(shape, jnp.float32) for shape in shapes],
-        in_specs=[SMEM if operand.dtype == jnp.int32 else VMEM for operand in operands],
-        out_specs=[VMEM] * len(shapes),
+        in_specs=[
+            SMEM if operand.dtype == jnp.int32 else HBM if i in takes else VMEM for i, operand in enumerate(operands)
+        ],
+        out_specs=[HBM if i in gives else VMEM for i in range(len(shapes))],
         scratch_shapes=list(scratch),
         compiler_params=pltpu.CompilerParams(vmem_limit_bytes=limit * 2**20),
         cost_estimate=pl.CostEstimate(flops=flops, bytes_accessed=4 * 2**20, transcendentals=0),
@@ -278,11 +305,33 @@
             core,
             gram_own,
             gram_other,
-            scratch=[pltpu.VMEM((rank, rank), jnp.float32)],
+            scratch=[
+                pltpu.VMEM(gram_own.shape, jnp.float32),
+                pltpu.VMEM(gram_own.shape, jnp.float32),
+                pltpu.VMEM((rank, rank), jnp.float32),
+                pltpu.VMEM((rank, rank), jnp.float32),
+                pltpu.SemaphoreType.DMA((3,)),
+            ],
+            takes=(1, 2),
+            gives=(0,),
         )
     with jax.named_scope("right"):
         shapes = [(rank, cols), (rank, rows), (rank // BLOCK, BLOCK)]
-        right, ortho, squares = call(right_kernel, "right", shapes, 2 * 10**9, inverse, right_raw, left)
+        scratch = [pltpu.VMEM((rank, width), jnp.float32) for width in (rank, cols, rows)]
+        scratch += [pltpu.SemaphoreType.DMA((rank // BLOCK,)), pltpu.SemaphoreType.DMA((2, rank // BLOCK))]
+        right, ortho, squares = call(
+            right_kernel,
+            "right",
+            shapes,
+            2 * 10**9,
+            inverse,
+            right_raw,
+            left,
+            scratch=scratch,
+            limit=14,
+            takes=(0,),
+            gives=(0, 1),
+        )
     with jax.named_scope("squares"):
         squares = jnp.broadcast_to(squares[None], (lax.axis_size("col"),) + squares.shape)
         squares = lax.all_to_all(squares, "col", 0, 0, tiled=False)

time: 221 us -> 225 us (1.018)
  Pallas kernels: 32.8 us -> 36.6 us
    pallas_call x6, Pallas kernels: 32.8 us -> 36.6 us  [call(): pl.pallas_call(kernel, out_shape=[jax.ShapeDtypeStruct(shape, jnp.float32...]
where the time goes in v3:
time: 225 us; the launch traced here: 224 us
  blocking collectives  104 us (46%)
  Pallas kernels  36.6 us (16%)
  starting transfers between devices  33.7 us (15%)
  waiting for transfers between devices  32.8 us (15%)
  local copies, waits for them, and re-layouts  12.5 us (6%)
  other arithmetic  3.18 us (1%)
    all_to_all x6, blocking collectives, exchange(): lax.all_to_all(blocks, name, 0, 0, axis_index_groups=groups, tiled=False)  104 us
    pallas_call x6, Pallas kernels, call(): pl.pallas_call(kernel, out_shape=[jax.ShapeDtypeStruct(shape, jnp.float32...  36.6 us
    all_to_all x3, waiting for transfers between devices, exchange(): lax.all_to_all(blocks, name, 0, 0, axis_index_groups=groups, tiled=False)  25.9 us
    ppermute x3, starting transfers between devices, swap(): return lax.ppermute(part, 'col', [(i, i ^ 1) for i in range(Y * CORES)])  16.8 us
    all_to_all x3, starting transfers between devices, exchange(): lax.all_to_all(blocks, name, 0, 0, axis_index_groups=groups, tiled=False)  13.3 us
    unnamed x22, local copies, waits for them, and re-layouts  8.56 us
  transfers between devices with their start and end apart: 7, of which 6 were waited for; matrix products, arithmetic and copies ran while one was open for 1% of the time, Pallas kernels for 12%

profile of v3, /device:TPU:1, one launch (start us, length us, event | category | flops | bytes accessed | tf_op | source)
XLA Modules:
  0.0 224.1 jit_solution(8598136334675841010)
XLA Ops:
  1.5 19.0 %all_to_all.50 = f32[4,16,896]{2,1,0:T(8,128)S(1)} all-to-all(f32[4,16,896]{2,1,0:T(8,128)S(1)} %broadcast_in_dim.12), channel_id=1, replica_groups={{0,32,64,96},{16,48,80,112},{128,160,192,224},{144,176,208,240},{256,28..., dimensions={0} | all-to-all | bytes 458752 | tf_op jit(solution)/shard_map/basis_gather/all_to_all | solution.py:45
  20.4 1.4 broadcast_in_dim.13
  21.9 6.2 %all-to-all-start.1 = ((f32[8,4,16,896]{3,2,1,0:T(8,128)}), f32[8,4,16,896]{3,2,1,0:T(8,128)S(1)}, u32[]{:S(2)}, u32[]{:S(2)}) async-start(f32[8,4,16,896]{3,2,1,0:T(8,128)} %broadcast_in_dim.13), calls=%async_computation.1 | async-start | bytes 3670016 | tf_op jit(solution)/shard_map/basis_gather/all_to_all | solution.py:45
  28.1 1.3 convert_add_fusion.blended_ref
  29.4 20.5 %all-to-all-done.1 = f32[8,4,16,896]{3,2,1,0:T(8,128)S(1)} async-done(((f32[8,4,16,896]{3,2,1,0:T(8,128)}), f32[8,4,16,896]{3,2,1,0:T(8,128)S(1)}, u32[]{:S(2)}, u32[]{:S(2)}) %all-to-all-start.1) | async-done | bytes 1835040 | tf_op jit(solution)/shard_map/basis_gather/all_to_all | solution.py:45
  49.9 1.0 fusion
  51.0 5.2 %collective-permute-start = (f32[256,256]{0,1:T(8,128)S(1)}, f32[256,256]{0,1:T(8,128)S(1)}, u32[]{:S(2)}, u32[]{:S(2)}) collective-permute-start(f32[256,256]{0,1:T(8,128)S(1)} %dynamic-slice_bitcast_fusion), channel_id=1, source_target_pairs={{0,1},{1,0},{2,3},{3,2},{4,5},{5,4},{6,7},{7,6},{8,9},{9,8},{10,11... | collective-permute-start | bytes 786440 | tf_op jit(solution)/shard_map/left/ppermute | solution.py:61
  56.2 1.1 collective-permute-done
  57.5 17.7 %all_to_all.51 = f32[8,32,256]{2,1,0:T(8,128)S(1)} all-to-all(f32[8,32,256]{2,1,0:T(8,128)S(1)} %bitcast.25), channel_id=1, replica_groups={{0,2,4,6,8,10,12,14},{1,3,5,7,9,11,13,15},{16,18,20,22,24,26,28,30},{17..., dimensions={0} | all-to-all | bytes 524288 | tf_op jit(solution)/shard_map/left/all_to_all | solution.py:45
  75.3 12.1 %all_to_all.52 = f32[8,32,256]{2,1,0:T(8,128)S(1)} all-to-all(f32[8,32,256]{2,1,0:T(8,128)S(1)} %broadcast_in_dim.14), channel_id=1, replica_groups={{0,2,4,6,8,10,12,14},{1,3,5,7,9,11,13,15},{16,18,20,22,24,26,28,30},{17..., dimensions={0} | all-to-all | bytes 524288 | tf_op jit(solution)/shard_map/left/all_to_all | solution.py:45
  87.4 5.0 %collective-permute-start.1 = (f32[256,256]{1,0:T(8,128)S(1)}, f32[256,256]{1,0:T(8,128)S(1)}, u32[]{:S(2)}, u32[]{:S(2)}) collective-permute-start(f32[256,256]{1,0:T(8,128)S(1)} %bitcast.26), channel_id=1, source_target_pairs={{0,1},{1,0},{2,3},{3,2},{4,5},{5,4},{6,7},{7,6},{8,9},{9,8},{10,11... | collective-permute-start | bytes 786440 | tf_op jit(solution)/shard_map/left/ppermute | solution.py:61
  92.4 1.1 collective-permute-done.1
  93.7 1.7 products.1
  95.4 31.2 %all_to_all.53 = f32[8,4,17,8,128]{4,3,2,1,0:T(8,128)} all-to-all(f32[8,4,17,8,128]{4,3,2,1,0:T(8,128)S(1)} %products.1), channel_id=1, replica_groups={{0,16,128,144,256,272,384,400},{32,48,160,176,288,304,416,432},{64,80,1..., dimensions={0} | all-to-all | bytes 4456448 | tf_op jit(solution)/shard_map/sums/all_to_all | solution.py:45
  126.6 1.8 reduce_sum.28
  128.4 10.9 %all_to_all.54 = f32[4,17,8,128]{3,2,1,0:T(8,128)S(1)} all-to-all(f32[4,17,8,128]{3,2,1,0:T(8,128)S(1)} %reduce_sum.28), channel_id=1, replica_groups={{0,32,64,96},{16,48,80,112},{128,160,192,224},{144,176,208,240},{256,28..., dimensions={0} | all-to-all | bytes 557056 | tf_op jit(solution)/shard_map/sums/all_to_all | solution.py:45
  139.3 12.6 %all_to_all.55.sums_ref = f32[4,17,8,128]{3,2,1,0:T(8,128)S(1)} all-to-all(f32[4,17,8,128]{3,2,1,0:T(8,128)S(1)} %broadcast_in_dim.15), channel_id=1, replica_groups={{0,32,64,96},{16,48,80,112},{128,160,192,224},{144,176,208,240},{256,28..., dimensions={0} | all-to-all | bytes 557056 | tf_op jit(solution)/shard_map/sums/all_to_all | solution.py:45
  152.7 3.5 %all-to-all-start.7 = ((f32[8,4,3,8,128]{4,3,2,1,0:T(8,128)}), f32[8,4,3,8,128]{4,3,2,1,0:T(8,128)S(1)}, u32[]{:S(2)}, u32[]{:S(2)}) async-start(f32[8,4,3,8,128]{4,3,2,1,0:T(8,128)} %broadcast_in_dim.16), calls=%async_computation.7 | async-start | bytes 786432 | tf_op jit(solution)/shard_map/sums/all_to_all | solution.py:45
  156.2 1.4 copies.1
  157.6 5.4 %all-to-all-done.7.own_hbm = f32[8,4,3,8,128]{4,3,2,1,0:T(8,128)S(1)} async-done(((f32[8,4,3,8,128]{4,3,2,1,0:T(8,128)}), f32[8,4,3,8,128]{4,3,2,1,0:T(8,128)S(1)}, u32[]{:S(2)}, u32[]{:S(2)}) %all-to-all-start.7) | async-done | bytes 393248 | tf_op jit(solution)/shard_map/sums/all_to_all | solution.py:45
  163.7 3.6 %all-to-all-start.8 = ((f32[8,64,896]{2,1,0:T(8,128)}), f32[8,64,896]{2,1,0:T(8,128)S(1)}, u32[]{:S(2)}, u32[]{:S(2)}) async-start(f32[8,64,896]{2,1,0:T(8,128)} %copies.1), calls=%async_computation.8 | async-start | bytes 3670016 | tf_op jit(solution)/shard_map/sums/all_to_all | solution.py:45
  167.3 6.6 %collective-permute-start.2 = (f32[8,4,3,8,128]{4,3,2,1,0:T(8,128)}, f32[8,4,3,8,128]{4,3,2,1,0:T(8,128)}, u32[]{:S(2)}, u32[]{:S(2)}) collective-permute-start(f32[8,4,3,8,128]{4,3,2,1,0:T(8,128)} %copy-done.6), channel_id=1, source_target_pairs={{0,1},{1,0},{2,3},{3,2},{4,5},{5,4},{6,7},{7,6},{8,9},{9,8},{10,11... | collective-permute-start | bytes 1179656 | tf_op jit(solution)/shard_map/sums/ppermute | solution.py:61
  173.9 1.7 collective-permute-done.2.other_hbm
  176.5 24.0 %inverse_factor.1.inverse_hbm = f32[512,512]{1,0:T(8,128)S(1)} custom-call(s32[1]{0:T(128)} %bitcast.1.core_ref, f32[8,4,3,8,128]{4,3,2,1,0:T(8,128)S(1)} %copy-done.7, f32[8,4,3,8,128]{4,3,2,1,0:T(8,128)} %collective-permute-done.2.other_hbm), custom_call_target="tpu_custom_call" | custom-call | flops 2000000000 | bytes 4194304 | tf_op jit(solution)/shard_map/factor/inverse_factor/pallas_call | solution.py:259
  201.5 1.2 copy-done.9
  202.7 5.4 %right.1 = (f32[512,896]{1,0:T(8,128)S(1)}, f32[512,256]{1,0:T(8,128)S(1)}, f32[4,128]{1,0:T(4,128)S(1)}) custom-call(f32[512,512]{1,0:T(8,128)S(1)} %copy-done.9, f32[512,896]{1,0:T(8,128)S(1)} %bitcast.20, f32[512,256]{1,0:T(8,128)S(1)} %bitcast.22), custom_call_target="tpu_custom_call" | custom-call | flops 2000000000 | bytes 4194304 | tf_op jit(solution)/shard_map/right/right/pallas_call | solution.py:259
  208.1 1.3 copy-done
  210.8 3.7 %all-to-all-start.9 = ((f32[16,4,128]{2,1,0:T(4,128)}), f32[16,4,128]{2,1,0:T(4,128)S(1)}, u32[]{:S(2)}, u32[]{:S(2)}) async-start(f32[16,4,128]{2,1,0:T(4,128)} %broadcast_in_dim.17), calls=%async_computation.9 | async-start | bytes 65536 | tf_op jit(solution)/shard_map/squares/all_to_all | solution.py:337
  214.5 1.5 copy-done.1
  217.0 2.0 momentum.1
  219.0 3.0 %all-to-all-done.9.squares_ref = f32[16,4,128]{2,1,0:T(4,128)S(1)} async-done(((f32[16,4,128]{2,1,0:T(4,128)}), f32[16,4,128]{2,1,0:T(4,128)S(1)}, u32[]{:S(2)}, u32[]{:S(2)}) %all-to-all-start.9) | async-done | bytes 32800 | tf_op jit(solution)/shard_map/squares/all_to_all | solution.py:337
  221.9 2.2 update.1
  (34 shorter events, 7.2 us)
Async XLA Ops:
  21.9 6.2 %copy-start.10 = (bf16[256,896]{1,0:T(8,128)(2,1)S(1)}, bf16[256,896]{1,0:T(8,128)(2,1)}, u32[]{:S(2)}) copy-start(bf16[256,896]{1,0:T(8,128)(2,1)} %param.4) | copy-start | bytes 1376260
  21.9 28.0 %all-to-all-start.1 = ((f32[8,4,16,896]{3,2,1,0:T(8,128)}), f32[8,4,16,896]{3,2,1,0:T(8,128)S(1)}, u32[]{:S(2)}, u32[]{:S(2)}) async-start(f32[8,4,16,896]{3,2,1,0:T(8,128)} %broadcast_in_dim.13), calls=%async_computation.1 | async-start | bytes 3670016 | tf_op jit(solution)/shard_map/basis_gather/all_to_all | solution.py:45
  51.0 6.3 %collective-permute-start = (f32[256,256]{0,1:T(8,128)S(1)}, f32[256,256]{0,1:T(8,128)S(1)}, u32[]{:S(2)}, u32[]{:S(2)}) collective-permute-start(f32[256,256]{0,1:T(8,128)S(1)} %dynamic-slice_bitcast_fusion), channel_id=1, source_target_pairs={{0,1},{1,0},{2,3},{3,2},{4,5},{5,4},{6,7},{7,6},{8,9},{9,8},{10,11... | collective-permute-start | bytes 786440 | tf_op jit(solution)/shard_map/left/ppermute | solution.py:61
  87.4 6.2 %collective-permute-start.1 = (f32[256,256]{1,0:T(8,128)S(1)}, f32[256,256]{1,0:T(8,128)S(1)}, u32[]{:S(2)}, u32[]{:S(2)}) collective-permute-start(f32[256,256]{1,0:T(8,128)S(1)} %bitcast.26), channel_id=1, source_target_pairs={{0,1},{1,0},{2,3},{3,2},{4,5},{5,4},{6,7},{7,6},{8,9},{9,8},{10,11... | collective-permute-start | bytes 786440 | tf_op jit(solution)/shard_map/left/ppermute | solution.py:61
  152.7 10.2 %all-to-all-start.7 = ((f32[8,4,3,8,128]{4,3,2,1,0:T(8,128)}), f32[8,4,3,8,128]{4,3,2,1,0:T(8,128)S(1)}, u32[]{:S(2)}, u32[]{:S(2)}) async-start(f32[8,4,3,8,128]{4,3,2,1,0:T(8,128)} %broadcast_in_dim.16), calls=%async_computation.7 | async-start | bytes 786432 | tf_op jit(solution)/shard_map/sums/all_to_all | solution.py:45
  162.9 0.7 copy-start.6
  163.7 37.8 %all-to-all-start.8 = ((f32[8,64,896]{2,1,0:T(8,128)}), f32[8,64,896]{2,1,0:T(8,128)S(1)}, u32[]{:S(2)}, u32[]{:S(2)}) async-start(f32[8,64,896]{2,1,0:T(8,128)} %copies.1), calls=%async_computation.8 | async-start | bytes 3670016 | tf_op jit(solution)/shard_map/sums/all_to_all | solution.py:45
  167.3 8.3 %collective-permute-start.2 = (f32[8,4,3,8,128]{4,3,2,1,0:T(8,128)}, f32[8,4,3,8,128]{4,3,2,1,0:T(8,128)}, u32[]{:S(2)}, u32[]{:S(2)}) collective-permute-start(f32[8,4,3,8,128]{4,3,2,1,0:T(8,128)} %copy-done.6), channel_id=1, source_target_pairs={{0,1},{1,0},{2,3},{3,2},{4,5},{5,4},{6,7},{7,6},{8,9},{9,8},{10,11... | collective-permute-start | bytes 1179656 | tf_op jit(solution)/shard_map/sums/ppermute | solution.py:61
  175.5 1.0 copy-start.7
  200.5 1.0 copy-start.8
  201.5 1.2 copy-start.9
  208.1 1.3 copy-start
  209.4 0.8 copy-start.3
  210.8 11.1 %all-to-all-start.9 = ((f32[16,4,128]{2,1,0:T(4,128)}), f32[16,4,128]{2,1,0:T(4,128)S(1)}, u32[]{:S(2)}, u32[]{:S(2)}) async-start(f32[16,4,128]{2,1,0:T(4,128)} %broadcast_in_dim.17), calls=%async_computation.9 | async-start | bytes 65536 | tf_op jit(solution)/shard_map/squares/all_to_all | solution.py:337
  214.5 1.5 copy-start.1
  216.0 1.0 copy-start.4
  217.0 4.9 %copy-start.2 = (f32[512,896]{1,0:T(8,128)S(1)}, f32[512,896]{1,0:T(8,128)}, u32[]{:S(2)}) copy-start(f32[512,896]{1,0:T(8,128)} %copy-done) | copy-start | bytes 5505028
  217.0 4.9 %copy-start.5 = (f32[512,256]{1,0:T(8,128)S(1)}, f32[512,256]{1,0:T(8,128)}, u32[]{:S(2)}) copy-start(f32[512,256]{1,0:T(8,128)} %copy-done.3) | copy-start | bytes 1572868

commit v4 on v3

--- a/solution.py
+++ b/solution.py
@@ -258,7 +258,10 @@
 def call(kernel, name, shapes, flops, *operands, scratch=(), limit=10, takes=(), gives=()):
     return pl.pallas_call(
         kernel,
-        out_shape=[jax.ShapeDtypeStruct(shape, jnp.float32) for shape in shapes],
+        out_shape=[
+            pltpu.HBM(shape, jnp.float32) if i in gives else jax.ShapeDtypeStruct(shape, jnp.float32)
+            for i, shape in enumerate(shapes)
+        ],
         in_specs=[
             SMEM if operand.dtype == jnp.int32 else HBM if i in takes else VMEM for i, operand in enumerate(operands)
         ],
@@ -267,7 +270,7 @@
         compiler_params=pltpu.CompilerParams(vmem_limit_bytes=limit * 2**20),
         cost_estimate=pl.CostEstimate(flops=flops, bytes_accessed=4 * 2**20, transcendentals=0),
         name=name,
-    )(*operands)
+    )(*[pltpu.with_memory_space_constraint(x, pltpu.HBM) if i in takes else x for i, x in enumerate(operands)])
 
 
 def body(momentum, gradient, right_basis):

time: 225 us -> 220 us (0.978)
  local copies, waits for them, and re-layouts: 12.5 us -> 7.18 us
    unnamed x22 -> x12, local copies, waits for them, and re-layouts: 8.56 us -> 3.29 us
  transfers between devices with their start and end apart: 7 -> 7, of which waited for: 6 -> 6; matrix products, arithmetic and copies ran while one was open for 1% -> 1% of each run, Pallas kernels for 12% -> 13%
where the time goes in v4:
time: 220 us; the launch traced here: 219 us
  blocking collectives  104 us (47%)
  Pallas kernels  36.5 us (17%)
  starting transfers between devices  33.8 us (15%)
  waiting for transfers between devices  32.8 us (15%)
  local copies, waits for them, and re-layouts  7.18 us (3%)
  other arithmetic  3.18 us (1%)
    all_to_all x6, blocking collectives, exchange(): lax.all_to_all(blocks, name, 0, 0, axis_index_groups=groups, tiled=False)  104 us
    pallas_call x6, Pallas kernels, call(): pl.pallas_call(kernel, out_shape=[pltpu.HBM(shape, jnp.float32) if i in g...  36.5 us
    all_to_all x3, waiting for transfers between devices, exchange(): lax.all_to_all(blocks, name, 0, 0, axis_index_groups=groups, tiled=False)  25.9 us
    ppermute x3, starting transfers between devices, swap(): return lax.ppermute(part, 'col', [(i, i ^ 1) for i in range(Y * CORES)])  16.9 us
    all_to_all x3, starting transfers between devices, exchange(): lax.all_to_all(blocks, name, 0, 0, axis_index_groups=groups, tiled=False)  13.3 us
  transfers between devices with their start and end apart: 7, of which 6 were waited for; matrix products, arithmetic and copies ran while one was open for 1% of the time, Pallas kernels for 13%

profile of v4, /device:TPU:1, one launch (start us, length us, event | category | flops | bytes accessed | tf_op | source)
XLA Modules:
  0.0 218.9 jit_solution(9683868761418964371)
XLA Ops:
  0.6 0.8 broadcast_in_dim.12
  1.5 19.0 %all_to_all.50 = f32[4,16,896]{2,1,0:T(8,128)S(1)} all-to-all(f32[4,16,896]{2,1,0:T(8,128)S(1)} %broadcast_in_dim.12), channel_id=1, replica_groups={{0,32,64,96},{16,48,80,112},{128,160,192,224},{144,176,208,240},{256,28..., dimensions={0} | all-to-all | bytes 458752 | tf_op jit(solution)/shard_map/basis_gather/all_to_all | solution.py:45
  20.4 1.4 broadcast_in_dim.13
  21.9 6.2 %all-to-all-start.1 = ((f32[8,4,16,896]{3,2,1,0:T(8,128)}), f32[8,4,16,896]{3,2,1,0:T(8,128)S(1)}, u32[]{:S(2)}, u32[]{:S(2)}) async-start(f32[8,4,16,896]{3,2,1,0:T(8,128)} %broadcast_in_dim.13), calls=%async_computation.1 | async-start | bytes 3670016 | tf_op jit(solution)/shard_map/basis_gather/all_to_all | solution.py:45
  28.1 1.3 convert_add_fusion.blended_ref
  29.3 20.5 %all-to-all-done.1 = f32[8,4,16,896]{3,2,1,0:T(8,128)S(1)} async-done(((f32[8,4,16,896]{3,2,1,0:T(8,128)}), f32[8,4,16,896]{3,2,1,0:T(8,128)S(1)}, u32[]{:S(2)}, u32[]{:S(2)}) %all-to-all-start.1) | async-done | bytes 1835040 | tf_op jit(solution)/shard_map/basis_gather/all_to_all | solution.py:45
  49.9 1.0 fusion
  51.0 5.2 %collective-permute-start = (f32[256,256]{0,1:T(8,128)S(1)}, f32[256,256]{0,1:T(8,128)S(1)}, u32[]{:S(2)}, u32[]{:S(2)}) collective-permute-start(f32[256,256]{0,1:T(8,128)S(1)} %dynamic-slice_bitcast_fusion), channel_id=1, source_target_pairs={{0,1},{1,0},{2,3},{3,2},{4,5},{5,4},{6,7},{7,6},{8,9},{9,8},{10,11... | collective-permute-start | bytes 786440 | tf_op jit(solution)/shard_map/left/ppermute | solution.py:61
  56.2 1.1 collective-permute-done
  57.5 17.7 %all_to_all.51 = f32[8,32,256]{2,1,0:T(8,128)S(1)} all-to-all(f32[8,32,256]{2,1,0:T(8,128)S(1)} %bitcast.25), channel_id=1, replica_groups={{0,2,4,6,8,10,12,14},{1,3,5,7,9,11,13,15},{16,18,20,22,24,26,28,30},{17..., dimensions={0} | all-to-all | bytes 524288 | tf_op jit(solution)/shard_map/left/all_to_all | solution.py:45
  75.3 12.1 %all_to_all.52 = f32[8,32,256]{2,1,0:T(8,128)S(1)} all-to-all(f32[8,32,256]{2,1,0:T(8,128)S(1)} %broadcast_in_dim.14), channel_id=1, replica_groups={{0,2,4,6,8,10,12,14},{1,3,5,7,9,11,13,15},{16,18,20,22,24,26,28,30},{17..., dimensions={0} | all-to-all | bytes 524288 | tf_op jit(solution)/shard_map/left/all_to_all | solution.py:45
  87.4 5.0 %collective-permute-start.1 = (f32[256,256]{1,0:T(8,128)S(1)}, f32[256,256]{1,0:T(8,128)S(1)}, u32[]{:S(2)}, u32[]{:S(2)}) collective-permute-start(f32[256,256]{1,0:T(8,128)S(1)} %bitcast.26), channel_id=1, source_target_pairs={{0,1},{1,0},{2,3},{3,2},{4,5},{5,4},{6,7},{7,6},{8,9},{9,8},{10,11... | collective-permute-start | bytes 786440 | tf_op jit(solution)/shard_map/left/ppermute | solution.py:61
  92.4 1.1 collective-permute-done.1
  93.7 1.7 products.1
  95.3 31.2 %all_to_all.53 = f32[8,4,17,8,128]{4,3,2,1,0:T(8,128)} all-to-all(f32[8,4,17,8,128]{4,3,2,1,0:T(8,128)S(1)} %products.1), channel_id=1, replica_groups={{0,16,128,144,256,272,384,400},{32,48,160,176,288,304,416,432},{64,80,1..., dimensions={0} | all-to-all | bytes 4456448 | tf_op jit(solution)/shard_map/sums/all_to_all | solution.py:45
  126.6 1.8 reduce_sum.28
  128.4 10.9 %all_to_all.54 = f32[4,17,8,128]{3,2,1,0:T(8,128)S(1)} all-to-all(f32[4,17,8,128]{3,2,1,0:T(8,128)S(1)} %reduce_sum.28), channel_id=1, replica_groups={{0,32,64,96},{16,48,80,112},{128,160,192,224},{144,176,208,240},{256,28..., dimensions={0} | all-to-all | bytes 557056 | tf_op jit(solution)/shard_map/sums/all_to_all | solution.py:45
  139.3 12.6 %all_to_all.55.sums_ref = f32[4,17,8,128]{3,2,1,0:T(8,128)S(1)} all-to-all(f32[4,17,8,128]{3,2,1,0:T(8,128)S(1)} %broadcast_in_dim.15), channel_id=1, replica_groups={{0,32,64,96},{16,48,80,112},{128,160,192,224},{144,176,208,240},{256,28..., dimensions={0} | all-to-all | bytes 557056 | tf_op jit(solution)/shard_map/sums/all_to_all | solution.py:45
  152.7 3.5 %all-to-all-start.7 = ((f32[8,4,3,8,128]{4,3,2,1,0:T(8,128)}), f32[8,4,3,8,128]{4,3,2,1,0:T(8,128)S(1)}, u32[]{:S(2)}, u32[]{:S(2)}) async-start(f32[8,4,3,8,128]{4,3,2,1,0:T(8,128)} %broadcast_in_dim.16), calls=%async_computation.7 | async-start | bytes 786432 | tf_op jit(solution)/shard_map/sums/all_to_all | solution.py:45
  156.2 1.4 copies.1
  157.5 5.4 %all-to-all-done.7.own_hbm = f32[8,4,3,8,128]{4,3,2,1,0:T(8,128)S(1)} async-done(((f32[8,4,3,8,128]{4,3,2,1,0:T(8,128)}), f32[8,4,3,8,128]{4,3,2,1,0:T(8,128)S(1)}, u32[]{:S(2)}, u32[]{:S(2)}) %all-to-all-start.7) | async-done | bytes 393248 | tf_op jit(solution)/shard_map/sums/all_to_all | solution.py:45
  163.7 3.6 %all-to-all-start.8 = ((f32[8,64,896]{2,1,0:T(8,128)}), f32[8,64,896]{2,1,0:T(8,128)S(1)}, u32[]{:S(2)}, u32[]{:S(2)}) async-start(f32[8,64,896]{2,1,0:T(8,128)} %copies.1), calls=%async_computation.8 | async-start | bytes 3670016 | tf_op jit(solution)/shard_map/sums/all_to_all | solution.py:45
  167.3 6.7 %collective-permute-start.2 = (f32[8,4,3,8,128]{4,3,2,1,0:T(8,128)}, f32[8,4,3,8,128]{4,3,2,1,0:T(8,128)}, u32[]{:S(2)}, u32[]{:S(2)}) collective-permute-start(f32[8,4,3,8,128]{4,3,2,1,0:T(8,128)} %copy-done.5), channel_id=1, source_target_pairs={{0,1},{1,0},{2,3},{3,2},{4,5},{5,4},{6,7},{7,6},{8,9},{9,8},{10,11... | collective-permute-start | bytes 1179656 | tf_op jit(solution)/shard_map/sums/ppermute | solution.py:61
  173.9 1.7 collective-permute-done.2.other_hbm
  175.6 24.8 %inverse_factor.1.inverse_hbm = f32[512,512]{1,0:T(8,128)} custom-call(s32[1]{0:T(128)} %bitcast.1.core_ref, f32[8,4,3,8,128]{4,3,2,1,0:T(8,128)} %copy-done.5, f32[8,4,3,8,128]{4,3,2,1,0:T(8,128)} %collective-permute-done.2.other_hbm), custom_call_target="tpu_custom_call" | custom-call | flops 2000000000 | bytes 4194304 | tf_op jit(solution)/shard_map/factor/inverse_factor/pallas_call | solution.py:259
  200.4 4.5 %right.1 = (f32[512,896]{1,0:T(8,128)}, f32[512,256]{1,0:T(8,128)}, f32[4,128]{1,0:T(4,128)S(1)}) custom-call(f32[512,512]{1,0:T(8,128)} %inverse_factor.1.inverse_hbm, f32[512,896]{1,0:T(8,128)S(1)} %bitcast.20, f32[512,256]{1,0:T(8,128)S(1)} %bitcast.22), custom_call_target="tpu_custom_call" | custom-call | flops 2000000000 | bytes 4194304 | tf_op jit(solution)/shard_map/right/right/pallas_call | solution.py:259
  205.5 3.7 %all-to-all-start.9 = ((f32[16,4,128]{2,1,0:T(4,128)}), f32[16,4,128]{2,1,0:T(4,128)S(1)}, u32[]{:S(2)}, u32[]{:S(2)}) async-start(f32[16,4,128]{2,1,0:T(4,128)} %broadcast_in_dim.17), calls=%async_computation.9 | async-start | bytes 65536 | tf_op jit(solution)/shard_map/squares/all_to_all | solution.py:340
  209.2 1.5 copy-done
  210.7 1.0 copy-done.2
  211.7 2.0 momentum.1
  213.7 3.0 %all-to-all-done.9.squares_ref = f32[16,4,128]{2,1,0:T(4,128)S(1)} async-done(((f32[16,4,128]{2,1,0:T(4,128)}), f32[16,4,128]{2,1,0:T(4,128)S(1)}, u32[]{:S(2)}, u32[]{:S(2)}) %all-to-all-start.9) | async-done | bytes 32800 | tf_op jit(solution)/shard_map/squares/all_to_all | solution.py:340
  216.7 2.2 %update.1 = (f32[256,896]{1,0:T(8,128)}, f32[16,896]{1,0:T(8,128)}) custom-call(s32[1]{0:T(128)} %bitcast.start_ref, f32[16,4,128]{2,1,0:T(4,128)S(1)} %all-to-all-done.9.squares_ref, f32[512,256]{1,0:T(8,128)S(1)} %copy-done.3, f32[512,896]{1,0:T(8,128)S(1)} %copy-done.1), custom_call_target="tpu_custom_call" | custom-call | flops 1000000000 | bytes 4194304 | tf_op jit(solution)/shard_map/outputs/update/pallas_call | solution.py:259
  (24 shorter events, 2.6 us)
Async XLA Ops:
  21.9 6.2 %copy-start.4 = (bf16[256,896]{1,0:T(8,128)(2,1)S(1)}, bf16[256,896]{1,0:T(8,128)(2,1)}, u32[]{:S(2)}) copy-start(bf16[256,896]{1,0:T(8,128)(2,1)} %param.4) | copy-start | bytes 1376260
  21.9 28.0 %all-to-all-start.1 = ((f32[8,4,16,896]{3,2,1,0:T(8,128)}), f32[8,4,16,896]{3,2,1,0:T(8,128)S(1)}, u32[]{:S(2)}, u32[]{:S(2)}) async-start(f32[8,4,16,896]{3,2,1,0:T(8,128)} %broadcast_in_dim.13), calls=%async_computation.1 | async-start | bytes 3670016 | tf_op jit(solution)/shard_map/basis_gather/all_to_all | solution.py:45
  51.0 6.3 %collective-permute-start = (f32[256,256]{0,1:T(8,128)S(1)}, f32[256,256]{0,1:T(8,128)S(1)}, u32[]{:S(2)}, u32[]{:S(2)}) collective-permute-start(f32[256,256]{0,1:T(8,128)S(1)} %dynamic-slice_bitcast_fusion), channel_id=1, source_target_pairs={{0,1},{1,0},{2,3},{3,2},{4,5},{5,4},{6,7},{7,6},{8,9},{9,8},{10,11... | collective-permute-start | bytes 786440 | tf_op jit(solution)/shard_map/left/ppermute | solution.py:61
  87.4 6.2 %collective-permute-start.1 = (f32[256,256]{1,0:T(8,128)S(1)}, f32[256,256]{1,0:T(8,128)S(1)}, u32[]{:S(2)}, u32[]{:S(2)}) collective-permute-start(f32[256,256]{1,0:T(8,128)S(1)} %bitcast.26), channel_id=1, source_target_pairs={{0,1},{1,0},{2,3},{3,2},{4,5},{5,4},{6,7},{7,6},{8,9},{9,8},{10,11... | collective-permute-start | bytes 786440 | tf_op jit(solution)/shard_map/left/ppermute | solution.py:61
  152.7 10.2 %all-to-all-start.7 = ((f32[8,4,3,8,128]{4,3,2,1,0:T(8,128)}), f32[8,4,3,8,128]{4,3,2,1,0:T(8,128)S(1)}, u32[]{:S(2)}, u32[]{:S(2)}) async-start(f32[8,4,3,8,128]{4,3,2,1,0:T(8,128)} %broadcast_in_dim.16), calls=%async_computation.7 | async-start | bytes 786432 | tf_op jit(solution)/shard_map/sums/all_to_all | solution.py:45
  162.9 0.7 copy-start.5
  163.7 36.8 %all-to-all-start.8 = ((f32[8,64,896]{2,1,0:T(8,128)}), f32[8,64,896]{2,1,0:T(8,128)S(1)}, u32[]{:S(2)}, u32[]{:S(2)}) async-start(f32[8,64,896]{2,1,0:T(8,128)} %copies.1), calls=%async_computation.8 | async-start | bytes 3670016 | tf_op jit(solution)/shard_map/sums/all_to_all | solution.py:45
  167.3 8.3 %collective-permute-start.2 = (f32[8,4,3,8,128]{4,3,2,1,0:T(8,128)}, f32[8,4,3,8,128]{4,3,2,1,0:T(8,128)}, u32[]{:S(2)}, u32[]{:S(2)}) collective-permute-start(f32[8,4,3,8,128]{4,3,2,1,0:T(8,128)} %copy-done.5), channel_id=1, source_target_pairs={{0,1},{1,0},{2,3},{3,2},{4,5},{5,4},{6,7},{7,6},{8,9},{9,8},{10,11... | collective-permute-start | bytes 1179656 | tf_op jit(solution)/shard_map/sums/ppermute | solution.py:61
  205.5 11.1 %all-to-all-start.9 = ((f32[16,4,128]{2,1,0:T(4,128)}), f32[16,4,128]{2,1,0:T(4,128)S(1)}, u32[]{:S(2)}, u32[]{:S(2)}) async-start(f32[16,4,128]{2,1,0:T(4,128)} %broadcast_in_dim.17), calls=%async_computation.9 | async-start | bytes 65536 | tf_op jit(solution)/shard_map/squares/all_to_all | solution.py:340
  209.2 1.5 copy-start
  210.7 1.0 copy-start.2
  211.7 4.9 %copy-start.1 = (f32[512,896]{1,0:T(8,128)S(1)}, f32[512,896]{1,0:T(8,128)}, u32[]{:S(2)}) copy-start(f32[512,896]{1,0:T(8,128)} %get-tuple-element.14.right_ref) | copy-start | bytes 5505028
  211.7 4.9 %copy-start.3 = (f32[512,256]{1,0:T(8,128)S(1)}, f32[512,256]{1,0:T(8,128)}, u32[]{:S(2)}) copy-start(f32[512,256]{1,0:T(8,128)} %get-tuple-element.13.ortho_ref) | copy-start | bytes 1572868

commit v5 on v4

--- a/solution.py
+++ b/solution.py
@@ -1,3 +1,4 @@
+import functools
 import math
 
 import jax
@@ -123,7 +124,7 @@
             out_ref[member, :, j * BLOCK : (j + 1) * BLOCK] = piece
 
 
-def invert_block(block):
+def invert_block(block, pending):
     groups = BLOCK // 8
     sub = lax.broadcasted_iota(jnp.int32, (8, BLOCK), 0)
     lane = lax.broadcasted_iota(jnp.int32, (8, BLOCK), 1)
@@ -131,6 +132,8 @@
     side = [jnp.where(lane == sub + 8 * q, 1.0, 0.0).astype(jnp.float32) for q in range(groups)]
     out = []
     for p in range(groups):
+        if pending:
+            pending.pop(0)()
         spread = {
             q: [jnp.broadcast_to(work[q][:, 8 * p + j : 8 * p + j + 1], (8, BLOCK)) for j in range(8)]
             for q in range(p, groups)
@@ -154,16 +157,54 @@
     return jnp.concatenate(out, axis=0)
 
 
-def factor_kernel(core_ref, own_hbm, other_hbm, out_hbm, own_ref, other_ref, out_ref, work, sems):
-    rank = out_ref.shape[0]
-    count = rank // BLOCK
+def eliminate(work):
+    count = work.shape[0] // BLOCK
+    span = lambda first, last: pl.ds(first * BLOCK, (last - first) * BLOCK)
+    pending = []
+    for k in range(count):
+        inverse = invert_block(work[square(k), square(k)], pending)
+        while pending:
+            pending.pop(0)()
+        work[square(k), square(k)] = inverse
+        if k + 1 < count:
+            near = dot(inverse, work[square(k), square(k + 1)], (1, 0), HIGHEST)
+            work[square(k), square(k + 1)] = near
+            work[square(k + 1), square(k + 1)] -= dot(near, near, (0, 0), HIGHEST)
+
+        def row(first, last, k=k, inverse=inverse):
+            at = (square(k), span(first, last))
+            work[at] = dot(inverse, work[at], (1, 0), HIGHEST)
+
+        def below(i, first, last, k=k):
+            change = dot(work[square(k), square(i)], work[square(k), span(first, last)], (0, 0), HIGHEST)
+            at = (square(i), span(first, last))
+            work[at] = -change if first == k else work[at] - change
+
+        if k + 2 < count:
+            pending.append(functools.partial(row, k + 2, count))
+        if k:
+            pending.append(functools.partial(row, 0, k))
+        for i in range(k + 1, count):
+            right = max(i, k + 2)
+            if right < count:
+                pending.append(functools.partial(below, i, right, count))
+            pending.append(functools.partial(below, i, k, k + 1))
+            if k:
+                pending.append(functools.partial(below, i, 0, k))
+    while pending:
+        pending.pop(0)()
+
+
+def factor_kernel(
+    core_ref, own_hbm, other_hbm, left_ref, out_hbm, ortho_hbm, own_ref, other_ref, work, ortho_ref, sems
+):
+    rank = work.shape[0]
     arrive = [
         pltpu.make_async_copy(own_hbm, own_ref, sems.at[0]),
         pltpu.make_async_copy(other_hbm, other_ref, sems.at[1]),
     ]
     for part in arrive:
         part.start()
-    work[...] = jnp.zeros((rank, rank), jnp.float32)
 
     def place(parts):
         for part_ref, blocks in zip(parts, CORE_BLOCKS):
@@ -176,53 +217,34 @@
         part.wait()
     pl.when(core_ref[0] == 0)(lambda: place((own_ref, other_ref)))
     pl.when(core_ref[0] != 0)(lambda: place((other_ref, own_ref)))
-    rows = lax.broadcasted_iota(jnp.int32, (rank, rank), 0)
-    cols = lax.broadcasted_iota(jnp.int32, (rank, rank), 1)
-    out_ref[...] = jnp.where(rows == cols, 1.0, 0.0)
-
-    def step(k, carry):
-        at = pl.ds(pl.multiple_of(k * BLOCK, BLOCK), BLOCK)
-        inverse = invert_block(work[at, at])
-        upper = dot(inverse, work[at, :], (1, 0), HIGHEST)
-        side = dot(inverse, out_ref[at, :], (1, 0), HIGHEST)
-        out_ref[at, :] = side
-        for i in range(1, count):
-
-            @pl.when(i > k)
-            def _():
-                below = pl.ds(i * BLOCK, BLOCK)
-                times = upper[:, i * BLOCK : (i + 1) * BLOCK]
-                work[below, :] -= dot(times, upper, (0, 0), HIGHEST)
-                out_ref[below, :] -= dot(times, side, (0, 0), HIGHEST)
-
-        return carry
-
-    lax.fori_loop(0, count, step, 0)
-    leave = pltpu.make_async_copy(out_ref, out_hbm, sems.at[2])
-    leave.start()
-    leave.wait()
-
-
-def right_kernel(
-    inverse_hbm, raw_ref, left_ref, right_hbm, ortho_hbm, squares_ref, inverse_ref, right_ref, ortho_ref, arrive, leave
-):
+    eliminate(work)
+    leave = [pltpu.make_async_copy(work, out_hbm, sems.at[2]), pltpu.make_async_copy(ortho_ref, ortho_hbm, sems.at[3])]
+    leave[0].start()
+    left = split(left_ref[...])
+    for i in range(rank // BLOCK):
+        upto = (i + 1) * BLOCK
+        ortho_ref[square(i), :] = dot3(split(work[square(i), :upto]), [part[:upto] for part in left], (1, 0))
+    leave[1].start()
+    for part in leave:
+        part.wait()
+
+
+def right_kernel(inverse_hbm, raw_ref, right_hbm, squares_ref, inverse_ref, right_ref, arrive, leave):
     count = raw_ref.shape[0] // BLOCK
-    blocks = [pltpu.make_async_copy(inverse_hbm.at[square(i)], inverse_ref.at[square(i)], arrive.at[i]) for i in range(count)]
+    blocks = [
+        pltpu.make_async_copy(inverse_hbm.at[square(i)], inverse_ref.at[square(i)], arrive.at[i]) for i in range(count)
+    ]
     for block in blocks:
         block.start()
-    raw, left = split(raw_ref[...]), split(left_ref[...])
+    raw = split(raw_ref[...])
     eye = lax.broadcasted_iota(jnp.int32, (BLOCK, BLOCK), 0) == lax.broadcasted_iota(jnp.int32, (BLOCK, BLOCK), 1)
     out = []
     for i in range(count):
         at, upto = square(i), (i + 1) * BLOCK
         blocks[i].wait()
-        inverse = split(inverse_ref[at, :upto])
-        right = dot3(inverse, [part[:upto] for part in raw], (1, 0))
+        right = dot3(split(inverse_ref[at, :upto]), [part[:upto] for part in raw], (1, 0))
         right_ref[at, :] = right
-        ortho_ref[at, :] = dot3(inverse, [part[:upto] for part in left], (1, 0))
-        out.append(pltpu.make_async_copy(right_ref.at[at], right_hbm.at[at], leave.at[0, i]))
-        out.append(pltpu.make_async_copy(ortho_ref.at[at], ortho_hbm.at[at], leave.at[1, i]))
-        out[-2].start()
+        out.append(pltpu.make_async_copy(right_ref.at[at], right_hbm.at[at], leave.at[i]))
         out[-1].start()
         sums = jnp.sum(right * right, axis=1, keepdims=True)
         squares_ref[pl.ds(i, 1), :] = jnp.sum(jnp.where(eye, sums, 0.0), axis=0, keepdims=True)
@@ -300,40 +322,42 @@
         gram_other = swap(gram_own)
         right_raw = exchange(raw, "wide").reshape(rank, cols)
     with jax.named_scope("factor"):
-        (inverse,) = call(
+        inverse, ortho = call(
             factor_kernel,
-            "inverse_factor",
-            [(rank, rank)],
+            "factor",
+            [(rank, rank), (rank, rows)],
             2 * 10**9,
             core,
             gram_own,
             gram_other,
+            left,
             scratch=[
                 pltpu.VMEM(gram_own.shape, jnp.float32),
                 pltpu.VMEM(gram_own.shape, jnp.float32),
                 pltpu.VMEM((rank, rank), jnp.float32),
-                pltpu.VMEM((rank, rank), jnp.float32),
-                pltpu.SemaphoreType.DMA((3,)),
+                pltpu.VMEM((rank, rows), jnp.float32),
+                pltpu.SemaphoreType.DMA((4,)),
             ],
             takes=(1, 2),
-            gives=(0,),
+            gives=(0, 1),
         )
     with jax.named_scope("right"):
-        shapes = [(rank, cols), (rank, rows), (rank // BLOCK, BLOCK)]
-        scratch = [pltpu.VMEM((rank, width), jnp.float32) for width in (rank, cols, rows)]
-        scratch += [pltpu.SemaphoreType.DMA((rank // BLOCK,)), pltpu.SemaphoreType.DMA((2, rank // BLOCK))]
-        right, ortho, squares = call(
+        right, squares = call(
             right_kernel,
             "right",
-            shapes,
+            [(rank, cols), (rank // BLOCK, BLOCK)],
             2 * 10**9,
             inverse,
             right_raw,
-            left,
-            scratch=scratch,
+            scratch=[
+                pltpu.VMEM((rank, rank), jnp.float32),
+                pltpu.VMEM((rank, cols), jnp.float32),
+                pltpu.SemaphoreType.DMA((rank // BLOCK,)),
+                pltpu.SemaphoreType.DMA((rank // BLOCK,)),
+            ],
             limit=14,
             takes=(0,),
-            gives=(0, 1),
+            gives=(0,),
         )
     with jax.named_scope("squares"):
         squares = jnp.broadcast_to(squares[None], (lax.axis_size("col"),) + squares.shape)

time: 220 us -> 216 us (0.982)
  Pallas kernels: 36.5 us -> 32.6 us
    pallas_call x6, Pallas kernels: 36.5 us -> 32.6 us  [call(): pl.pallas_call(kernel, out_shape=[pltpu.HBM(shape, jnp.float32) if i in g...]
  transfers between devices with their start and end apart: 7 -> 7, of which waited for: 6 -> 6; matrix products, arithmetic and copies ran while one was open for 1% -> 1% of each run, Pallas kernels for 13% -> 12%
where the time goes in v5:
time: 216 us; the launch traced here: 215 us
  blocking collectives  104 us (48%)
  waiting for transfers between devices  33.9 us (16%)
  starting transfers between devices  33.8 us (16%)
  Pallas kernels  32.6 us (15%)
  local copies, waits for them, and re-layouts  6.14 us (3%)
  other arithmetic  3.18 us (1%)
    all_to_all x6, blocking collectives, exchange(): lax.all_to_all(blocks, name, 0, 0, axis_index_groups=groups, tiled=False)  104 us
    pallas_call x6, Pallas kernels, call(): pl.pallas_call(kernel, out_shape=[pltpu.HBM(shape, jnp.float32) if i in g...  32.6 us
    all_to_all x3, waiting for transfers between devices, exchange(): lax.all_to_all(blocks, name, 0, 0, axis_index_groups=groups, tiled=False)  25.9 us
    ppermute x3, starting transfers between devices, swap(): return lax.ppermute(part, 'col', [(i, i ^ 1) for i in range(Y * CORES)])  16.9 us
    all_to_all x3, starting transfers between devices, exchange(): lax.all_to_all(blocks, name, 0, 0, axis_index_groups=groups, tiled=False)  13.3 us
  transfers between devices with their start and end apart: 7, of which 6 were waited for; matrix products, arithmetic and copies ran while one was open for 1% of the time, Pallas kernels for 12%

profile of v5, /device:TPU:1, one launch (start us, length us, event | category | flops | bytes accessed | tf_op | source)
XLA Modules:
  0.0 215.0 jit_solution(8963981211881516704)
XLA Ops:
  0.6 0.8 broadcast_in_dim.12
  1.5 19.0 %all_to_all.50 = f32[4,16,896]{2,1,0:T(8,128)S(1)} all-to-all(f32[4,16,896]{2,1,0:T(8,128)S(1)} %broadcast_in_dim.12), channel_id=1, replica_groups={{0,32,64,96},{16,48,80,112},{128,160,192,224},{144,176,208,240},{256,28..., dimensions={0} | all-to-all | bytes 458752 | tf_op jit(solution)/shard_map/basis_gather/all_to_all | solution.py:46
  20.4 1.4 broadcast_in_dim.13
  21.9 6.2 %all-to-all-start.1 = ((f32[8,4,16,896]{3,2,1,0:T(8,128)}), f32[8,4,16,896]{3,2,1,0:T(8,128)S(1)}, u32[]{:S(2)}, u32[]{:S(2)}) async-start(f32[8,4,16,896]{3,2,1,0:T(8,128)} %broadcast_in_dim.13), calls=%async_computation.1 | async-start | bytes 3670016 | tf_op jit(solution)/shard_map/basis_gather/all_to_all | solution.py:46
  28.1 1.3 convert_add_fusion.blended_ref
  29.3 20.5 %all-to-all-done.1 = f32[8,4,16,896]{3,2,1,0:T(8,128)S(1)} async-done(((f32[8,4,16,896]{3,2,1,0:T(8,128)}), f32[8,4,16,896]{3,2,1,0:T(8,128)S(1)}, u32[]{:S(2)}, u32[]{:S(2)}) %all-to-all-start.1) | async-done | bytes 1835040 | tf_op jit(solution)/shard_map/basis_gather/all_to_all | solution.py:46
  49.9 1.0 fusion
  51.0 5.2 %collective-permute-start = (f32[256,256]{0,1:T(8,128)S(1)}, f32[256,256]{0,1:T(8,128)S(1)}, u32[]{:S(2)}, u32[]{:S(2)}) collective-permute-start(f32[256,256]{0,1:T(8,128)S(1)} %dynamic-slice_bitcast_fusion), channel_id=1, source_target_pairs={{0,1},{1,0},{2,3},{3,2},{4,5},{5,4},{6,7},{7,6},{8,9},{9,8},{10,11... | collective-permute-start | bytes 786440 | tf_op jit(solution)/shard_map/left/ppermute | solution.py:62
  56.2 1.1 collective-permute-done
  57.5 17.7 %all_to_all.51 = f32[8,32,256]{2,1,0:T(8,128)S(1)} all-to-all(f32[8,32,256]{2,1,0:T(8,128)S(1)} %bitcast.25), channel_id=1, replica_groups={{0,2,4,6,8,10,12,14},{1,3,5,7,9,11,13,15},{16,18,20,22,24,26,28,30},{17..., dimensions={0} | all-to-all | bytes 524288 | tf_op jit(solution)/shard_map/left/all_to_all | solution.py:46
  75.3 12.1 %all_to_all.52 = f32[8,32,256]{2,1,0:T(8,128)S(1)} all-to-all(f32[8,32,256]{2,1,0:T(8,128)S(1)} %broadcast_in_dim.14), channel_id=1, replica_groups={{0,2,4,6,8,10,12,14},{1,3,5,7,9,11,13,15},{16,18,20,22,24,26,28,30},{17..., dimensions={0} | all-to-all | bytes 524288 | tf_op jit(solution)/shard_map/left/all_to_all | solution.py:46
  87.4 5.0 %collective-permute-start.1 = (f32[256,256]{1,0:T(8,128)S(1)}, f32[256,256]{1,0:T(8,128)S(1)}, u32[]{:S(2)}, u32[]{:S(2)}) collective-permute-start(f32[256,256]{1,0:T(8,128)S(1)} %bitcast.26), channel_id=1, source_target_pairs={{0,1},{1,0},{2,3},{3,2},{4,5},{5,4},{6,7},{7,6},{8,9},{9,8},{10,11... | collective-permute-start | bytes 786440 | tf_op jit(solution)/shard_map/left/ppermute | solution.py:62
  92.4 1.1 collective-permute-done.1
  93.7 1.7 products.1
  95.3 31.2 %all_to_all.53 = f32[8,4,17,8,128]{4,3,2,1,0:T(8,128)} all-to-all(f32[8,4,17,8,128]{4,3,2,1,0:T(8,128)S(1)} %products.1), channel_id=1, replica_groups={{0,16,128,144,256,272,384,400},{32,48,160,176,288,304,416,432},{64,80,1..., dimensions={0} | all-to-all | bytes 4456448 | tf_op jit(solution)/shard_map/sums/all_to_all | solution.py:46
  126.6 1.8 reduce_sum.28
  128.4 10.9 %all_to_all.54 = f32[4,17,8,128]{3,2,1,0:T(8,128)S(1)} all-to-all(f32[4,17,8,128]{3,2,1,0:T(8,128)S(1)} %reduce_sum.28), channel_id=1, replica_groups={{0,32,64,96},{16,48,80,112},{128,160,192,224},{144,176,208,240},{256,28..., dimensions={0} | all-to-all | bytes 557056 | tf_op jit(solution)/shard_map/sums/all_to_all | solution.py:46
  139.3 12.6 %all_to_all.55.sums_ref = f32[4,17,8,128]{3,2,1,0:T(8,128)S(1)} all-to-all(f32[4,17,8,128]{3,2,1,0:T(8,128)S(1)} %broadcast_in_dim.15), channel_id=1, replica_groups={{0,32,64,96},{16,48,80,112},{128,160,192,224},{144,176,208,240},{256,28..., dimensions={0} | all-to-all | bytes 557056 | tf_op jit(solution)/shard_map/sums/all_to_all | solution.py:46
  151.9 0.8 broadcast_in_dim.16
  152.7 3.5 %all-to-all-start.7 = ((f32[8,4,3,8,128]{4,3,2,1,0:T(8,128)}), f32[8,4,3,8,128]{4,3,2,1,0:T(8,128)S(1)}, u32[]{:S(2)}, u32[]{:S(2)}) async-start(f32[8,4,3,8,128]{4,3,2,1,0:T(8,128)} %broadcast_in_dim.16), calls=%async_computation.7 | async-start | bytes 786432 | tf_op jit(solution)/shard_map/sums/all_to_all | solution.py:46
  156.2 1.4 copies.1
  157.5 5.4 %all-to-all-done.7.own_hbm = f32[8,4,3,8,128]{4,3,2,1,0:T(8,128)S(1)} async-done(((f32[8,4,3,8,128]{4,3,2,1,0:T(8,128)}), f32[8,4,3,8,128]{4,3,2,1,0:T(8,128)S(1)}, u32[]{:S(2)}, u32[]{:S(2)}) %all-to-all-start.7) | async-done | bytes 393248 | tf_op jit(solution)/shard_map/sums/all_to_all | solution.py:46
  163.7 3.6 %all-to-all-start.8 = ((f32[8,64,896]{2,1,0:T(8,128)}), f32[8,64,896]{2,1,0:T(8,128)S(1)}, u32[]{:S(2)}, u32[]{:S(2)}) async-start(f32[8,64,896]{2,1,0:T(8,128)} %copies.1), calls=%async_computation.8 | async-start | bytes 3670016 | tf_op jit(solution)/shard_map/sums/all_to_all | solution.py:46
  167.3 6.7 %collective-permute-start.2 = (f32[8,4,3,8,128]{4,3,2,1,0:T(8,128)}, f32[8,4,3,8,128]{4,3,2,1,0:T(8,128)}, u32[]{:S(2)}, u32[]{:S(2)}) collective-permute-start(f32[8,4,3,8,128]{4,3,2,1,0:T(8,128)} %copy-done.4), channel_id=1, source_target_pairs={{0,1},{1,0},{2,3},{3,2},{4,5},{5,4},{6,7},{7,6},{8,9},{9,8},{10,11... | collective-permute-start | bytes 1179656 | tf_op jit(solution)/shard_map/sums/ppermute | solution.py:62
  173.9 1.7 collective-permute-done.2.other_hbm
  175.6 21.4 %factor.1 = (f32[512,512]{1,0:T(8,128)}, f32[512,256]{1,0:T(8,128)}) custom-call(s32[1]{0:T(128)} %bitcast.1.core_ref, f32[8,4,3,8,128]{4,3,2,1,0:T(8,128)} %copy-done.4, f32[8,4,3,8,128]{4,3,2,1,0:T(8,128)} %collective-permute-done.2.other_hbm, f32[512,256]{1,0:T(8,128)S(1)} %bitcast.22), custom_call_target="tpu_custom_call" | custom-call | flops 2000000000 | bytes 4194304 | tf_op jit(solution)/shard_map/factor/factor/pallas_call | solution.py:281
  197.0 4.0 %right.1 = (f32[512,896]{1,0:T(8,128)}, f32[4,128]{1,0:T(4,128)S(1)}) custom-call(f32[512,512]{1,0:T(8,128)} %get-tuple-element.12.inverse_hbm, f32[512,896]{1,0:T(8,128)S(1)} %bitcast.20), custom_call_target="tpu_custom_call" | custom-call | flops 2000000000 | bytes 4194304 | tf_op jit(solution)/shard_map/right/right/pallas_call | solution.py:281
  201.7 3.6 %all-to-all-start.9 = ((f32[16,4,128]{2,1,0:T(4,128)}), f32[16,4,128]{2,1,0:T(4,128)S(1)}, u32[]{:S(2)}, u32[]{:S(2)}) async-start(f32[16,4,128]{2,1,0:T(4,128)} %broadcast_in_dim.17), calls=%async_computation.9 | async-start | bytes 65536 | tf_op jit(solution)/shard_map/squares/all_to_all | solution.py:364
  205.4 1.5 copy-done
  206.8 2.0 momentum.1
  208.8 4.0 %all-to-all-done.9.squares_ref = f32[16,4,128]{2,1,0:T(4,128)S(1)} async-done(((f32[16,4,128]{2,1,0:T(4,128)}), f32[16,4,128]{2,1,0:T(4,128)S(1)}, u32[]{:S(2)}, u32[]{:S(2)}) %all-to-all-start.9) | async-done | bytes 32800 | tf_op jit(solution)/shard_map/squares/all_to_all | solution.py:364
  212.8 2.2 %update.1 = (f32[256,896]{1,0:T(8,128)}, f32[16,896]{1,0:T(8,128)}) custom-call(s32[1]{0:T(128)} %bitcast.start_ref, f32[16,4,128]{2,1,0:T(4,128)S(1)} %all-to-all-done.9.squares_ref, f32[512,256]{1,0:T(8,128)S(1)} %copy-done.2, f32[512,896]{1,0:T(8,128)S(1)} %copy-done.1), custom_call_target="tpu_custom_call" | custom-call | flops 1000000000 | bytes 4194304 | tf_op jit(solution)/shard_map/outputs/update/pallas_call | solution.py:281
  (22 shorter events, 1.8 us)
Async XLA Ops:
  21.9 6.2 %copy-start.3 = (bf16[256,896]{1,0:T(8,128)(2,1)S(1)}, bf16[256,896]{1,0:T(8,128)(2,1)}, u32[]{:S(2)}) copy-start(bf16[256,896]{1,0:T(8,128)(2,1)} %param.4) | copy-start | bytes 1376260
  21.9 28.0 %all-to-all-start.1 = ((f32[8,4,16,896]{3,2,1,0:T(8,128)}), f32[8,4,16,896]{3,2,1,0:T(8,128)S(1)}, u32[]{:S(2)}, u32[]{:S(2)}) async-start(f32[8,4,16,896]{3,2,1,0:T(8,128)} %broadcast_in_dim.13), calls=%async_computation.1 | async-start | bytes 3670016 | tf_op jit(solution)/shard_map/basis_gather/all_to_all | solution.py:46
  51.0 6.3 %collective-permute-start = (f32[256,256]{0,1:T(8,128)S(1)}, f32[256,256]{0,1:T(8,128)S(1)}, u32[]{:S(2)}, u32[]{:S(2)}) collective-permute-start(f32[256,256]{0,1:T(8,128)S(1)} %dynamic-slice_bitcast_fusion), channel_id=1, source_target_pairs={{0,1},{1,0},{2,3},{3,2},{4,5},{5,4},{6,7},{7,6},{8,9},{9,8},{10,11... | collective-permute-start | bytes 786440 | tf_op jit(solution)/shard_map/left/ppermute | solution.py:62
  87.4 6.2 %collective-permute-start.1 = (f32[256,256]{1,0:T(8,128)S(1)}, f32[256,256]{1,0:T(8,128)S(1)}, u32[]{:S(2)}, u32[]{:S(2)}) collective-permute-start(f32[256,256]{1,0:T(8,128)S(1)} %bitcast.26), channel_id=1, source_target_pairs={{0,1},{1,0},{2,3},{3,2},{4,5},{5,4},{6,7},{7,6},{8,9},{9,8},{10,11... | collective-permute-start | bytes 786440 | tf_op jit(solution)/shard_map/left/ppermute | solution.py:62
  152.7 10.2 %all-to-all-start.7 = ((f32[8,4,3,8,128]{4,3,2,1,0:T(8,128)}), f32[8,4,3,8,128]{4,3,2,1,0:T(8,128)S(1)}, u32[]{:S(2)}, u32[]{:S(2)}) async-start(f32[8,4,3,8,128]{4,3,2,1,0:T(8,128)} %broadcast_in_dim.16), calls=%async_computation.7 | async-start | bytes 786432 | tf_op jit(solution)/shard_map/sums/all_to_all | solution.py:46
  162.9 0.7 copy-start.4
  163.7 33.3 %all-to-all-start.8 = ((f32[8,64,896]{2,1,0:T(8,128)}), f32[8,64,896]{2,1,0:T(8,128)S(1)}, u32[]{:S(2)}, u32[]{:S(2)}) async-start(f32[8,64,896]{2,1,0:T(8,128)} %copies.1), calls=%async_computation.8 | async-start | bytes 3670016 | tf_op jit(solution)/shard_map/sums/all_to_all | solution.py:46
  167.3 8.3 %collective-permute-start.2 = (f32[8,4,3,8,128]{4,3,2,1,0:T(8,128)}, f32[8,4,3,8,128]{4,3,2,1,0:T(8,128)}, u32[]{:S(2)}, u32[]{:S(2)}) collective-permute-start(f32[8,4,3,8,128]{4,3,2,1,0:T(8,128)} %copy-done.4), channel_id=1, source_target_pairs={{0,1},{1,0},{2,3},{3,2},{4,5},{5,4},{6,7},{7,6},{8,9},{9,8},{10,11... | collective-permute-start | bytes 1179656 | tf_op jit(solution)/shard_map/sums/ppermute | solution.py:62
  197.0 8.3 %copy-start.2 = (f32[512,256]{1,0:T(8,128)S(1)}, f32[512,256]{1,0:T(8,128)}, u32[]{:S(2)}) copy-start(f32[512,256]{1,0:T(8,128)} %get-tuple-element.15.ortho_ref) | copy-start | bytes 1572868
  201.7 11.1 %all-to-all-start.9 = ((f32[16,4,128]{2,1,0:T(4,128)}), f32[16,4,128]{2,1,0:T(4,128)S(1)}, u32[]{:S(2)}, u32[]{:S(2)}) async-start(f32[16,4,128]{2,1,0:T(4,128)} %broadcast_in_dim.17), calls=%async_computation.9 | async-start | bytes 65536 | tf_op jit(solution)/shard_map/squares/all_to_all | solution.py:364
  205.3 1.5 copy-start
  206.8 6.0 %copy-start.1 = (f32[512,896]{1,0:T(8,128)S(1)}, f32[512,896]{1,0:T(8,128)}, u32[]{:S(2)}) copy-start(f32[512,896]{1,0:T(8,128)} %get-tuple-element.16.right_ref) | copy-start | bytes 5505028

commit v6 on v5

--- a/solution.py
+++ b/solution.py
@@ -19,7 +19,6 @@
 )
 
 
-HIGH = lax.Precision.HIGH
 HIGHEST = lax.Precision.HIGHEST
 epsilon_norm = 1e-06
 retain = 0.7
@@ -46,10 +45,6 @@
     return lax.all_to_all(blocks, name, 0, 0, axis_index_groups=groups, tiled=False)
 
 
-def scatter_sum(blocks, way):
-    return jnp.sum(exchange(blocks, way), axis=0)
-
-
 def copies(part, way):
     return jnp.broadcast_to(part[None], (chips(way)[2],) + part.shape)
 
@@ -60,15 +55,6 @@
 
 def swap(part):
     return lax.ppermute(part, "col", [(i, i ^ 1) for i in range(Y * CORES)])
-
-
-def halves(whole):
-    half = whole.shape[0] // CORES
-    core = lax.axis_index("col") % CORES
-    return (
-        lax.dynamic_slice_in_dim(whole, core * half, half, 0),
-        lax.dynamic_slice_in_dim(whole, (1 - core) * half, half, 0),
-    )
 
 
 def join(own, other):
@@ -86,6 +72,24 @@
         a, b, ((over[:1], over[1:]), ((), ())), preferred_element_type=jnp.float32
     )
     return one(first[0], second[0]) + (one(first[0], second[1]) + one(first[1], second[0]))
+
+
+def left_kernel(half_ref, basis_ref, blended_ref, out_ref):
+    half = out_ref.shape[0]
+    rows = pl.ds(pl.multiple_of(half_ref[0] * half, half), half)
+    out_ref[...] = dot3(split(basis_ref[rows, :]), split(blended_ref[...]), (1, 1))
+
+
+def sum_kernel(blocks_ref, out_ref):
+    for i in range(out_ref.shape[0]):
+        out_ref[i] = sum(blocks_ref[member, i] for member in range(blocks_ref.shape[0]))
+
+
+def sum_copies_kernel(blocks_ref, out_ref):
+    members = range(blocks_ref.shape[0])
+    total = sum(blocks_ref[member] for member in members)
+    for member in members:
+        out_ref[member] = total
 
 
 def square(k):
@@ -157,7 +161,7 @@
     return jnp.concatenate(out, axis=0)
 
 
-def eliminate(work):
+def eliminate(work, finish):
     count = work.shape[0] // BLOCK
     span = lambda first, last: pl.ds(first * BLOCK, (last - first) * BLOCK)
     pending = []
@@ -184,6 +188,7 @@
             pending.append(functools.partial(row, k + 2, count))
         if k:
             pending.append(functools.partial(row, 0, k))
+        pending.append(functools.partial(finish, k))
         for i in range(k + 1, count):
             right = max(i, k + 2)
             if right < count:
@@ -196,15 +201,15 @@
 
 
 def factor_kernel(
-    core_ref, own_hbm, other_hbm, left_ref, out_hbm, ortho_hbm, own_ref, other_ref, work, ortho_ref, sems
+    core_ref, own_hbm, other_hbm, left_ref, out_hbm, ortho_hbm, own_ref, other_ref, work, ortho_ref, high, low, sems
 ):
-    rank = work.shape[0]
     arrive = [
         pltpu.make_async_copy(own_hbm, own_ref, sems.at[0]),
         pltpu.make_async_copy(other_hbm, other_ref, sems.at[1]),
     ]
     for part in arrive:
         part.start()
+    high[...], low[...] = split(left_ref[...])
 
     def place(parts):
         for part_ref, blocks in zip(parts, CORE_BLOCKS):
@@ -217,22 +222,26 @@
         part.wait()
     pl.when(core_ref[0] == 0)(lambda: place((own_ref, other_ref)))
     pl.when(core_ref[0] != 0)(lambda: place((other_ref, own_ref)))
-    eliminate(work)
-    leave = [pltpu.make_async_copy(work, out_hbm, sems.at[2]), pltpu.make_async_copy(ortho_ref, ortho_hbm, sems.at[3])]
-    leave[0].start()
-    left = split(left_ref[...])
-    for i in range(rank // BLOCK):
-        upto = (i + 1) * BLOCK
-        ortho_ref[square(i), :] = dot3(split(work[square(i), :upto]), [part[:upto] for part in left], (1, 0))
-    leave[1].start()
+    leave = []
+
+    def finish(k):
+        at, upto = square(k), pl.ds(0, (k + 1) * BLOCK)
+        leave.append(pltpu.make_async_copy(work.at[at, upto], out_hbm.at[at, upto], sems.at[2 + 2 * k]))
+        leave[-1].start()
+        ortho_ref[at, :] = dot3(split(work[at, upto]), (high[upto, :], low[upto, :]), (1, 0))
+        leave.append(pltpu.make_async_copy(ortho_ref.at[at], ortho_hbm.at[at], sems.at[3 + 2 * k]))
+        leave[-1].start()
+
+    eliminate(work, finish)
     for part in leave:
         part.wait()
 
 
 def right_kernel(inverse_hbm, raw_ref, right_hbm, squares_ref, inverse_ref, right_ref, arrive, leave):
     count = raw_ref.shape[0] // BLOCK
+    lower = [(square(i), pl.ds(0, (i + 1) * BLOCK)) for i in range(count)]
     blocks = [
-        pltpu.make_async_copy(inverse_hbm.at[square(i)], inverse_ref.at[square(i)], arrive.at[i]) for i in range(count)
+        pltpu.make_async_copy(inverse_hbm.at[at], inverse_ref.at[at], arrive.at[i]) for i, at in enumerate(lower)
     ]
     for block in blocks:
         block.start()
@@ -305,9 +314,13 @@
         basis = gather(gather(right_basis.T, "long"), "wide").reshape(rank, cols)
     blended = momentum + gradient.astype(jnp.float32)
     with jax.named_scope("left"):
-        left_own, left_other = halves(dot(basis, blended, (1, 1), HIGH))
-        left_own = left_own + swap(left_other)
-        left_own = gather(scatter_sum(left_own.reshape(Y, -1, rows), "y"), "y").reshape(-1, rows)
+        half = [(rank // CORES, rows)]
+        (left_other,) = call(left_kernel, "left_other", half, 10**9, 1 - core, basis, blended)
+        left_other = swap(left_other)
+        (left_own,) = call(left_kernel, "left_own", half, 10**9, core, basis, blended)
+        parts = exchange((left_own + left_other).reshape(Y, -1, rows), "y")
+        (parts,) = call(sum_copies_kernel, "left_sum", [parts.shape], 10**6, parts)
+        left_own = exchange(parts, "y").reshape(-1, rows)
         left = join(left_own, swap(left_own)).reshape(X, 2, uppers, width, rows)
         left = left.transpose(0, 2, 1, 3, 4).reshape(rank, rows)
     with jax.named_scope("sums"):
@@ -315,7 +328,11 @@
         per_core = (len(CORE_BLOCKS[0]) + 1) // 2
         shape = (members, uppers, tiles + per_core, 8, BLOCK)
         (sums,) = call(products_kernel, "products", [shape], 2 * 10**9, core, left, blended)
-        sums = gather(scatter_sum(scatter_sum(sums, "wide"), "long"), "long")
+        sums = exchange(sums, "wide")
+        (sums,) = call(sum_kernel, "wide_sum", [sums.shape[1:]], 10**6, sums)
+        sums = exchange(sums, "long")
+        (sums,) = call(sum_copies_kernel, "long_sum", [sums.shape], 10**6, sums)
+        sums = exchange(sums, "long")
         gram_own = gather(sums[:, tiles:], "wide")
         (raw,) = call(copies_kernel, "copies", [(members, rank // members, cols)], 10**6, sums)
         gram_own, raw = lax.optimization_barrier((gram_own, raw))
@@ -336,7 +353,9 @@
                 pltpu.VMEM(gram_own.shape, jnp.float32),
                 pltpu.VMEM((rank, rank), jnp.float32),
                 pltpu.VMEM((rank, rows), jnp.float32),
-                pltpu.SemaphoreType.DMA((4,)),
+                pltpu.VMEM((rank, rows), jnp.bfloat16),
+                pltpu.VMEM((rank, rows), jnp.bfloat16),
+                pltpu.SemaphoreType.DMA((2 + 2 * (rank // BLOCK),)),
             ],
             takes=(1, 2),
             gives=(0, 1),

time: 216 us -> 212 us (0.981)
    pallas_call x6 -> x11, Pallas kernels: 32.6 us -> 33.5 us  [call(): pl.pallas_call(kernel, out_shape=[pltpu.HBM(shape, jnp.float32) if i in g...]
where the time goes in v6:
time: 212 us
  blocking collectives  103 us (49%)
  starting transfers between devices  34 us (16%)
  Pallas kernels  33.5 us (16%)
  waiting for transfers between devices  33.3 us (16%)
  local copies, waits for them, and re-layouts  5.94 us (3%)
    all_to_all x6, blocking collectives, exchange(): lax.all_to_all(blocks, name, 0, 0, axis_index_groups=groups, tiled=False)  103 us
    pallas_call x11, Pallas kernels, call(): pl.pallas_call(kernel, out_shape=[pltpu.HBM(shape, jnp.float32) if i in g...  33.5 us
    all_to_all x3, waiting for transfers between devices, exchange(): lax.all_to_all(blocks, name, 0, 0, axis_index_groups=groups, tiled=False)  25.9 us
    ppermute x3, starting transfers between devices, swap(): return lax.ppermute(part, 'col', [(i, i ^ 1) for i in range(Y * CORES)])  17 us
    all_to_all x3, starting transfers between devices, exchange(): lax.all_to_all(blocks, name, 0, 0, axis_index_groups=groups, tiled=False)  13.3 us
  transfers between devices with their start and end apart: 7, of which 6 were waited for; matrix products, arithmetic and copies ran while one was open for 1% of the time, Pallas kernels for 12%

profile of v6, /device:TPU:1, one launch (start us, length us, event | category | flops | bytes accessed | tf_op | source)
XLA Modules:
  0.0 211.6 jit_solution(14872534146980846542)
XLA Ops:
  0.6 0.8 broadcast_in_dim.8
  1.5 19.0 %all_to_all.50 = f32[4,16,896]{2,1,0:T(8,128)S(1)} all-to-all(f32[4,16,896]{2,1,0:T(8,128)S(1)} %broadcast_in_dim.8), channel_id=1, replica_groups={{0,32,64,96},{16,48,80,112},{128,160,192,224},{144,176,208,240},{256,28..., dimensions={0} | all-to-all | bytes 458752 | tf_op jit(solution)/shard_map/basis_gather/all_to_all | solution.py:45
  20.4 1.4 broadcast_in_dim.9
  21.9 6.2 %all-to-all-start.1 = ((f32[8,4,16,896]{3,2,1,0:T(8,128)}), f32[8,4,16,896]{3,2,1,0:T(8,128)S(1)}, u32[]{:S(2)}, u32[]{:S(2)}) async-start(f32[8,4,16,896]{3,2,1,0:T(8,128)} %broadcast_in_dim.9), calls=%async_computation.1 | async-start | bytes 3670016 | tf_op jit(solution)/shard_map/basis_gather/all_to_all | solution.py:45
  28.1 1.3 convert_add_fusion.blended_ref
  29.3 20.5 %all-to-all-done.1 = f32[8,4,16,896]{3,2,1,0:T(8,128)S(1)} async-done(((f32[8,4,16,896]{3,2,1,0:T(8,128)}), f32[8,4,16,896]{3,2,1,0:T(8,128)S(1)}, u32[]{:S(2)}, u32[]{:S(2)}) %all-to-all-start.1) | async-done | bytes 1835040 | tf_op jit(solution)/shard_map/basis_gather/all_to_all | solution.py:45
  50.5 5.2 %collective-permute-start = (f32[256,256]{1,0:T(8,128)S(1)}, f32[256,256]{1,0:T(8,128)S(1)}, u32[]{:S(2)}, u32[]{:S(2)}) collective-permute-start(f32[256,256]{1,0:T(8,128)S(1)} %left_other.1), channel_id=1, source_target_pairs={{0,1},{1,0},{2,3},{3,2},{4,5},{5,4},{6,7},{7,6},{8,9},{9,8},{10,11... | collective-permute-start | bytes 786440 | tf_op jit(solution)/shard_map/left/ppermute | solution.py:57
  55.7 0.6 left_own.1
  56.8 17.7 %all_to_all.51.blocks_ref = f32[8,32,256]{2,1,0:T(8,128)S(1)} all-to-all(f32[8,32,256]{2,1,0:T(8,128)S(1)} %bitcast.20), channel_id=1, replica_groups={{0,2,4,6,8,10,12,14},{1,3,5,7,9,11,13,15},{16,18,20,22,24,26,28,30},{17..., dimensions={0} | all-to-all | bytes 524288 | tf_op jit(solution)/shard_map/left/all_to_all | solution.py:45
  74.6 12.1 %all_to_all.52 = f32[8,32,256]{2,1,0:T(8,128)S(1)} all-to-all(f32[8,32,256]{2,1,0:T(8,128)S(1)} %left_sum.1), channel_id=1, replica_groups={{0,2,4,6,8,10,12,14},{1,3,5,7,9,11,13,15},{16,18,20,22,24,26,28,30},{17..., dimensions={0} | all-to-all | bytes 524288 | tf_op jit(solution)/shard_map/left/all_to_all | solution.py:45
  86.6 5.1 %collective-permute-start.1 = (f32[256,256]{1,0:T(8,128)S(1)}, f32[256,256]{1,0:T(8,128)S(1)}, u32[]{:S(2)}, u32[]{:S(2)}) collective-permute-start(f32[256,256]{1,0:T(8,128)S(1)} %bitcast.21), channel_id=1, source_target_pairs={{0,1},{1,0},{2,3},{3,2},{4,5},{5,4},{6,7},{7,6},{8,9},{9,8},{10,11... | collective-permute-start | bytes 786440 | tf_op jit(solution)/shard_map/left/ppermute | solution.py:57
  91.7 1.1 collective-permute-done.1
  93.0 1.7 products.1
  94.7 30.4 %all_to_all.53.blocks_ref = f32[8,4,17,8,128]{4,3,2,1,0:T(8,128)S(1)} all-to-all(f32[8,4,17,8,128]{4,3,2,1,0:T(8,128)S(1)} %products.1), channel_id=1, replica_groups={{0,16,128,144,256,272,384,400},{32,48,160,176,288,304,416,432},{64,80,1..., dimensions={0} | all-to-all | bytes 4456448 | tf_op jit(solution)/shard_map/sums/all_to_all | solution.py:45
  125.1 11.1 %all_to_all.54.blocks_ref = f32[4,17,8,128]{3,2,1,0:T(8,128)S(1)} all-to-all(f32[4,17,8,128]{3,2,1,0:T(8,128)S(1)} %wide_sum.1), channel_id=1, replica_groups={{0,32,64,96},{16,48,80,112},{128,160,192,224},{144,176,208,240},{256,28..., dimensions={0} | all-to-all | bytes 557056 | tf_op jit(solution)/shard_map/sums/all_to_all | solution.py:45
  136.2 12.5 %all_to_all.55.sums_ref = f32[4,17,8,128]{3,2,1,0:T(8,128)S(1)} all-to-all(f32[4,17,8,128]{3,2,1,0:T(8,128)S(1)} %long_sum.1), channel_id=1, replica_groups={{0,32,64,96},{16,48,80,112},{128,160,192,224},{144,176,208,240},{256,28..., dimensions={0} | all-to-all | bytes 557056 | tf_op jit(solution)/shard_map/sums/all_to_all | solution.py:45
  148.8 0.8 broadcast_in_dim.10
  149.5 3.5 %all-to-all-start.7 = ((f32[8,4,3,8,128]{4,3,2,1,0:T(8,128)}), f32[8,4,3,8,128]{4,3,2,1,0:T(8,128)S(1)}, u32[]{:S(2)}, u32[]{:S(2)}) async-start(f32[8,4,3,8,128]{4,3,2,1,0:T(8,128)} %broadcast_in_dim.10), calls=%async_computation.7 | async-start | bytes 786432 | tf_op jit(solution)/shard_map/sums/all_to_all | solution.py:45
  153.0 1.4 copies.1
  154.4 5.4 %all-to-all-done.7.own_hbm = f32[8,4,3,8,128]{4,3,2,1,0:T(8,128)S(1)} async-done(((f32[8,4,3,8,128]{4,3,2,1,0:T(8,128)}), f32[8,4,3,8,128]{4,3,2,1,0:T(8,128)S(1)}, u32[]{:S(2)}, u32[]{:S(2)}) %all-to-all-start.7) | async-done | bytes 393248 | tf_op jit(solution)/shard_map/sums/all_to_all | solution.py:45
  159.8 0.7 copy-done.4
  160.5 3.6 %all-to-all-start.8 = ((f32[8,64,896]{2,1,0:T(8,128)}), f32[8,64,896]{2,1,0:T(8,128)S(1)}, u32[]{:S(2)}, u32[]{:S(2)}) async-start(f32[8,64,896]{2,1,0:T(8,128)} %copies.1), calls=%async_computation.8 | async-start | bytes 3670016 | tf_op jit(solution)/shard_map/sums/all_to_all | solution.py:45
  164.1 6.8 %collective-permute-start.2 = (f32[8,4,3,8,128]{4,3,2,1,0:T(8,128)}, f32[8,4,3,8,128]{4,3,2,1,0:T(8,128)}, u32[]{:S(2)}, u32[]{:S(2)}) collective-permute-start(f32[8,4,3,8,128]{4,3,2,1,0:T(8,128)} %copy-done.4), channel_id=1, source_target_pairs={{0,1},{1,0},{2,3},{3,2},{4,5},{5,4},{6,7},{7,6},{8,9},{9,8},{10,11... | collective-permute-start | bytes 1179656 | tf_op jit(solution)/shard_map/sums/ppermute | solution.py:57
  170.9 1.7 collective-permute-done.2.other_hbm
  172.6 21.1 %factor.1 = (f32[512,512]{1,0:T(8,128)}, f32[512,256]{1,0:T(8,128)}) custom-call(s32[1]{0:T(128)} %bitcast.1.half_ref.core_ref, f32[8,4,3,8,128]{4,3,2,1,0:T(8,128)} %copy-done.4, f32[8,4,3,8,128]{4,3,2,1,0:T(8,128)} %collective-permute-done.2.other_hbm, f32[512,256]{1,0:T(8,128)S(1)} %bitcast.18), custom_call_target="tpu_custom_call" | custom-call | flops 2000000000 | bytes 4194304 | tf_op jit(solution)/shard_map/factor/factor/pallas_call | solution.py:290
  193.7 3.9 %right.1 = (f32[512,896]{1,0:T(8,128)}, f32[4,128]{1,0:T(4,128)S(1)}) custom-call(f32[512,512]{1,0:T(8,128)} %get-tuple-element.12.inverse_hbm, f32[512,896]{1,0:T(8,128)S(1)} %bitcast.16), custom_call_target="tpu_custom_call" | custom-call | flops 2000000000 | bytes 4194304 | tf_op jit(solution)/shard_map/right/right/pallas_call | solution.py:290
  197.6 0.6 broadcast_in_dim.11
  198.2 3.7 %all-to-all-start.9 = ((f32[16,4,128]{2,1,0:T(4,128)}), f32[16,4,128]{2,1,0:T(4,128)S(1)}, u32[]{:S(2)}, u32[]{:S(2)}) async-start(f32[16,4,128]{2,1,0:T(4,128)} %broadcast_in_dim.11), calls=%async_computation.9 | async-start | bytes 65536 | tf_op jit(solution)/shard_map/squares/all_to_all | solution.py:383
  201.9 1.5 copy-done
  203.4 2.0 momentum.1
  205.4 4.0 %all-to-all-done.9.squares_ref = f32[16,4,128]{2,1,0:T(4,128)S(1)} async-done(((f32[16,4,128]{2,1,0:T(4,128)}), f32[16,4,128]{2,1,0:T(4,128)S(1)}, u32[]{:S(2)}, u32[]{:S(2)}) %all-to-all-start.9) | async-done | bytes 32800 | tf_op jit(solution)/shard_map/squares/all_to_all | solution.py:383
  209.4 2.2 %update.1 = (f32[256,896]{1,0:T(8,128)}, f32[16,896]{1,0:T(8,128)}) custom-call(s32[1]{0:T(128)} %bitcast.start_ref, f32[16,4,128]{2,1,0:T(4,128)S(1)} %all-to-all-done.9.squares_ref, f32[512,256]{1,0:T(8,128)S(1)} %copy-done.2, f32[512,896]{1,0:T(8,128)S(1)} %copy-done.1), custom_call_target="tpu_custom_call" | custom-call | flops 1000000000 | bytes 4194304 | tf_op jit(solution)/shard_map/outputs/update/pallas_call | solution.py:290
  (19 shorter events, 1.4 us)
Async XLA Ops:
  21.9 6.2 %copy-start.3 = (bf16[256,896]{1,0:T(8,128)(2,1)S(1)}, bf16[256,896]{1,0:T(8,128)(2,1)}, u32[]{:S(2)}) copy-start(bf16[256,896]{1,0:T(8,128)(2,1)} %param.4) | copy-start | bytes 1376260
  21.9 28.0 %all-to-all-start.1 = ((f32[8,4,16,896]{3,2,1,0:T(8,128)}), f32[8,4,16,896]{3,2,1,0:T(8,128)S(1)}, u32[]{:S(2)}, u32[]{:S(2)}) async-start(f32[8,4,16,896]{3,2,1,0:T(8,128)} %broadcast_in_dim.9), calls=%async_computation.1 | async-start | bytes 3670016 | tf_op jit(solution)/shard_map/basis_gather/all_to_all | solution.py:45
  50.5 6.3 %collective-permute-start = (f32[256,256]{1,0:T(8,128)S(1)}, f32[256,256]{1,0:T(8,128)S(1)}, u32[]{:S(2)}, u32[]{:S(2)}) collective-permute-start(f32[256,256]{1,0:T(8,128)S(1)} %left_other.1), channel_id=1, source_target_pairs={{0,1},{1,0},{2,3},{3,2},{4,5},{5,4},{6,7},{7,6},{8,9},{9,8},{10,11... | collective-permute-start | bytes 786440 | tf_op jit(solution)/shard_map/left/ppermute | solution.py:57
  86.6 6.2 %collective-permute-start.1 = (f32[256,256]{1,0:T(8,128)S(1)}, f32[256,256]{1,0:T(8,128)S(1)}, u32[]{:S(2)}, u32[]{:S(2)}) collective-permute-start(f32[256,256]{1,0:T(8,128)S(1)} %bitcast.21), channel_id=1, source_target_pairs={{0,1},{1,0},{2,3},{3,2},{4,5},{5,4},{6,7},{7,6},{8,9},{9,8},{10,11... | collective-permute-start | bytes 786440 | tf_op jit(solution)/shard_map/left/ppermute | solution.py:57
  149.5 10.2 %all-to-all-start.7 = ((f32[8,4,3,8,128]{4,3,2,1,0:T(8,128)}), f32[8,4,3,8,128]{4,3,2,1,0:T(8,128)S(1)}, u32[]{:S(2)}, u32[]{:S(2)}) async-start(f32[8,4,3,8,128]{4,3,2,1,0:T(8,128)} %broadcast_in_dim.10), calls=%async_computation.7 | async-start | bytes 786432 | tf_op jit(solution)/shard_map/sums/all_to_all | solution.py:45
  159.8 0.7 copy-start.4
  160.5 33.2 %all-to-all-start.8 = ((f32[8,64,896]{2,1,0:T(8,128)}), f32[8,64,896]{2,1,0:T(8,128)S(1)}, u32[]{:S(2)}, u32[]{:S(2)}) async-start(f32[8,64,896]{2,1,0:T(8,128)} %copies.1), calls=%async_computation.8 | async-start | bytes 3670016 | tf_op jit(solution)/shard_map/sums/all_to_all | solution.py:45
  164.1 8.5 %collective-permute-start.2 = (f32[8,4,3,8,128]{4,3,2,1,0:T(8,128)}, f32[8,4,3,8,128]{4,3,2,1,0:T(8,128)}, u32[]{:S(2)}, u32[]{:S(2)}) collective-permute-start(f32[8,4,3,8,128]{4,3,2,1,0:T(8,128)} %copy-done.4), channel_id=1, source_target_pairs={{0,1},{1,0},{2,3},{3,2},{4,5},{5,4},{6,7},{7,6},{8,9},{9,8},{10,11... | collective-permute-start | bytes 1179656 | tf_op jit(solution)/shard_map/sums/ppermute | solution.py:57
  193.7 8.2 %copy-start.2 = (f32[512,256]{1,0:T(8,128)S(1)}, f32[512,256]{1,0:T(8,128)}, u32[]{:S(2)}) copy-start(f32[512,256]{1,0:T(8,128)} %get-tuple-element.15.ortho_ref) | copy-start | bytes 1572868
  198.2 11.2 %all-to-all-start.9 = ((f32[16,4,128]{2,1,0:T(4,128)}), f32[16,4,128]{2,1,0:T(4,128)S(1)}, u32[]{:S(2)}, u32[]{:S(2)}) async-start(f32[16,4,128]{2,1,0:T(4,128)} %broadcast_in_dim.11), calls=%async_computation.9 | async-start | bytes 65536 | tf_op jit(solution)/shard_map/squares/all_to_all | solution.py:383
  201.9 1.5 copy-start
  203.4 6.0 %copy-start.1 = (f32[512,896]{1,0:T(8,128)S(1)}, f32[512,896]{1,0:T(8,128)}, u32[]{:S(2)}) copy-start(f32[512,896]{1,0:T(8,128)} %get-tuple-element.16.right_ref) | copy-start | bytes 5505028

commit v7 on v6

--- a/solution.py
+++ b/solution.py
@@ -135,28 +135,33 @@
     work = [block[8 * q : 8 * q + 8, :] for q in range(groups)]
     side = [jnp.where(lane == sub + 8 * q, 1.0, 0.0).astype(jnp.float32) for q in range(groups)]
     out = []
+    column = lambda q, c: jnp.broadcast_to(work[q][:, c : c + 1], (8, BLOCK))
+    ahead = [column(0, j) for j in range(8)]
     for p in range(groups):
         if pending:
             pending.pop(0)()
-        spread = {
-            q: [jnp.broadcast_to(work[q][:, 8 * p + j : 8 * p + j + 1], (8, BLOCK)) for j in range(8)]
-            for q in range(p, groups)
-        }
+        spread = {q: [column(q, 8 * p + j) for j in range(8)] for q in range(p + 1, groups)}
+        spread[p] = ahead
+        nearby = {q: [column(q, 8 * p + 8 + j) for j in range(8)] for q in (p, p + 1) if p + 1 < groups}
         pivots = jnp.ones((8, BLOCK), jnp.float32)
         for j in range(8):
-            row = [jnp.broadcast_to(spread[p][k][j : j + 1, :], (8, BLOCK)) for k in range(j, 8)]
-            pivots = jnp.where(sub == j, row[0], pivots)
-            inverse = 1.0 / row[0]
-            row_work = jnp.broadcast_to(work[p][j : j + 1, :], (8, BLOCK))
-            row_side = jnp.broadcast_to(side[p][j : j + 1, :], (8, BLOCK))
+            over = lambda part: jnp.broadcast_to(part[j : j + 1, :], (8, BLOCK))
+            row = {k: over(spread[p][k]) for k in range(j, 8)}
+            pivots = jnp.where(sub == j, row[j], pivots)
+            inverse = 1.0 / row[j]
+            row_work, row_side = over(work[p]), over(side[p])
+            row_near = [over(part) for part in nearby[p]] if nearby else []
             for q in range(p, groups):
                 times = spread[q][j] * inverse
                 if q == p:
                     times = jnp.where(sub > j, times, 0.0)
                 for k in range(j + 1, 8):
-                    spread[q][k] = spread[q][k] - times * row[k - j]
+                    spread[q][k] = spread[q][k] - times * row[k]
+                if q in nearby:
+                    nearby[q] = [part - times * over_row for part, over_row in zip(nearby[q], row_near)]
                 work[q] = work[q] - times * row_work
                 side[q] = side[q] - times * row_side
+        ahead = nearby.get(p + 1)
         out.append(side[p] * lax.rsqrt(pivots))
     return jnp.concatenate(out, axis=0)
 
@@ -256,7 +261,9 @@
         out.append(pltpu.make_async_copy(right_ref.at[at], right_hbm.at[at], leave.at[i]))
         out[-1].start()
         sums = jnp.sum(right * right, axis=1, keepdims=True)
-        squares_ref[pl.ds(i, 1), :] = jnp.sum(jnp.where(eye, sums, 0.0), axis=0, keepdims=True)
+        line = jnp.sum(jnp.where(eye, sums, 0.0), axis=0, keepdims=True)
+        for peer in range(squares_ref.shape[0]):
+            squares_ref[peer, pl.ds(i, 1), :] = line
     for block in out:
         block.wait()
 
@@ -265,7 +272,7 @@
     out_ref[...] = blended_ref[...] - (1.0 - retain) * dot3(split(ortho_ref[...]), split(right_ref[...]), (0, 0))
 
 
-def update_kernel(start_ref, squares_ref, ortho_ref, right_ref, update_ref, basis_ref, scaled):
+def update_kernel(start_ref, squares_ref, ortho_ref, right_ref, update_hbm, basis_ref, scaled, update_ref, leave):
     scale = math.sqrt(ROWS * COLS / RANK)
     rank, width = ortho_ref.shape[0], basis_ref.shape[0]
     rows = jnp.sum(squares_ref[...], axis=0)
@@ -275,10 +282,18 @@
         at = pl.ds(i * BLOCK, BLOCK)
         column = jnp.sum(jnp.where(eye, factors[i : i + 1, :], 0.0), axis=1, keepdims=True)
         scaled[at, :] = jnp.broadcast_to(column, (BLOCK, BLOCK))
-    ortho = ortho_ref[...] * (scale * scaled[:, :1])
-    update_ref[...] = dot3(split(ortho), split(right_ref[...]), (0, 0))
+    ortho = split(ortho_ref[...] * (scale * scaled[:, :1]))
+    cols = right_ref.shape[1]
+    cut = cols // BLOCK // 2 * BLOCK
+    parts = []
+    for i, at in enumerate((pl.ds(0, cut), pl.ds(cut, cols - cut))):
+        update_ref[:, at] = dot3(ortho, split(right_ref[:, at]), (0, 0))
+        parts.append(pltpu.make_async_copy(update_ref.at[:, at], update_hbm.at[:, at], leave.at[i]))
+        parts[-1].start()
     own = pl.ds(pl.multiple_of(start_ref[0], width), width)
     basis_ref[...] = right_ref[own, :] * scaled[own, :1]
+    for part in parts:
+        part.wait()
 
 
 VMEM = pl.BlockSpec(memory_space=pltpu.VMEM)
@@ -364,7 +379,7 @@
         right, squares = call(
             right_kernel,
             "right",
-            [(rank, cols), (rank // BLOCK, BLOCK)],
+            [(rank, cols), (lax.axis_size("col"), rank // BLOCK, BLOCK)],
             2 * 10**9,
             inverse,
             right_raw,
@@ -379,15 +394,15 @@
             gives=(0,),
         )
     with jax.named_scope("squares"):
-        squares = jnp.broadcast_to(squares[None], (lax.axis_size("col"),) + squares.shape)
         squares = lax.all_to_all(squares, "col", 0, 0, tiled=False)
     with jax.named_scope("outputs"):
         (new_momentum,) = call(momentum_kernel, "momentum", [(rows, cols)], 10**9, blended, ortho, right)
         start = (lax.axis_index("row") * width).astype(jnp.int32).reshape(1)
         shapes = [(rows, cols), (width, cols)]
-        scratch = [pltpu.VMEM((rank, BLOCK), jnp.float32)]
+        scratch = [pltpu.VMEM((rank, BLOCK), jnp.float32), pltpu.VMEM((rows, cols), jnp.float32)]
+        scratch += [pltpu.SemaphoreType.DMA((2,))]
         update, new_basis = call(
-            update_kernel, "update", shapes, 10**9, start, squares, ortho, right, scratch=scratch
+            update_kernel, "update", shapes, 10**9, start, squares, ortho, right, scratch=scratch, gives=(0,)
         )
         new_basis = new_basis.T
     return (update, new_momentum, new_basis)

time: 212 us -> 211 us (level)
  transfers between devices with their start and end apart: 7 -> 7, of which waited for: 6 -> 6; matrix products, arithmetic and copies ran while one was open for 1% -> 1% of each run, Pallas kernels for 12% -> 11%
where the time goes in v7:
time: 211 us
  blocking collectives  103 us (49%)
  starting transfers between devices  34 us (16%)
  waiting for transfers between devices  33.3 us (16%)
  Pallas kernels  33 us (16%)
  local copies, waits for them, and re-layouts  5.32 us (3%)
    all_to_all x6, blocking collectives, exchange(): lax.all_to_all(blocks, name, 0, 0, axis_index_groups=groups, tiled=False)  103 us
    pallas_call x11, Pallas kernels, call(): pl.pallas_call(kernel, out_shape=[pltpu.HBM(shape, jnp.float32) if i in g...  33 us
    all_to_all x3, waiting for transfers between devices, exchange(): lax.all_to_all(blocks, name, 0, 0, axis_index_groups=groups, tiled=False)  25.9 us
    ppermute x3, starting transfers between devices, swap(): return lax.ppermute(part, 'col', [(i, i ^ 1) for i in range(Y * CORES)])  17 us
    all_to_all x3, starting transfers between devices, exchange(): lax.all_to_all(blocks, name, 0, 0, axis_index_groups=groups, tiled=False)  13.3 us
  transfers between devices with their start and end apart: 7, of which 6 were waited for; matrix products, arithmetic and copies ran while one was open for 1% of the time, Pallas kernels for 11%

profile of v7, /device:TPU:1, one launch (start us, length us, event | category | flops | bytes accessed | tf_op | source)
XLA Modules:
  0.0 210.6 jit_solution(11940864012182577856)
XLA Ops:
  0.6 0.8 broadcast_in_dim.6
  1.5 19.0 %all_to_all.50 = f32[4,16,896]{2,1,0:T(8,128)S(1)} all-to-all(f32[4,16,896]{2,1,0:T(8,128)S(1)} %broadcast_in_dim.6), channel_id=1, replica_groups={{0,32,64,96},{16,48,80,112},{128,160,192,224},{144,176,208,240},{256,28..., dimensions={0} | all-to-all | bytes 458752 | tf_op jit(solution)/shard_map/basis_gather/all_to_all | solution.py:45
  20.4 1.4 broadcast_in_dim.7
  21.9 6.2 %all-to-all-start.1 = ((f32[8,4,16,896]{3,2,1,0:T(8,128)}), f32[8,4,16,896]{3,2,1,0:T(8,128)S(1)}, u32[]{:S(2)}, u32[]{:S(2)}) async-start(f32[8,4,16,896]{3,2,1,0:T(8,128)} %broadcast_in_dim.7), calls=%async_computation.1 | async-start | bytes 3670016 | tf_op jit(solution)/shard_map/basis_gather/all_to_all | solution.py:45
  28.1 1.3 convert_add_fusion.blended_ref
  29.3 20.5 %all-to-all-done.1 = f32[8,4,16,896]{3,2,1,0:T(8,128)S(1)} async-done(((f32[8,4,16,896]{3,2,1,0:T(8,128)}), f32[8,4,16,896]{3,2,1,0:T(8,128)S(1)}, u32[]{:S(2)}, u32[]{:S(2)}) %all-to-all-start.1) | async-done | bytes 1835040 | tf_op jit(solution)/shard_map/basis_gather/all_to_all | solution.py:45
  49.9 0.6 left_other.1
  50.5 5.2 %collective-permute-start = (f32[256,256]{1,0:T(8,128)S(1)}, f32[256,256]{1,0:T(8,128)S(1)}, u32[]{:S(2)}, u32[]{:S(2)}) collective-permute-start(f32[256,256]{1,0:T(8,128)S(1)} %left_other.1), channel_id=1, source_target_pairs={{0,1},{1,0},{2,3},{3,2},{4,5},{5,4},{6,7},{7,6},{8,9},{9,8},{10,11... | collective-permute-start | bytes 786440 | tf_op jit(solution)/shard_map/left/ppermute | solution.py:57
  55.7 0.6 left_own.1
  56.8 17.7 %all_to_all.51.blocks_ref = f32[8,32,256]{2,1,0:T(8,128)S(1)} all-to-all(f32[8,32,256]{2,1,0:T(8,128)S(1)} %bitcast.20), channel_id=1, replica_groups={{0,2,4,6,8,10,12,14},{1,3,5,7,9,11,13,15},{16,18,20,22,24,26,28,30},{17..., dimensions={0} | all-to-all | bytes 524288 | tf_op jit(solution)/shard_map/left/all_to_all | solution.py:45
  74.6 12.1 %all_to_all.52 = f32[8,32,256]{2,1,0:T(8,128)S(1)} all-to-all(f32[8,32,256]{2,1,0:T(8,128)S(1)} %left_sum.1), channel_id=1, replica_groups={{0,2,4,6,8,10,12,14},{1,3,5,7,9,11,13,15},{16,18,20,22,24,26,28,30},{17..., dimensions={0} | all-to-all | bytes 524288 | tf_op jit(solution)/shard_map/left/all_to_all | solution.py:45
  86.6 5.1 %collective-permute-start.1 = (f32[256,256]{1,0:T(8,128)S(1)}, f32[256,256]{1,0:T(8,128)S(1)}, u32[]{:S(2)}, u32[]{:S(2)}) collective-permute-start(f32[256,256]{1,0:T(8,128)S(1)} %bitcast.21), channel_id=1, source_target_pairs={{0,1},{1,0},{2,3},{3,2},{4,5},{5,4},{6,7},{7,6},{8,9},{9,8},{10,11... | collective-permute-start | bytes 786440 | tf_op jit(solution)/shard_map/left/ppermute | solution.py:57
  91.7 1.1 collective-permute-done.1
  93.0 1.7 products.1
  94.7 30.4 %all_to_all.53.blocks_ref = f32[8,4,17,8,128]{4,3,2,1,0:T(8,128)S(1)} all-to-all(f32[8,4,17,8,128]{4,3,2,1,0:T(8,128)S(1)} %products.1), channel_id=1, replica_groups={{0,16,128,144,256,272,384,400},{32,48,160,176,288,304,416,432},{64,80,1..., dimensions={0} | all-to-all | bytes 4456448 | tf_op jit(solution)/shard_map/sums/all_to_all | solution.py:45
  125.1 11.1 %all_to_all.54.blocks_ref = f32[4,17,8,128]{3,2,1,0:T(8,128)S(1)} all-to-all(f32[4,17,8,128]{3,2,1,0:T(8,128)S(1)} %wide_sum.1), channel_id=1, replica_groups={{0,32,64,96},{16,48,80,112},{128,160,192,224},{144,176,208,240},{256,28..., dimensions={0} | all-to-all | bytes 557056 | tf_op jit(solution)/shard_map/sums/all_to_all | solution.py:45
  136.2 12.5 %all_to_all.55.sums_ref = f32[4,17,8,128]{3,2,1,0:T(8,128)S(1)} all-to-all(f32[4,17,8,128]{3,2,1,0:T(8,128)S(1)} %long_sum.1), channel_id=1, replica_groups={{0,32,64,96},{16,48,80,112},{128,160,192,224},{144,176,208,240},{256,28..., dimensions={0} | all-to-all | bytes 557056 | tf_op jit(solution)/shard_map/sums/all_to_all | solution.py:45
  148.8 0.8 broadcast_in_dim.8
  149.5 3.5 %all-to-all-start.7 = ((f32[8,4,3,8,128]{4,3,2,1,0:T(8,128)}), f32[8,4,3,8,128]{4,3,2,1,0:T(8,128)S(1)}, u32[]{:S(2)}, u32[]{:S(2)}) async-start(f32[8,4,3,8,128]{4,3,2,1,0:T(8,128)} %broadcast_in_dim.8), calls=%async_computation.7 | async-start | bytes 786432 | tf_op jit(solution)/shard_map/sums/all_to_all | solution.py:45
  153.0 1.4 copies.1
  154.4 5.4 %all-to-all-done.7.own_hbm = f32[8,4,3,8,128]{4,3,2,1,0:T(8,128)S(1)} async-done(((f32[8,4,3,8,128]{4,3,2,1,0:T(8,128)}), f32[8,4,3,8,128]{4,3,2,1,0:T(8,128)S(1)}, u32[]{:S(2)}, u32[]{:S(2)}) %all-to-all-start.7) | async-done | bytes 393248 | tf_op jit(solution)/shard_map/sums/all_to_all | solution.py:45
  159.8 0.7 copy-done.4
  160.5 3.6 %all-to-all-start.8 = ((f32[8,64,896]{2,1,0:T(8,128)}), f32[8,64,896]{2,1,0:T(8,128)S(1)}, u32[]{:S(2)}, u32[]{:S(2)}) async-start(f32[8,64,896]{2,1,0:T(8,128)} %copies.1), calls=%async_computation.8 | async-start | bytes 3670016 | tf_op jit(solution)/shard_map/sums/all_to_all | solution.py:45
  164.1 6.8 %collective-permute-start.2 = (f32[8,4,3,8,128]{4,3,2,1,0:T(8,128)}, f32[8,4,3,8,128]{4,3,2,1,0:T(8,128)}, u32[]{:S(2)}, u32[]{:S(2)}) collective-permute-start(f32[8,4,3,8,128]{4,3,2,1,0:T(8,128)} %copy-done.4), channel_id=1, source_target_pairs={{0,1},{1,0},{2,3},{3,2},{4,5},{5,4},{6,7},{7,6},{8,9},{9,8},{10,11... | collective-permute-start | bytes 1179656 | tf_op jit(solution)/shard_map/sums/ppermute | solution.py:57
  170.9 1.7 collective-permute-done.2.other_hbm
  172.6 19.4 %factor.1 = (f32[512,512]{1,0:T(8,128)}, f32[512,256]{1,0:T(8,128)}) custom-call(s32[1]{0:T(128)} %bitcast.1.half_ref.core_ref, f32[8,4,3,8,128]{4,3,2,1,0:T(8,128)} %copy-done.4, f32[8,4,3,8,128]{4,3,2,1,0:T(8,128)} %collective-permute-done.2.other_hbm, f32[512,256]{1,0:T(8,128)S(1)} %bitcast.18), custom_call_target="tpu_custom_call" | custom-call | flops 2000000000 | bytes 4194304 | tf_op jit(solution)/shard_map/factor/factor/pallas_call | solution.py:305
  192.0 4.5 %right.1 = (f32[512,896]{1,0:T(8,128)}, f32[16,4,128]{2,1,0:T(4,128)}) custom-call(f32[512,512]{1,0:T(8,128)} %get-tuple-element.12.inverse_hbm, f32[512,896]{1,0:T(8,128)S(1)} %bitcast.16), custom_call_target="tpu_custom_call" | custom-call | flops 2000000000 | bytes 4194304 | tf_op jit(solution)/shard_map/right/right/pallas_call | solution.py:305
  196.6 3.7 %all-to-all-start.9 = ((f32[16,4,128]{2,1,0:T(4,128)}), f32[16,4,128]{2,1,0:T(4,128)S(1)}, u32[]{:S(2)}, u32[]{:S(2)}) async-start(f32[16,4,128]{2,1,0:T(4,128)} %get-tuple-element.14), calls=%async_computation.9 | async-start | bytes 65536 | tf_op jit(solution)/shard_map/squares/all_to_all | solution.py:397
  200.3 1.5 copy-done
  201.7 2.0 momentum.1
  203.7 4.0 %all-to-all-done.9.squares_ref = f32[16,4,128]{2,1,0:T(4,128)S(1)} async-done(((f32[16,4,128]{2,1,0:T(4,128)}), f32[16,4,128]{2,1,0:T(4,128)S(1)}, u32[]{:S(2)}, u32[]{:S(2)}) %all-to-all-start.9) | async-done | bytes 32800 | tf_op jit(solution)/shard_map/squares/all_to_all | solution.py:397
  207.7 2.7 %update.1 = (f32[256,896]{1,0:T(8,128)}, f32[16,896]{1,0:T(8,128)}) custom-call(s32[1]{0:T(128)} %bitcast.start_ref, f32[16,4,128]{2,1,0:T(4,128)S(1)} %all-to-all-done.9.squares_ref, f32[512,256]{1,0:T(8,128)S(1)} %copy-done.2, f32[512,896]{1,0:T(8,128)S(1)} %copy-done.1), custom_call_target="tpu_custom_call" | custom-call | flops 1000000000 | bytes 4194304 | tf_op jit(solution)/shard_map/outputs/update/pallas_call | solution.py:305
  (18 shorter events, 0.9 us)
Async XLA Ops:
  21.9 6.2 %copy-start.3 = (bf16[256,896]{1,0:T(8,128)(2,1)S(1)}, bf16[256,896]{1,0:T(8,128)(2,1)}, u32[]{:S(2)}) copy-start(bf16[256,896]{1,0:T(8,128)(2,1)} %param.4) | copy-start | bytes 1376260
  21.9 28.0 %all-to-all-start.1 = ((f32[8,4,16,896]{3,2,1,0:T(8,128)}), f32[8,4,16,896]{3,2,1,0:T(8,128)S(1)}, u32[]{:S(2)}, u32[]{:S(2)}) async-start(f32[8,4,16,896]{3,2,1,0:T(8,128)} %broadcast_in_dim.7), calls=%async_computation.1 | async-start | bytes 3670016 | tf_op jit(solution)/shard_map/basis_gather/all_to_all | solution.py:45
  50.5 6.3 %collective-permute-start = (f32[256,256]{1,0:T(8,128)S(1)}, f32[256,256]{1,0:T(8,128)S(1)}, u32[]{:S(2)}, u32[]{:S(2)}) collective-permute-start(f32[256,256]{1,0:T(8,128)S(1)} %left_other.1), channel_id=1, source_target_pairs={{0,1},{1,0},{2,3},{3,2},{4,5},{5,4},{6,7},{7,6},{8,9},{9,8},{10,11... | collective-permute-start | bytes 786440 | tf_op jit(solution)/shard_map/left/ppermute | solution.py:57
  86.6 6.2 %collective-permute-start.1 = (f32[256,256]{1,0:T(8,128)S(1)}, f32[256,256]{1,0:T(8,128)S(1)}, u32[]{:S(2)}, u32[]{:S(2)}) collective-permute-start(f32[256,256]{1,0:T(8,128)S(1)} %bitcast.21), channel_id=1, source_target_pairs={{0,1},{1,0},{2,3},{3,2},{4,5},{5,4},{6,7},{7,6},{8,9},{9,8},{10,11... | collective-permute-start | bytes 786440 | tf_op jit(solution)/shard_map/left/ppermute | solution.py:57
  149.5 10.2 %all-to-all-start.7 = ((f32[8,4,3,8,128]{4,3,2,1,0:T(8,128)}), f32[8,4,3,8,128]{4,3,2,1,0:T(8,128)S(1)}, u32[]{:S(2)}, u32[]{:S(2)}) async-start(f32[8,4,3,8,128]{4,3,2,1,0:T(8,128)} %broadcast_in_dim.8), calls=%async_computation.7 | async-start | bytes 786432 | tf_op jit(solution)/shard_map/sums/all_to_all | solution.py:45
  159.8 0.7 copy-start.4
  160.5 31.5 %all-to-all-start.8 = ((f32[8,64,896]{2,1,0:T(8,128)}), f32[8,64,896]{2,1,0:T(8,128)S(1)}, u32[]{:S(2)}, u32[]{:S(2)}) async-start(f32[8,64,896]{2,1,0:T(8,128)} %copies.1), calls=%async_computation.8 | async-start | bytes 3670016 | tf_op jit(solution)/shard_map/sums/all_to_all | solution.py:45
  164.1 8.5 %collective-permute-start.2 = (f32[8,4,3,8,128]{4,3,2,1,0:T(8,128)}, f32[8,4,3,8,128]{4,3,2,1,0:T(8,128)}, u32[]{:S(2)}, u32[]{:S(2)}) collective-permute-start(f32[8,4,3,8,128]{4,3,2,1,0:T(8,128)} %copy-done.4), channel_id=1, source_target_pairs={{0,1},{1,0},{2,3},{3,2},{4,5},{5,4},{6,7},{7,6},{8,9},{9,8},{10,11... | collective-permute-start | bytes 1179656 | tf_op jit(solution)/shard_map/sums/ppermute | solution.py:57
  192.0 8.2 %copy-start.2 = (f32[512,256]{1,0:T(8,128)S(1)}, f32[512,256]{1,0:T(8,128)}, u32[]{:S(2)}) copy-start(f32[512,256]{1,0:T(8,128)} %get-tuple-element.15.ortho_ref) | copy-start | bytes 1572868
  196.6 11.1 %all-to-all-start.9 = ((f32[16,4,128]{2,1,0:T(4,128)}), f32[16,4,128]{2,1,0:T(4,128)S(1)}, u32[]{:S(2)}, u32[]{:S(2)}) async-start(f32[16,4,128]{2,1,0:T(4,128)} %get-tuple-element.14), calls=%async_computation.9 | async-start | bytes 65536 | tf_op jit(solution)/shard_map/squares/all_to_all | solution.py:397
  200.2 1.5 copy-start
  201.7 6.0 %copy-start.1 = (f32[512,896]{1,0:T(8,128)S(1)}, f32[512,896]{1,0:T(8,128)}, u32[]{:S(2)}) copy-start(f32[512,896]{1,0:T(8,128)} %get-tuple-element.16.right_ref) | copy-start | bytes 5505028

commit v8 on v7

--- a/solution.py
+++ b/solution.py
@@ -57,11 +57,6 @@
     return lax.ppermute(part, "col", [(i, i ^ 1) for i in range(Y * CORES)])
 
 
-def join(own, other):
-    first = lax.axis_index("col") % CORES == 0
-    return jnp.concatenate([jnp.where(first, own, other), jnp.where(first, other, own)], axis=0)
-
-
 def split(value):
     high = value.astype(jnp.bfloat16)
     return high, (value - high.astype(jnp.float32)).astype(jnp.bfloat16)
@@ -96,22 +91,46 @@
     return pl.ds(k * BLOCK, BLOCK)
 
 
-def products_kernel(core_ref, left_ref, blended_ref, out_ref):
-    members, uppers = out_ref.shape[:2]
-    deep = left_ref.shape[0] // (8 * members * uppers)
-    lanes = blended_ref.shape[1] // BLOCK
-    right = dot3(split(left_ref[...]), split(blended_ref[...]), (1, 0))
+def natural(part):
+    upper = Z // 2
+    width = part.shape[0] // (X // CORES * Z)
+    order = [(x * 2 + low) * upper + high for x in range(X // CORES) for high in range(upper) for low in range(2)]
+    return jnp.concatenate([part[i * width : (i + 1) * width] for i in order], axis=0)
+
+
+def store_tiles(out_ref, first, members, right):
+    uppers = out_ref.shape[1]
+    deep, lanes = right.shape[0] // (8 * members * uppers), right.shape[1] // BLOCK
     for j in range(lanes):
         tiles = right[:, j * BLOCK : (j + 1) * BLOCK].reshape(members, uppers, deep, 8, BLOCK)
         for i in range(deep):
-            out_ref[:, :, i * lanes + j] = tiles[:, :, i]
+            out_ref[pl.ds(first, members), :, i * lanes + j] = tiles[:, :, i]
+
+
+def own_products_kernel(part_ref, blended_ref, out_ref, rows_ref):
+    rows = natural(part_ref[...])
+    rows_ref[...] = rows
+    store_tiles(out_ref, 0, out_ref.shape[0], dot3(split(rows), split(blended_ref[...]), (1, 0)))
+
+
+def products_kernel(core_ref, done_ref, rows_ref, part_ref, blended_ref, out_ref, left_ref):
+    members, uppers, tiles = done_ref.shape[:3]
+    half = rows_ref.shape[0]
+    core = core_ref[0]
+    own = pl.ds(pl.multiple_of(core * half, half), half)
+    other = pl.ds(pl.multiple_of((1 - core) * half, half), half)
+    rows = natural(part_ref[...])
+    left_ref[own, :] = rows_ref[...]
+    left_ref[other, :] = rows
+    out_ref[pl.ds(core * members, members), :, pl.ds(0, tiles)] = done_ref[...]
+    store_tiles(out_ref, (1 - core) * members, members, dot3(split(rows), split(blended_ref[...]), (1, 0)))
 
     def gram(blocks):
         found = [dot(left_ref[square(k), :], left_ref[square(l), :], (1, 1), HIGHEST) for k, l in blocks]
         found.append(jnp.zeros((BLOCK, BLOCK), jnp.float32))
         for t in range(len(found) // 2):
             pair = jnp.concatenate(found[2 * t : 2 * t + 2], axis=0)
-            out_ref[:, :, deep * lanes + t] = pair.reshape(members, uppers, 8, BLOCK)
+            out_ref[:, :, tiles + t] = pair.reshape(CORES * members, uppers, 8, BLOCK)
 
     pl.when(core_ref[0] == 0)(lambda: gram(CORE_BLOCKS[0]))
     pl.when(core_ref[0] != 0)(lambda: gram(CORE_BLOCKS[1]))
@@ -251,11 +270,12 @@
     for block in blocks:
         block.start()
     raw = split(raw_ref[...])
+    for block in blocks:
+        block.wait()
     eye = lax.broadcasted_iota(jnp.int32, (BLOCK, BLOCK), 0) == lax.broadcasted_iota(jnp.int32, (BLOCK, BLOCK), 1)
     out = []
     for i in range(count):
         at, upto = square(i), (i + 1) * BLOCK
-        blocks[i].wait()
         right = dot3(split(inverse_ref[at, :upto]), [part[:upto] for part in raw], (1, 0))
         right_ref[at, :] = right
         out.append(pltpu.make_async_copy(right_ref.at[at], right_hbm.at[at], leave.at[i]))
@@ -272,7 +292,7 @@
     out_ref[...] = blended_ref[...] - (1.0 - retain) * dot3(split(ortho_ref[...]), split(right_ref[...]), (0, 0))
 
 
-def update_kernel(start_ref, squares_ref, ortho_ref, right_ref, update_hbm, basis_ref, scaled, update_ref, leave):
+def update_kernel(start_ref, squares_ref, ortho_ref, right_ref, update_ref, basis_ref, scaled):
     scale = math.sqrt(ROWS * COLS / RANK)
     rank, width = ortho_ref.shape[0], basis_ref.shape[0]
     rows = jnp.sum(squares_ref[...], axis=0)
@@ -282,18 +302,10 @@
         at = pl.ds(i * BLOCK, BLOCK)
         column = jnp.sum(jnp.where(eye, factors[i : i + 1, :], 0.0), axis=1, keepdims=True)
         scaled[at, :] = jnp.broadcast_to(column, (BLOCK, BLOCK))
-    ortho = split(ortho_ref[...] * (scale * scaled[:, :1]))
-    cols = right_ref.shape[1]
-    cut = cols // BLOCK // 2 * BLOCK
-    parts = []
-    for i, at in enumerate((pl.ds(0, cut), pl.ds(cut, cols - cut))):
-        update_ref[:, at] = dot3(ortho, split(right_ref[:, at]), (0, 0))
-        parts.append(pltpu.make_async_copy(update_ref.at[:, at], update_hbm.at[:, at], leave.at[i]))
-        parts[-1].start()
+    ortho = ortho_ref[...] * (scale * scaled[:, :1])
+    update_ref[...] = dot3(split(ortho), split(right_ref[...]), (0, 0))
     own = pl.ds(pl.multiple_of(start_ref[0], width), width)
     basis_ref[...] = right_ref[own, :] * scaled[own, :1]
-    for part in parts:
-        part.wait()
 
 
 VMEM = pl.BlockSpec(memory_space=pltpu.VMEM)
@@ -336,13 +348,15 @@
         parts = exchange((left_own + left_other).reshape(Y, -1, rows), "y")
         (parts,) = call(sum_copies_kernel, "left_sum", [parts.shape], 10**6, parts)
         left_own = exchange(parts, "y").reshape(-1, rows)
-        left = join(left_own, swap(left_own)).reshape(X, 2, uppers, width, rows)
-        left = left.transpose(0, 2, 1, 3, 4).reshape(rank, rows)
     with jax.named_scope("sums"):
         tiles = width // 8 * (cols // BLOCK)
         per_core = (len(CORE_BLOCKS[0]) + 1) // 2
         shape = (members, uppers, tiles + per_core, 8, BLOCK)
-        (sums,) = call(products_kernel, "products", [shape], 2 * 10**9, core, left, blended)
+        mine = [(members // CORES, uppers, tiles, 8, BLOCK), (rank // CORES, rows)]
+        left_other = swap(left_own)
+        mine = call(own_products_kernel, "own_products", mine, 10**9, left_own, blended)
+        shapes = [shape, (rank, rows)]
+        sums, left = call(products_kernel, "products", shapes, 2 * 10**9, core, *mine, left_other, blended)
         sums = exchange(sums, "wide")
         (sums,) = call(sum_kernel, "wide_sum", [sums.shape[1:]], 10**6, sums)
         sums = exchange(sums, "long")
@@ -399,10 +413,9 @@
         (new_momentum,) = call(momentum_kernel, "momentum", [(rows, cols)], 10**9, blended, ortho, right)
         start = (lax.axis_index("row") * width).astype(jnp.int32).reshape(1)
         shapes = [(rows, cols), (width, cols)]
-        scratch = [pltpu.VMEM((rank, BLOCK), jnp.float32), pltpu.VMEM((rows, cols), jnp.float32)]
-        scratch += [pltpu.SemaphoreType.DMA((2,))]
+        scratch = [pltpu.VMEM((rank, BLOCK), jnp.float32)]
         update, new_basis = call(
-            update_kernel, "update", shapes, 10**9, start, squares, ortho, right, scratch=scratch, gives=(0,)
+            update_kernel, "update", shapes, 10**9, start, squares, ortho, right, scratch=scratch
         )
         new_basis = new_basis.T
     return (update, new_momentum, new_basis)

time: 211 us -> 210 us (level)
    pallas_call x11 -> x12, Pallas kernels: 33 us -> 32.3 us  [call(): pl.pallas_call(kernel, out_shape=[pltpu.HBM(shape, jnp.float32) if i in g...]
where the time goes in v8:
time: 210 us; the launch traced here: 209 us
  blocking collectives  103 us (49%)
  starting transfers between devices  34 us (16%)
  waiting for transfers between devices  32.7 us (16%)
  Pallas kernels  32.3 us (15%)
  local copies, waits for them, and re-layouts  5.28 us (3%)
    all_to_all x6, blocking collectives, exchange(): lax.all_to_all(blocks, name, 0, 0, axis_index_groups=groups, tiled=False)  103 us
    pallas_call x12, Pallas kernels, call(): pl.pallas_call(kernel, out_shape=[pltpu.HBM(shape, jnp.float32) if i in g...  32.3 us
    all_to_all x3, waiting for transfers between devices, exchange(): lax.all_to_all(blocks, name, 0, 0, axis_index_groups=groups, tiled=False)  25.9 us
    ppermute x3, starting transfers between devices, swap(): return lax.ppermute(part, 'col', [(i, i ^ 1) for i in range(Y * CORES)])  17 us
    all_to_all x3, starting transfers between devices, exchange(): lax.all_to_all(blocks, name, 0, 0, axis_index_groups=groups, tiled=False)  13.3 us
  transfers between devices with their start and end apart: 7, of which 6 were waited for; matrix products, arithmetic and copies ran while one was open for 1% of the time, Pallas kernels for 11%

profile of v8, /device:TPU:1, one launch (start us, length us, event | category | flops | bytes accessed | tf_op | source)
XLA Modules:
  0.0 209.0 jit_solution(7450336059787494738)
XLA Ops:
  0.6 0.8 broadcast_in_dim.6
  1.5 19.0 %all_to_all.50 = f32[4,16,896]{2,1,0:T(8,128)S(1)} all-to-all(f32[4,16,896]{2,1,0:T(8,128)S(1)} %broadcast_in_dim.6), channel_id=1, replica_groups={{0,32,64,96},{16,48,80,112},{128,160,192,224},{144,176,208,240},{256,28..., dimensions={0} | all-to-all | bytes 458752 | tf_op jit(solution)/shard_map/basis_gather/all_to_all | solution.py:45
  20.4 1.4 broadcast_in_dim.7
  21.8 6.2 %all-to-all-start.1 = ((f32[8,4,16,896]{3,2,1,0:T(8,128)}), f32[8,4,16,896]{3,2,1,0:T(8,128)S(1)}, u32[]{:S(2)}, u32[]{:S(2)}) async-start(f32[8,4,16,896]{3,2,1,0:T(8,128)} %broadcast_in_dim.7), calls=%async_computation.1 | async-start | bytes 3670016 | tf_op jit(solution)/shard_map/basis_gather/all_to_all | solution.py:45
  28.1 1.3 convert_add_fusion.blended_ref
  29.3 20.5 %all-to-all-done.1 = f32[8,4,16,896]{3,2,1,0:T(8,128)S(1)} async-done(((f32[8,4,16,896]{3,2,1,0:T(8,128)}), f32[8,4,16,896]{3,2,1,0:T(8,128)S(1)}, u32[]{:S(2)}, u32[]{:S(2)}) %all-to-all-start.1) | async-done | bytes 1835040 | tf_op jit(solution)/shard_map/basis_gather/all_to_all | solution.py:45
  49.9 0.6 left_other.1
  50.5 5.2 %collective-permute-start = (f32[256,256]{1,0:T(8,128)S(1)}, f32[256,256]{1,0:T(8,128)S(1)}, u32[]{:S(2)}, u32[]{:S(2)}) collective-permute-start(f32[256,256]{1,0:T(8,128)S(1)} %left_other.1), channel_id=1, source_target_pairs={{0,1},{1,0},{2,3},{3,2},{4,5},{5,4},{6,7},{7,6},{8,9},{9,8},{10,11... | collective-permute-start | bytes 786440 | tf_op jit(solution)/shard_map/left/ppermute | solution.py:57
  55.7 0.6 left_own.1
  56.8 17.7 %all_to_all.51.blocks_ref = f32[8,32,256]{2,1,0:T(8,128)S(1)} all-to-all(f32[8,32,256]{2,1,0:T(8,128)S(1)} %bitcast.13), channel_id=1, replica_groups={{0,2,4,6,8,10,12,14},{1,3,5,7,9,11,13,15},{16,18,20,22,24,26,28,30},{17..., dimensions={0} | all-to-all | bytes 524288 | tf_op jit(solution)/shard_map/left/all_to_all | solution.py:45
  74.6 12.1 %all_to_all.52 = f32[8,32,256]{2,1,0:T(8,128)S(1)} all-to-all(f32[8,32,256]{2,1,0:T(8,128)S(1)} %left_sum.1), channel_id=1, replica_groups={{0,2,4,6,8,10,12,14},{1,3,5,7,9,11,13,15},{16,18,20,22,24,26,28,30},{17..., dimensions={0} | all-to-all | bytes 524288 | tf_op jit(solution)/shard_map/left/all_to_all | solution.py:45
  86.6 5.1 %collective-permute-start.1 = (f32[256,256]{1,0:T(8,128)S(1)}, f32[256,256]{1,0:T(8,128)S(1)}, u32[]{:S(2)}, u32[]{:S(2)}) collective-permute-start(f32[256,256]{1,0:T(8,128)S(1)} %bitcast.11), channel_id=1, source_target_pairs={{0,1},{1,0},{2,3},{3,2},{4,5},{5,4},{6,7},{7,6},{8,9},{9,8},{10,11... | collective-permute-start | bytes 786440 | tf_op jit(solution)/shard_map/sums/ppermute | solution.py:57
  91.7 0.6 own_products.1
  92.9 1.3 products.1
  94.2 30.4 %all_to_all.53.blocks_ref = f32[8,4,17,8,128]{4,3,2,1,0:T(8,128)S(1)} all-to-all(f32[8,4,17,8,128]{4,3,2,1,0:T(8,128)S(1)} %get-tuple-element.17), channel_id=1, replica_groups={{0,16,128,144,256,272,384,400},{32,48,160,176,288,304,416,432},{64,80,1..., dimensions={0} | all-to-all | bytes 4456448 | tf_op jit(solution)/shard_map/sums/all_to_all | solution.py:45
  124.7 11.0 %all_to_all.54.blocks_ref = f32[4,17,8,128]{3,2,1,0:T(8,128)S(1)} all-to-all(f32[4,17,8,128]{3,2,1,0:T(8,128)S(1)} %wide_sum.1), channel_id=1, replica_groups={{0,32,64,96},{16,48,80,112},{128,160,192,224},{144,176,208,240},{256,28..., dimensions={0} | all-to-all | bytes 557056 | tf_op jit(solution)/shard_map/sums/all_to_all | solution.py:45
  135.8 12.5 %all_to_all.55.sums_ref = f32[4,17,8,128]{3,2,1,0:T(8,128)S(1)} all-to-all(f32[4,17,8,128]{3,2,1,0:T(8,128)S(1)} %long_sum.1), channel_id=1, replica_groups={{0,32,64,96},{16,48,80,112},{128,160,192,224},{144,176,208,240},{256,28..., dimensions={0} | all-to-all | bytes 557056 | tf_op jit(solution)/shard_map/sums/all_to_all | solution.py:45
  148.3 0.8 broadcast_in_dim.8
  149.1 3.5 %all-to-all-start.7 = ((f32[8,4,3,8,128]{4,3,2,1,0:T(8,128)}), f32[8,4,3,8,128]{4,3,2,1,0:T(8,128)S(1)}, u32[]{:S(2)}, u32[]{:S(2)}) async-start(f32[8,4,3,8,128]{4,3,2,1,0:T(8,128)} %broadcast_in_dim.8), calls=%async_computation.7 | async-start | bytes 786432 | tf_op jit(solution)/shard_map/sums/all_to_all | solution.py:45
  152.6 1.4 copies.1
  154.0 5.4 %all-to-all-done.7.own_hbm = f32[8,4,3,8,128]{4,3,2,1,0:T(8,128)S(1)} async-done(((f32[8,4,3,8,128]{4,3,2,1,0:T(8,128)}), f32[8,4,3,8,128]{4,3,2,1,0:T(8,128)S(1)}, u32[]{:S(2)}, u32[]{:S(2)}) %all-to-all-start.7) | async-done | bytes 393248 | tf_op jit(solution)/shard_map/sums/all_to_all | solution.py:45
  159.3 0.7 copy-done.4
  160.1 3.6 %all-to-all-start.8 = ((f32[8,64,896]{2,1,0:T(8,128)}), f32[8,64,896]{2,1,0:T(8,128)S(1)}, u32[]{:S(2)}, u32[]{:S(2)}) async-start(f32[8,64,896]{2,1,0:T(8,128)} %copies.1), calls=%async_computation.8 | async-start | bytes 3670016 | tf_op jit(solution)/shard_map/sums/all_to_all | solution.py:45
  163.7 6.8 %collective-permute-start.2 = (f32[8,4,3,8,128]{4,3,2,1,0:T(8,128)}, f32[8,4,3,8,128]{4,3,2,1,0:T(8,128)}, u32[]{:S(2)}, u32[]{:S(2)}) collective-permute-start(f32[8,4,3,8,128]{4,3,2,1,0:T(8,128)} %copy-done.4), channel_id=1, source_target_pairs={{0,1},{1,0},{2,3},{3,2},{4,5},{5,4},{6,7},{7,6},{8,9},{9,8},{10,11... | collective-permute-start | bytes 1179656 | tf_op jit(solution)/shard_map/sums/ppermute | solution.py:57
  170.5 1.7 collective-permute-done.2.other_hbm
  172.2 19.4 %factor.1 = (f32[512,512]{1,0:T(8,128)}, f32[512,256]{1,0:T(8,128)}) custom-call(s32[1]{0:T(128)} %bitcast.1.half_ref.core_ref, f32[8,4,3,8,128]{4,3,2,1,0:T(8,128)} %copy-done.4, f32[8,4,3,8,128]{4,3,2,1,0:T(8,128)} %collective-permute-done.2.other_hbm, f32[512,256]{1,0:T(8,128)S(1)} %get-tuple-element.19.left_ref), custom_call_target="tpu_custom_call" | custom-call | flops 2000000000 | bytes 4194304 | tf_op jit(solution)/shard_map/factor/factor/pallas_call | solution.py:317
  191.6 4.0 %right.1 = (f32[512,896]{1,0:T(8,128)}, f32[16,4,128]{2,1,0:T(4,128)}) custom-call(f32[512,512]{1,0:T(8,128)} %get-tuple-element.20.inverse_hbm, f32[512,896]{1,0:T(8,128)S(1)} %bitcast.10), custom_call_target="tpu_custom_call" | custom-call | flops 2000000000 | bytes 4194304 | tf_op jit(solution)/shard_map/right/right/pallas_call | solution.py:317
  195.7 3.7 %all-to-all-start.9 = ((f32[16,4,128]{2,1,0:T(4,128)}), f32[16,4,128]{2,1,0:T(4,128)S(1)}, u32[]{:S(2)}, u32[]{:S(2)}) async-start(f32[16,4,128]{2,1,0:T(4,128)} %get-tuple-element.22), calls=%async_computation.9 | async-start | bytes 65536 | tf_op jit(solution)/shard_map/squares/all_to_all | solution.py:411
  199.4 1.5 copy-done
  200.8 2.0 momentum.1
  202.8 4.0 %all-to-all-done.9.squares_ref = f32[16,4,128]{2,1,0:T(4,128)S(1)} async-done(((f32[16,4,128]{2,1,0:T(4,128)}), f32[16,4,128]{2,1,0:T(4,128)S(1)}, u32[]{:S(2)}, u32[]{:S(2)}) %all-to-all-start.9) | async-done | bytes 32800 | tf_op jit(solution)/shard_map/squares/all_to_all | solution.py:411
  206.8 2.2 %update.1 = (f32[256,896]{1,0:T(8,128)}, f32[16,896]{1,0:T(8,128)}) custom-call(s32[1]{0:T(128)} %bitcast.start_ref, f32[16,4,128]{2,1,0:T(4,128)S(1)} %all-to-all-done.9.squares_ref, f32[512,256]{1,0:T(8,128)S(1)} %copy-done.2, f32[512,896]{1,0:T(8,128)S(1)} %copy-done.1), custom_call_target="tpu_custom_call" | custom-call | flops 1000000000 | bytes 4194304 | tf_op jit(solution)/shard_map/outputs/update/pallas_call | solution.py:317
  (16 shorter events, 1.3 us)
Async XLA Ops:
  21.8 6.2 %copy-start.3 = (bf16[256,896]{1,0:T(8,128)(2,1)S(1)}, bf16[256,896]{1,0:T(8,128)(2,1)}, u32[]{:S(2)}) copy-start(bf16[256,896]{1,0:T(8,128)(2,1)} %param.4) | copy-start | bytes 1376260
  21.8 28.0 %all-to-all-start.1 = ((f32[8,4,16,896]{3,2,1,0:T(8,128)}), f32[8,4,16,896]{3,2,1,0:T(8,128)S(1)}, u32[]{:S(2)}, u32[]{:S(2)}) async-start(f32[8,4,16,896]{3,2,1,0:T(8,128)} %broadcast_in_dim.7), calls=%async_computation.1 | async-start | bytes 3670016 | tf_op jit(solution)/shard_map/basis_gather/all_to_all | solution.py:45
  50.5 6.3 %collective-permute-start = (f32[256,256]{1,0:T(8,128)S(1)}, f32[256,256]{1,0:T(8,128)S(1)}, u32[]{:S(2)}, u32[]{:S(2)}) collective-permute-start(f32[256,256]{1,0:T(8,128)S(1)} %left_other.1), channel_id=1, source_target_pairs={{0,1},{1,0},{2,3},{3,2},{4,5},{5,4},{6,7},{7,6},{8,9},{9,8},{10,11... | collective-permute-start | bytes 786440 | tf_op jit(solution)/shard_map/left/ppermute | solution.py:57
  86.6 6.2 %collective-permute-start.1 = (f32[256,256]{1,0:T(8,128)S(1)}, f32[256,256]{1,0:T(8,128)S(1)}, u32[]{:S(2)}, u32[]{:S(2)}) collective-permute-start(f32[256,256]{1,0:T(8,128)S(1)} %bitcast.11), channel_id=1, source_target_pairs={{0,1},{1,0},{2,3},{3,2},{4,5},{5,4},{6,7},{7,6},{8,9},{9,8},{10,11... | collective-permute-start | bytes 786440 | tf_op jit(solution)/shard_map/sums/ppermute | solution.py:57
  149.1 10.2 %all-to-all-start.7 = ((f32[8,4,3,8,128]{4,3,2,1,0:T(8,128)}), f32[8,4,3,8,128]{4,3,2,1,0:T(8,128)S(1)}, u32[]{:S(2)}, u32[]{:S(2)}) async-start(f32[8,4,3,8,128]{4,3,2,1,0:T(8,128)} %broadcast_in_dim.8), calls=%async_computation.7 | async-start | bytes 786432 | tf_op jit(solution)/shard_map/sums/all_to_all | solution.py:45
  159.3 0.7 copy-start.4
  160.1 31.5 %all-to-all-start.8 = ((f32[8,64,896]{2,1,0:T(8,128)}), f32[8,64,896]{2,1,0:T(8,128)S(1)}, u32[]{:S(2)}, u32[]{:S(2)}) async-start(f32[8,64,896]{2,1,0:T(8,128)} %copies.1), calls=%async_computation.8 | async-start | bytes 3670016 | tf_op jit(solution)/shard_map/sums/all_to_all | solution.py:45
  163.7 8.5 %collective-permute-start.2 = (f32[8,4,3,8,128]{4,3,2,1,0:T(8,128)}, f32[8,4,3,8,128]{4,3,2,1,0:T(8,128)}, u32[]{:S(2)}, u32[]{:S(2)}) collective-permute-start(f32[8,4,3,8,128]{4,3,2,1,0:T(8,128)} %copy-done.4), channel_id=1, source_target_pairs={{0,1},{1,0},{2,3},{3,2},{4,5},{5,4},{6,7},{7,6},{8,9},{9,8},{10,11... | collective-permute-start | bytes 1179656 | tf_op jit(solution)/shard_map/sums/ppermute | solution.py:57
  191.6 7.7 %copy-start.2 = (f32[512,256]{1,0:T(8,128)S(1)}, f32[512,256]{1,0:T(8,128)}, u32[]{:S(2)}) copy-start(f32[512,256]{1,0:T(8,128)} %get-tuple-element.23.ortho_ref) | copy-start | bytes 1572868
  195.7 11.2 %all-to-all-start.9 = ((f32[16,4,128]{2,1,0:T(4,128)}), f32[16,4,128]{2,1,0:T(4,128)S(1)}, u32[]{:S(2)}, u32[]{:S(2)}) async-start(f32[16,4,128]{2,1,0:T(4,128)} %get-tuple-element.22), calls=%async_computation.9 | async-start | bytes 65536 | tf_op jit(solution)/shard_map/squares/all_to_all | solution.py:411
  199.3 1.5 copy-start
  200.8 6.0 %copy-start.1 = (f32[512,896]{1,0:T(8,128)S(1)}, f32[512,896]{1,0:T(8,128)}, u32[]{:S(2)}) copy-start(f32[512,896]{1,0:T(8,128)} %get-tuple-element.24.right_ref) | copy-start | bytes 5505028

commit v9 on v8

--- a/solution.py
+++ b/solution.py
@@ -14,8 +14,8 @@
 BLOCK = 128
 X, Y, Z, CORES = 4, 8, 8, 2
 CORE_BLOCKS = (
-    ((0, 0), (0, 1), (0, 2), (0, 3), (1, 1)),
-    ((1, 2), (1, 3), (2, 2), (2, 3), (3, 3)),
+    ((0, 0), (0, 1), (1, 1), (0, 2), (0, 3)),
+    ((2, 2), (2, 3), (3, 3), (1, 2), (1, 3)),
 )
 
 
@@ -88,7 +88,7 @@
 
 
 def square(k):
-    return pl.ds(k * BLOCK, BLOCK)
+    return pl.ds(k * BLOCK if isinstance(k, int) else pl.multiple_of(k * BLOCK, BLOCK), BLOCK)
 
 
 def natural(part):
@@ -107,13 +107,16 @@
             out_ref[pl.ds(first, members), :, i * lanes + j] = tiles[:, :, i]
 
 
-def own_products_kernel(part_ref, blended_ref, out_ref, rows_ref):
+def own_products_kernel(part_ref, blended_ref, out_ref, rows_ref, gram_ref):
     rows = natural(part_ref[...])
     rows_ref[...] = rows
     store_tiles(out_ref, 0, out_ref.shape[0], dot3(split(rows), split(blended_ref[...]), (1, 0)))
-
-
-def products_kernel(core_ref, done_ref, rows_ref, part_ref, blended_ref, out_ref, left_ref):
+    for i, (k, l) in enumerate(CORE_BLOCKS[0][:3]):
+        first, second = rows[k * BLOCK : (k + 1) * BLOCK], rows[l * BLOCK : (l + 1) * BLOCK]
+        gram_ref[i] = dot(first, second, (1, 1), HIGHEST)
+
+
+def products_kernel(core_ref, done_ref, rows_ref, gram_ref, part_ref, blended_ref, out_ref, left_ref):
     members, uppers, tiles = done_ref.shape[:3]
     half = rows_ref.shape[0]
     core = core_ref[0]
@@ -124,16 +127,11 @@
     left_ref[other, :] = rows
     out_ref[pl.ds(core * members, members), :, pl.ds(0, tiles)] = done_ref[...]
     store_tiles(out_ref, (1 - core) * members, members, dot3(split(rows), split(blended_ref[...]), (1, 0)))
-
-    def gram(blocks):
-        found = [dot(left_ref[square(k), :], left_ref[square(l), :], (1, 1), HIGHEST) for k, l in blocks]
-        found.append(jnp.zeros((BLOCK, BLOCK), jnp.float32))
-        for t in range(len(found) // 2):
-            pair = jnp.concatenate(found[2 * t : 2 * t + 2], axis=0)
-            out_ref[:, :, tiles + t] = pair.reshape(CORES * members, uppers, 8, BLOCK)
-
-    pl.when(core_ref[0] == 0)(lambda: gram(CORE_BLOCKS[0]))
-    pl.when(core_ref[0] != 0)(lambda: gram(CORE_BLOCKS[1]))
+    across = dot(left_ref[square(core), :], left_ref[half:, :], (1, 1), HIGHEST)
+    found = [gram_ref[i] for i in range(3)] + [across[:, :BLOCK], across[:, BLOCK:], jnp.zeros_like(gram_ref[0])]
+    for t in range(len(found) // 2):
+        pair = jnp.concatenate(found[2 * t : 2 * t + 2], axis=0)
+        out_ref[:, :, tiles + t] = pair.reshape(CORES * members, uppers, 8, BLOCK)
 
 
 def copies_kernel(sums_ref, out_ref):
@@ -352,7 +350,7 @@
         tiles = width // 8 * (cols // BLOCK)
         per_core = (len(CORE_BLOCKS[0]) + 1) // 2
         shape = (members, uppers, tiles + per_core, 8, BLOCK)
-        mine = [(members // CORES, uppers, tiles, 8, BLOCK), (rank // CORES, rows)]
+        mine = [(members // CORES, uppers, tiles, 8, BLOCK), (rank // CORES, rows), (3, BLOCK, BLOCK)]
         left_other = swap(left_own)
         mine = call(own_products_kernel, "own_products", mine, 10**9, left_own, blended)
         shapes = [shape, (rank, rows)]

time: 210 us -> 209 us (level)
  transfers between devices with their start and end apart: 7 -> 7, of which waited for: 6 -> 6; matrix products, arithmetic and copies ran while one was open for 1% -> 1% of each run, Pallas kernels for 11% -> 12%
where the time goes in v9:
time: 209 us
  blocking collectives  103 us (49%)
  starting transfers between devices  34 us (16%)
  waiting for transfers between devices  32.4 us (16%)
  Pallas kernels  32 us (15%)
  local copies, waits for them, and re-layouts  5.28 us (3%)
    all_to_all x6, blocking collectives, exchange(): lax.all_to_all(blocks, name, 0, 0, axis_index_groups=groups, tiled=False)  103 us
    pallas_call x12, Pallas kernels, call(): pl.pallas_call(kernel, out_shape=[pltpu.HBM(shape, jnp.float32) if i in g...  32 us
    all_to_all x3, waiting for transfers between devices, exchange(): lax.all_to_all(blocks, name, 0, 0, axis_index_groups=groups, tiled=False)  25.9 us
    ppermute x3, starting transfers between devices, swap(): return lax.ppermute(part, 'col', [(i, i ^ 1) for i in range(Y * CORES)])  17 us
    all_to_all x3, starting transfers between devices, exchange(): lax.all_to_all(blocks, name, 0, 0, axis_index_groups=groups, tiled=False)  13.3 us
  transfers between devices with their start and end apart: 7, of which 6 were waited for; matrix products, arithmetic and copies ran while one was open for 1% of the time, Pallas kernels for 12%

profile of v9, /device:TPU:1, one launch (start us, length us, event | category | flops | bytes accessed | tf_op | source)
XLA Modules:
  0.0 208.5 jit_solution(10388505089766427668)
XLA Ops:
  0.6 0.8 broadcast_in_dim.6
  1.5 19.0 %all_to_all.50 = f32[4,16,896]{2,1,0:T(8,128)S(1)} all-to-all(f32[4,16,896]{2,1,0:T(8,128)S(1)} %broadcast_in_dim.6), channel_id=1, replica_groups={{0,32,64,96},{16,48,80,112},{128,160,192,224},{144,176,208,240},{256,28..., dimensions={0} | all-to-all | bytes 458752 | tf_op jit(solution)/shard_map/basis_gather/all_to_all | solution.py:45
  20.4 1.4 broadcast_in_dim.7
  21.8 6.2 %all-to-all-start.1 = ((f32[8,4,16,896]{3,2,1,0:T(8,128)}), f32[8,4,16,896]{3,2,1,0:T(8,128)S(1)}, u32[]{:S(2)}, u32[]{:S(2)}) async-start(f32[8,4,16,896]{3,2,1,0:T(8,128)} %broadcast_in_dim.7), calls=%async_computation.1 | async-start | bytes 3670016 | tf_op jit(solution)/shard_map/basis_gather/all_to_all | solution.py:45
  28.1 1.3 convert_add_fusion.blended_ref
  29.3 20.5 %all-to-all-done.1 = f32[8,4,16,896]{3,2,1,0:T(8,128)S(1)} async-done(((f32[8,4,16,896]{3,2,1,0:T(8,128)}), f32[8,4,16,896]{3,2,1,0:T(8,128)S(1)}, u32[]{:S(2)}, u32[]{:S(2)}) %all-to-all-start.1) | async-done | bytes 1835040 | tf_op jit(solution)/shard_map/basis_gather/all_to_all | solution.py:45
  49.9 0.6 left_other.1
  50.5 5.2 %collective-permute-start = (f32[256,256]{1,0:T(8,128)S(1)}, f32[256,256]{1,0:T(8,128)S(1)}, u32[]{:S(2)}, u32[]{:S(2)}) collective-permute-start(f32[256,256]{1,0:T(8,128)S(1)} %left_other.1), channel_id=1, source_target_pairs={{0,1},{1,0},{2,3},{3,2},{4,5},{5,4},{6,7},{7,6},{8,9},{9,8},{10,11... | collective-permute-start | bytes 786440 | tf_op jit(solution)/shard_map/left/ppermute | solution.py:57
  55.7 0.6 left_own.1
  56.8 17.7 %all_to_all.51.blocks_ref = f32[8,32,256]{2,1,0:T(8,128)S(1)} all-to-all(f32[8,32,256]{2,1,0:T(8,128)S(1)} %bitcast.13), channel_id=1, replica_groups={{0,2,4,6,8,10,12,14},{1,3,5,7,9,11,13,15},{16,18,20,22,24,26,28,30},{17..., dimensions={0} | all-to-all | bytes 524288 | tf_op jit(solution)/shard_map/left/all_to_all | solution.py:45
  74.6 12.1 %all_to_all.52 = f32[8,32,256]{2,1,0:T(8,128)S(1)} all-to-all(f32[8,32,256]{2,1,0:T(8,128)S(1)} %left_sum.1), channel_id=1, replica_groups={{0,2,4,6,8,10,12,14},{1,3,5,7,9,11,13,15},{16,18,20,22,24,26,28,30},{17..., dimensions={0} | all-to-all | bytes 524288 | tf_op jit(solution)/shard_map/left/all_to_all | solution.py:45
  86.6 5.1 %collective-permute-start.1 = (f32[256,256]{1,0:T(8,128)S(1)}, f32[256,256]{1,0:T(8,128)S(1)}, u32[]{:S(2)}, u32[]{:S(2)}) collective-permute-start(f32[256,256]{1,0:T(8,128)S(1)} %bitcast.11), channel_id=1, source_target_pairs={{0,1},{1,0},{2,3},{3,2},{4,5},{5,4},{6,7},{7,6},{8,9},{9,8},{10,11... | collective-permute-start | bytes 786440 | tf_op jit(solution)/shard_map/sums/ppermute | solution.py:57
  91.7 0.9 own_products.1
  92.9 0.8 products.1
  93.7 30.4 %all_to_all.53.blocks_ref = f32[8,4,17,8,128]{4,3,2,1,0:T(8,128)S(1)} all-to-all(f32[8,4,17,8,128]{4,3,2,1,0:T(8,128)S(1)} %get-tuple-element.19), channel_id=1, replica_groups={{0,16,128,144,256,272,384,400},{32,48,160,176,288,304,416,432},{64,80,1..., dimensions={0} | all-to-all | bytes 4456448 | tf_op jit(solution)/shard_map/sums/all_to_all | solution.py:45
  124.2 11.0 %all_to_all.54.blocks_ref = f32[4,17,8,128]{3,2,1,0:T(8,128)S(1)} all-to-all(f32[4,17,8,128]{3,2,1,0:T(8,128)S(1)} %wide_sum.1), channel_id=1, replica_groups={{0,32,64,96},{16,48,80,112},{128,160,192,224},{144,176,208,240},{256,28..., dimensions={0} | all-to-all | bytes 557056 | tf_op jit(solution)/shard_map/sums/all_to_all | solution.py:45
  135.2 12.6 %all_to_all.55.sums_ref = f32[4,17,8,128]{3,2,1,0:T(8,128)S(1)} all-to-all(f32[4,17,8,128]{3,2,1,0:T(8,128)S(1)} %long_sum.1), channel_id=1, replica_groups={{0,32,64,96},{16,48,80,112},{128,160,192,224},{144,176,208,240},{256,28..., dimensions={0} | all-to-all | bytes 557056 | tf_op jit(solution)/shard_map/sums/all_to_all | solution.py:45
  147.8 0.8 broadcast_in_dim.8
  148.6 3.5 %all-to-all-start.7 = ((f32[8,4,3,8,128]{4,3,2,1,0:T(8,128)}), f32[8,4,3,8,128]{4,3,2,1,0:T(8,128)S(1)}, u32[]{:S(2)}, u32[]{:S(2)}) async-start(f32[8,4,3,8,128]{4,3,2,1,0:T(8,128)} %broadcast_in_dim.8), calls=%async_computation.7 | async-start | bytes 786432 | tf_op jit(solution)/shard_map/sums/all_to_all | solution.py:45
  152.1 1.4 copies.1
  153.5 5.4 %all-to-all-done.7.own_hbm = f32[8,4,3,8,128]{4,3,2,1,0:T(8,128)S(1)} async-done(((f32[8,4,3,8,128]{4,3,2,1,0:T(8,128)}), f32[8,4,3,8,128]{4,3,2,1,0:T(8,128)S(1)}, u32[]{:S(2)}, u32[]{:S(2)}) %all-to-all-start.7) | async-done | bytes 393248 | tf_op jit(solution)/shard_map/sums/all_to_all | solution.py:45
  158.8 0.7 copy-done.4
  159.6 3.6 %all-to-all-start.8 = ((f32[8,64,896]{2,1,0:T(8,128)}), f32[8,64,896]{2,1,0:T(8,128)S(1)}, u32[]{:S(2)}, u32[]{:S(2)}) async-start(f32[8,64,896]{2,1,0:T(8,128)} %copies.1), calls=%async_computation.8 | async-start | bytes 3670016 | tf_op jit(solution)/shard_map/sums/all_to_all | solution.py:45
  163.2 6.8 %collective-permute-start.2 = (f32[8,4,3,8,128]{4,3,2,1,0:T(8,128)}, f32[8,4,3,8,128]{4,3,2,1,0:T(8,128)}, u32[]{:S(2)}, u32[]{:S(2)}) collective-permute-start(f32[8,4,3,8,128]{4,3,2,1,0:T(8,128)} %copy-done.4), channel_id=1, source_target_pairs={{0,1},{1,0},{2,3},{3,2},{4,5},{5,4},{6,7},{7,6},{8,9},{9,8},{10,11... | collective-permute-start | bytes 1179656 | tf_op jit(solution)/shard_map/sums/ppermute | solution.py:57
  170.0 1.7 collective-permute-done.2.other_hbm
  171.6 19.4 %factor.1 = (f32[512,512]{1,0:T(8,128)}, f32[512,256]{1,0:T(8,128)}) custom-call(s32[1]{0:T(128)} %bitcast.1.half_ref.core_ref, f32[8,4,3,8,128]{4,3,2,1,0:T(8,128)} %copy-done.4, f32[8,4,3,8,128]{4,3,2,1,0:T(8,128)} %collective-permute-done.2.other_hbm, f32[512,256]{1,0:T(8,128)S(1)} %get-tuple-element.21.left_ref), custom_call_target="tpu_custom_call" | custom-call | flops 2000000000 | bytes 4194304 | tf_op jit(solution)/shard_map/factor/factor/pallas_call | solution.py:315
  191.1 4.0 %right.1 = (f32[512,896]{1,0:T(8,128)}, f32[16,4,128]{2,1,0:T(4,128)}) custom-call(f32[512,512]{1,0:T(8,128)} %get-tuple-element.22.inverse_hbm, f32[512,896]{1,0:T(8,128)S(1)} %bitcast.10), custom_call_target="tpu_custom_call" | custom-call | flops 2000000000 | bytes 4194304 | tf_op jit(solution)/shard_map/right/right/pallas_call | solution.py:315
  195.1 3.7 %all-to-all-start.9 = ((f32[16,4,128]{2,1,0:T(4,128)}), f32[16,4,128]{2,1,0:T(4,128)S(1)}, u32[]{:S(2)}, u32[]{:S(2)}) async-start(f32[16,4,128]{2,1,0:T(4,128)} %get-tuple-element.24), calls=%async_computation.9 | async-start | bytes 65536 | tf_op jit(solution)/shard_map/squares/all_to_all | solution.py:409
  198.8 1.5 copy-done
  200.3 2.0 momentum.1
  202.3 4.0 %all-to-all-done.9.squares_ref = f32[16,4,128]{2,1,0:T(4,128)S(1)} async-done(((f32[16,4,128]{2,1,0:T(4,128)}), f32[16,4,128]{2,1,0:T(4,128)S(1)}, u32[]{:S(2)}, u32[]{:S(2)}) %all-to-all-start.9) | async-done | bytes 32800 | tf_op jit(solution)/shard_map/squares/all_to_all | solution.py:409
  206.3 2.2 %update.1 = (f32[256,896]{1,0:T(8,128)}, f32[16,896]{1,0:T(8,128)}) custom-call(s32[1]{0:T(128)} %bitcast.start_ref, f32[16,4,128]{2,1,0:T(4,128)S(1)} %all-to-all-done.9.squares_ref, f32[512,256]{1,0:T(8,128)S(1)} %copy-done.2, f32[512,896]{1,0:T(8,128)S(1)} %copy-done.1), custom_call_target="tpu_custom_call" | custom-call | flops 1000000000 | bytes 4194304 | tf_op jit(solution)/shard_map/outputs/update/pallas_call | solution.py:315
  (16 shorter events, 1.0 us)
Async XLA Ops:
  21.8 6.2 %copy-start.3 = (bf16[256,896]{1,0:T(8,128)(2,1)S(1)}, bf16[256,896]{1,0:T(8,128)(2,1)}, u32[]{:S(2)}) copy-start(bf16[256,896]{1,0:T(8,128)(2,1)} %param.4) | copy-start | bytes 1376260
  21.8 28.0 %all-to-all-start.1 = ((f32[8,4,16,896]{3,2,1,0:T(8,128)}), f32[8,4,16,896]{3,2,1,0:T(8,128)S(1)}, u32[]{:S(2)}, u32[]{:S(2)}) async-start(f32[8,4,16,896]{3,2,1,0:T(8,128)} %broadcast_in_dim.7), calls=%async_computation.1 | async-start | bytes 3670016 | tf_op jit(solution)/shard_map/basis_gather/all_to_all | solution.py:45
  50.5 6.3 %collective-permute-start = (f32[256,256]{1,0:T(8,128)S(1)}, f32[256,256]{1,0:T(8,128)S(1)}, u32[]{:S(2)}, u32[]{:S(2)}) collective-permute-start(f32[256,256]{1,0:T(8,128)S(1)} %left_other.1), channel_id=1, source_target_pairs={{0,1},{1,0},{2,3},{3,2},{4,5},{5,4},{6,7},{7,6},{8,9},{9,8},{10,11... | collective-permute-start | bytes 786440 | tf_op jit(solution)/shard_map/left/ppermute | solution.py:57
  86.6 6.2 %collective-permute-start.1 = (f32[256,256]{1,0:T(8,128)S(1)}, f32[256,256]{1,0:T(8,128)S(1)}, u32[]{:S(2)}, u32[]{:S(2)}) collective-permute-start(f32[256,256]{1,0:T(8,128)S(1)} %bitcast.11), channel_id=1, source_target_pairs={{0,1},{1,0},{2,3},{3,2},{4,5},{5,4},{6,7},{7,6},{8,9},{9,8},{10,11... | collective-permute-start | bytes 786440 | tf_op jit(solution)/shard_map/sums/ppermute | solution.py:57
  148.6 10.2 %all-to-all-start.7 = ((f32[8,4,3,8,128]{4,3,2,1,0:T(8,128)}), f32[8,4,3,8,128]{4,3,2,1,0:T(8,128)S(1)}, u32[]{:S(2)}, u32[]{:S(2)}) async-start(f32[8,4,3,8,128]{4,3,2,1,0:T(8,128)} %broadcast_in_dim.8), calls=%async_computation.7 | async-start | bytes 786432 | tf_op jit(solution)/shard_map/sums/all_to_all | solution.py:45
  158.8 0.7 copy-start.4
  159.6 31.5 %all-to-all-start.8 = ((f32[8,64,896]{2,1,0:T(8,128)}), f32[8,64,896]{2,1,0:T(8,128)S(1)}, u32[]{:S(2)}, u32[]{:S(2)}) async-start(f32[8,64,896]{2,1,0:T(8,128)} %copies.1), calls=%async_computation.8 | async-start | bytes 3670016 | tf_op jit(solution)/shard_map/sums/all_to_all | solution.py:45
  163.2 8.4 %collective-permute-start.2 = (f32[8,4,3,8,128]{4,3,2,1,0:T(8,128)}, f32[8,4,3,8,128]{4,3,2,1,0:T(8,128)}, u32[]{:S(2)}, u32[]{:S(2)}) collective-permute-start(f32[8,4,3,8,128]{4,3,2,1,0:T(8,128)} %copy-done.4), channel_id=1, source_target_pairs={{0,1},{1,0},{2,3},{3,2},{4,5},{5,4},{6,7},{7,6},{8,9},{9,8},{10,11... | collective-permute-start | bytes 1179656 | tf_op jit(solution)/shard_map/sums/ppermute | solution.py:57
  191.1 7.7 %copy-start.2 = (f32[512,256]{1,0:T(8,128)S(1)}, f32[512,256]{1,0:T(8,128)}, u32[]{:S(2)}) copy-start(f32[512,256]{1,0:T(8,128)} %get-tuple-element.25.ortho_ref) | copy-start | bytes 1572868
  195.1 11.2 %all-to-all-start.9 = ((f32[16,4,128]{2,1,0:T(4,128)}), f32[16,4,128]{2,1,0:T(4,128)S(1)}, u32[]{:S(2)}, u32[]{:S(2)}) async-start(f32[16,4,128]{2,1,0:T(4,128)} %get-tuple-element.24), calls=%async_computation.9 | async-start | bytes 65536 | tf_op jit(solution)/shard_map/squares/all_to_all | solution.py:409
  198.8 1.5 copy-start
  200.3 6.0 %copy-start.1 = (f32[512,896]{1,0:T(8,128)S(1)}, f32[512,896]{1,0:T(8,128)}, u32[]{:S(2)}) copy-start(f32[512,896]{1,0:T(8,128)} %get-tuple-element.26.right_ref) | copy-start | bytes 5505028

commit v10 on v9

--- a/solution.py
+++ b/solution.py
@@ -233,17 +233,14 @@
         part.start()
     high[...], low[...] = split(left_ref[...])
 
-    def place(parts):
-        for part_ref, blocks in zip(parts, CORE_BLOCKS):
-            half = part_ref.shape[0] // 2
-            for i, (k, l) in enumerate(blocks):
-                tiles = part_ref[i % 2 * half : (i % 2 + 1) * half, :, i // 2]
-                work[square(k), square(l)] = tiles.reshape(BLOCK, BLOCK)
-
-    for part in arrive:
+    core = core_ref[0]
+    for part, part_ref, half in zip(arrive, (own_ref, other_ref), (core, 1 - core)):
         part.wait()
-    pl.when(core_ref[0] == 0)(lambda: place((own_ref, other_ref)))
-    pl.when(core_ref[0] != 0)(lambda: place((other_ref, own_ref)))
+        for i, (k, l) in enumerate(CORE_BLOCKS[0]):
+            members = part_ref.shape[0] // 2
+            tiles = part_ref[i % 2 * members : (i % 2 + 1) * members, :, i // 2]
+            at = (square(half * 2 + k), square(half * 2 + l)) if l < 2 else (square(half), square(l))
+            work[at] = tiles.reshape(BLOCK, BLOCK)
     leave = []
 
     def finish(k):

time: 209 us -> 209 us (level)
  transfers between devices with their start and end apart: 7 -> 7, of which waited for: 6 -> 6; matrix products, arithmetic and copies ran while one was open for 1% -> 1% of each run, Pallas kernels for 12% -> 11%
where the time goes in v10:
time: 209 us; the launch traced here: 208 us
  blocking collectives  103 us (49%)
  starting transfers between devices  34.1 us (16%)
  waiting for transfers between devices  32.2 us (15%)
  Pallas kernels  31.7 us (15%)
  local copies, waits for them, and re-layouts  5.28 us (3%)
    all_to_all x6, blocking collectives, exchange(): lax.all_to_all(blocks, name, 0, 0, axis_index_groups=groups, tiled=False)  103 us
    pallas_call x12, Pallas kernels, call(): pl.pallas_call(kernel, out_shape=[pltpu.HBM(shape, jnp.float32) if i in g...  31.7 us
    all_to_all x3, waiting for transfers between devices, exchange(): lax.all_to_all(blocks, name, 0, 0, axis_index_groups=groups, tiled=False)  25.9 us
    ppermute x3, starting transfers between devices, swap(): return lax.ppermute(part, 'col', [(i, i ^ 1) for i in range(Y * CORES)])  17.2 us
    all_to_all x3, starting transfers between devices, exchange(): lax.all_to_all(blocks, name, 0, 0, axis_index_groups=groups, tiled=False)  13.3 us
  transfers between devices with their start and end apart: 7, of which 6 were waited for; matrix products, arithmetic and copies ran while one was open for 1% of the time, Pallas kernels for 11%

profile of v10, /device:TPU:1, one launch (start us, length us, event | category | flops | bytes accessed | tf_op | source)
XLA Modules:
  0.0 208.1 jit_solution(9933666265386707718)
XLA Ops:
  0.6 0.8 broadcast_in_dim.6
  1.5 19.0 %all_to_all.50 = f32[4,16,896]{2,1,0:T(8,128)S(1)} all-to-all(f32[4,16,896]{2,1,0:T(8,128)S(1)} %broadcast_in_dim.6), channel_id=1, replica_groups={{0,32,64,96},{16,48,80,112},{128,160,192,224},{144,176,208,240},{256,28..., dimensions={0} | all-to-all | bytes 458752 | tf_op jit(solution)/shard_map/basis_gather/all_to_all | solution.py:45
  20.4 1.4 broadcast_in_dim.7
  21.8 6.2 %all-to-all-start.1 = ((f32[8,4,16,896]{3,2,1,0:T(8,128)}), f32[8,4,16,896]{3,2,1,0:T(8,128)S(1)}, u32[]{:S(2)}, u32[]{:S(2)}) async-start(f32[8,4,16,896]{3,2,1,0:T(8,128)} %broadcast_in_dim.7), calls=%async_computation.1 | async-start | bytes 3670016 | tf_op jit(solution)/shard_map/basis_gather/all_to_all | solution.py:45
  28.1 1.3 convert_add_fusion.blended_ref
  29.3 20.5 %all-to-all-done.1 = f32[8,4,16,896]{3,2,1,0:T(8,128)S(1)} async-done(((f32[8,4,16,896]{3,2,1,0:T(8,128)}), f32[8,4,16,896]{3,2,1,0:T(8,128)S(1)}, u32[]{:S(2)}, u32[]{:S(2)}) %all-to-all-start.1) | async-done | bytes 1835040 | tf_op jit(solution)/shard_map/basis_gather/all_to_all | solution.py:45
  49.9 0.6 left_other.1
  50.5 5.2 %collective-permute-start = (f32[256,256]{1,0:T(8,128)S(1)}, f32[256,256]{1,0:T(8,128)S(1)}, u32[]{:S(2)}, u32[]{:S(2)}) collective-permute-start(f32[256,256]{1,0:T(8,128)S(1)} %left_other.1), channel_id=1, source_target_pairs={{0,1},{1,0},{2,3},{3,2},{4,5},{5,4},{6,7},{7,6},{8,9},{9,8},{10,11... | collective-permute-start | bytes 786440 | tf_op jit(solution)/shard_map/left/ppermute | solution.py:57
  55.7 0.6 left_own.1
  56.8 17.7 %all_to_all.51.blocks_ref = f32[8,32,256]{2,1,0:T(8,128)S(1)} all-to-all(f32[8,32,256]{2,1,0:T(8,128)S(1)} %bitcast.13), channel_id=1, replica_groups={{0,2,4,6,8,10,12,14},{1,3,5,7,9,11,13,15},{16,18,20,22,24,26,28,30},{17..., dimensions={0} | all-to-all | bytes 524288 | tf_op jit(solution)/shard_map/left/all_to_all | solution.py:45
  74.6 12.1 %all_to_all.52 = f32[8,32,256]{2,1,0:T(8,128)S(1)} all-to-all(f32[8,32,256]{2,1,0:T(8,128)S(1)} %left_sum.1), channel_id=1, replica_groups={{0,2,4,6,8,10,12,14},{1,3,5,7,9,11,13,15},{16,18,20,22,24,26,28,30},{17..., dimensions={0} | all-to-all | bytes 524288 | tf_op jit(solution)/shard_map/left/all_to_all | solution.py:45
  86.6 5.1 %collective-permute-start.1 = (f32[256,256]{1,0:T(8,128)S(1)}, f32[256,256]{1,0:T(8,128)S(1)}, u32[]{:S(2)}, u32[]{:S(2)}) collective-permute-start(f32[256,256]{1,0:T(8,128)S(1)} %bitcast.11), channel_id=1, source_target_pairs={{0,1},{1,0},{2,3},{3,2},{4,5},{5,4},{6,7},{7,6},{8,9},{9,8},{10,11... | collective-permute-start | bytes 786440 | tf_op jit(solution)/shard_map/sums/ppermute | solution.py:57
  91.7 0.9 own_products.1
  92.9 0.8 products.1
  93.7 30.4 %all_to_all.53.blocks_ref = f32[8,4,17,8,128]{4,3,2,1,0:T(8,128)S(1)} all-to-all(f32[8,4,17,8,128]{4,3,2,1,0:T(8,128)S(1)} %get-tuple-element.19), channel_id=1, replica_groups={{0,16,128,144,256,272,384,400},{32,48,160,176,288,304,416,432},{64,80,1..., dimensions={0} | all-to-all | bytes 4456448 | tf_op jit(solution)/shard_map/sums/all_to_all | solution.py:45
  124.2 11.0 %all_to_all.54.blocks_ref = f32[4,17,8,128]{3,2,1,0:T(8,128)S(1)} all-to-all(f32[4,17,8,128]{3,2,1,0:T(8,128)S(1)} %wide_sum.1), channel_id=1, replica_groups={{0,32,64,96},{16,48,80,112},{128,160,192,224},{144,176,208,240},{256,28..., dimensions={0} | all-to-all | bytes 557056 | tf_op jit(solution)/shard_map/sums/all_to_all | solution.py:45
  135.2 12.6 %all_to_all.55.sums_ref = f32[4,17,8,128]{3,2,1,0:T(8,128)S(1)} all-to-all(f32[4,17,8,128]{3,2,1,0:T(8,128)S(1)} %long_sum.1), channel_id=1, replica_groups={{0,32,64,96},{16,48,80,112},{128,160,192,224},{144,176,208,240},{256,28..., dimensions={0} | all-to-all | bytes 557056 | tf_op jit(solution)/shard_map/sums/all_to_all | solution.py:45
  147.8 0.8 broadcast_in_dim.8
  148.6 3.5 %all-to-all-start.7 = ((f32[8,4,3,8,128]{4,3,2,1,0:T(8,128)}), f32[8,4,3,8,128]{4,3,2,1,0:T(8,128)S(1)}, u32[]{:S(2)}, u32[]{:S(2)}) async-start(f32[8,4,3,8,128]{4,3,2,1,0:T(8,128)} %broadcast_in_dim.8), calls=%async_computation.7 | async-start | bytes 786432 | tf_op jit(solution)/shard_map/sums/all_to_all | solution.py:45
  152.1 1.4 copies.1
  153.5 5.4 %all-to-all-done.7.own_hbm = f32[8,4,3,8,128]{4,3,2,1,0:T(8,128)S(1)} async-done(((f32[8,4,3,8,128]{4,3,2,1,0:T(8,128)}), f32[8,4,3,8,128]{4,3,2,1,0:T(8,128)S(1)}, u32[]{:S(2)}, u32[]{:S(2)}) %all-to-all-start.7) | async-done | bytes 393248 | tf_op jit(solution)/shard_map/sums/all_to_all | solution.py:45
  158.8 0.7 copy-done.4
  159.6 3.6 %all-to-all-start.8 = ((f32[8,64,896]{2,1,0:T(8,128)}), f32[8,64,896]{2,1,0:T(8,128)S(1)}, u32[]{:S(2)}, u32[]{:S(2)}) async-start(f32[8,64,896]{2,1,0:T(8,128)} %copies.1), calls=%async_computation.8 | async-start | bytes 3670016 | tf_op jit(solution)/shard_map/sums/all_to_all | solution.py:45
  163.2 7.0 %collective-permute-start.2 = (f32[8,4,3,8,128]{4,3,2,1,0:T(8,128)}, f32[8,4,3,8,128]{4,3,2,1,0:T(8,128)}, u32[]{:S(2)}, u32[]{:S(2)}) collective-permute-start(f32[8,4,3,8,128]{4,3,2,1,0:T(8,128)} %copy-done.4), channel_id=1, source_target_pairs={{0,1},{1,0},{2,3},{3,2},{4,5},{5,4},{6,7},{7,6},{8,9},{9,8},{10,11... | collective-permute-start | bytes 1179656 | tf_op jit(solution)/shard_map/sums/ppermute | solution.py:57
  170.2 1.5 collective-permute-done.2.other_hbm
  171.6 19.1 %factor.1 = (f32[512,512]{1,0:T(8,128)}, f32[512,256]{1,0:T(8,128)}) custom-call(s32[1]{0:T(128)} %bitcast.1.half_ref.core_ref, f32[8,4,3,8,128]{4,3,2,1,0:T(8,128)} %copy-done.4, f32[8,4,3,8,128]{4,3,2,1,0:T(8,128)} %collective-permute-done.2.other_hbm, f32[512,256]{1,0:T(8,128)S(1)} %get-tuple-element.21.left_ref), custom_call_target="tpu_custom_call" | custom-call | flops 2000000000 | bytes 4194304 | tf_op jit(solution)/shard_map/factor/factor/pallas_call | solution.py:312
  190.7 4.0 %right.1 = (f32[512,896]{1,0:T(8,128)}, f32[16,4,128]{2,1,0:T(4,128)}) custom-call(f32[512,512]{1,0:T(8,128)} %get-tuple-element.22.inverse_hbm, f32[512,896]{1,0:T(8,128)S(1)} %bitcast.10), custom_call_target="tpu_custom_call" | custom-call | flops 2000000000 | bytes 4194304 | tf_op jit(solution)/shard_map/right/right/pallas_call | solution.py:312
  194.8 3.7 %all-to-all-start.9 = ((f32[16,4,128]{2,1,0:T(4,128)}), f32[16,4,128]{2,1,0:T(4,128)S(1)}, u32[]{:S(2)}, u32[]{:S(2)}) async-start(f32[16,4,128]{2,1,0:T(4,128)} %get-tuple-element.24), calls=%async_computation.9 | async-start | bytes 65536 | tf_op jit(solution)/shard_map/squares/all_to_all | solution.py:406
  198.5 1.5 copy-done
  200.0 2.0 momentum.1
  201.9 4.0 %all-to-all-done.9.squares_ref = f32[16,4,128]{2,1,0:T(4,128)S(1)} async-done(((f32[16,4,128]{2,1,0:T(4,128)}), f32[16,4,128]{2,1,0:T(4,128)S(1)}, u32[]{:S(2)}, u32[]{:S(2)}) %all-to-all-start.9) | async-done | bytes 32800 | tf_op jit(solution)/shard_map/squares/all_to_all | solution.py:406
  205.9 2.2 %update.1 = (f32[256,896]{1,0:T(8,128)}, f32[16,896]{1,0:T(8,128)}) custom-call(s32[1]{0:T(128)} %bitcast.start_ref, f32[16,4,128]{2,1,0:T(4,128)S(1)} %all-to-all-done.9.squares_ref, f32[512,256]{1,0:T(8,128)S(1)} %copy-done.2, f32[512,896]{1,0:T(8,128)S(1)} %copy-done.1), custom_call_target="tpu_custom_call" | custom-call | flops 1000000000 | bytes 4194304 | tf_op jit(solution)/shard_map/outputs/update/pallas_call | solution.py:312
  (16 shorter events, 1.0 us)
Async XLA Ops:
  21.8 6.2 %copy-start.3 = (bf16[256,896]{1,0:T(8,128)(2,1)S(1)}, bf16[256,896]{1,0:T(8,128)(2,1)}, u32[]{:S(2)}) copy-start(bf16[256,896]{1,0:T(8,128)(2,1)} %param.4) | copy-start | bytes 1376260
  21.8 28.0 %all-to-all-start.1 = ((f32[8,4,16,896]{3,2,1,0:T(8,128)}), f32[8,4,16,896]{3,2,1,0:T(8,128)S(1)}, u32[]{:S(2)}, u32[]{:S(2)}) async-start(f32[8,4,16,896]{3,2,1,0:T(8,128)} %broadcast_in_dim.7), calls=%async_computation.1 | async-start | bytes 3670016 | tf_op jit(solution)/shard_map/basis_gather/all_to_all | solution.py:45
  50.5 6.3 %collective-permute-start = (f32[256,256]{1,0:T(8,128)S(1)}, f32[256,256]{1,0:T(8,128)S(1)}, u32[]{:S(2)}, u32[]{:S(2)}) collective-permute-start(f32[256,256]{1,0:T(8,128)S(1)} %left_other.1), channel_id=1, source_target_pairs={{0,1},{1,0},{2,3},{3,2},{4,5},{5,4},{6,7},{7,6},{8,9},{9,8},{10,11... | collective-permute-start | bytes 786440 | tf_op jit(solution)/shard_map/left/ppermute | solution.py:57
  86.6 6.2 %collective-permute-start.1 = (f32[256,256]{1,0:T(8,128)S(1)}, f32[256,256]{1,0:T(8,128)S(1)}, u32[]{:S(2)}, u32[]{:S(2)}) collective-permute-start(f32[256,256]{1,0:T(8,128)S(1)} %bitcast.11), channel_id=1, source_target_pairs={{0,1},{1,0},{2,3},{3,2},{4,5},{5,4},{6,7},{7,6},{8,9},{9,8},{10,11... | collective-permute-start | bytes 786440 | tf_op jit(solution)/shard_map/sums/ppermute | solution.py:57
  148.6 10.2 %all-to-all-start.7 = ((f32[8,4,3,8,128]{4,3,2,1,0:T(8,128)}), f32[8,4,3,8,128]{4,3,2,1,0:T(8,128)S(1)}, u32[]{:S(2)}, u32[]{:S(2)}) async-start(f32[8,4,3,8,128]{4,3,2,1,0:T(8,128)} %broadcast_in_dim.8), calls=%async_computation.7 | async-start | bytes 786432 | tf_op jit(solution)/shard_map/sums/all_to_all | solution.py:45
  158.8 0.7 copy-start.4
  159.6 31.1 %all-to-all-start.8 = ((f32[8,64,896]{2,1,0:T(8,128)}), f32[8,64,896]{2,1,0:T(8,128)S(1)}, u32[]{:S(2)}, u32[]{:S(2)}) async-start(f32[8,64,896]{2,1,0:T(8,128)} %copies.1), calls=%async_computation.8 | async-start | bytes 3670016 | tf_op jit(solution)/shard_map/sums/all_to_all | solution.py:45
  163.2 8.4 %collective-permute-start.2 = (f32[8,4,3,8,128]{4,3,2,1,0:T(8,128)}, f32[8,4,3,8,128]{4,3,2,1,0:T(8,128)}, u32[]{:S(2)}, u32[]{:S(2)}) collective-permute-start(f32[8,4,3,8,128]{4,3,2,1,0:T(8,128)} %copy-done.4), channel_id=1, source_target_pairs={{0,1},{1,0},{2,3},{3,2},{4,5},{5,4},{6,7},{7,6},{8,9},{9,8},{10,11... | collective-permute-start | bytes 1179656 | tf_op jit(solution)/shard_map/sums/ppermute | solution.py:57
  190.7 7.7 %copy-start.2 = (f32[512,256]{1,0:T(8,128)S(1)}, f32[512,256]{1,0:T(8,128)}, u32[]{:S(2)}) copy-start(f32[512,256]{1,0:T(8,128)} %get-tuple-element.25.ortho_ref) | copy-start | bytes 1572868
  194.8 11.2 %all-to-all-start.9 = ((f32[16,4,128]{2,1,0:T(4,128)}), f32[16,4,128]{2,1,0:T(4,128)S(1)}, u32[]{:S(2)}, u32[]{:S(2)}) async-start(f32[16,4,128]{2,1,0:T(4,128)} %get-tuple-element.24), calls=%async_computation.9 | async-start | bytes 65536 | tf_op jit(solution)/shard_map/squares/all_to_all | solution.py:406
  198.4 1.5 copy-start
  200.0 6.0 %copy-start.1 = (f32[512,896]{1,0:T(8,128)S(1)}, f32[512,896]{1,0:T(8,128)}, u32[]{:S(2)}) copy-start(f32[512,896]{1,0:T(8,128)} %get-tuple-element.26.right_ref) | copy-start | bytes 5505028
